TPU v7x, 32 devices: a whole 2x2x4 slice. The times are simulated.
32 devices in a mesh: dp: 8 (over y, x, core), head: 4 (over z).
Axes of the slice: x: 2, y: 2, z: 4, core: 2. Of those that a mesh axis runs over, the one named last changes fastest.
Arguments:
- images: bfloat16 [24, 96, 96, 180], P('dp', 'head'), may hold values from -6 to 6
- cotangent: bfloat16 [24, 96, 96, 180], P('dp', 'head'), may hold values from -6 to 6
- valid_size: int32 [24], P('dp'), may hold values from 48 to 96, as said below
- vectors: float32 [11, 180], replicated, may hold values from -0.8 to 1.4, as said below
- vectors_first: float32 [11, 180], replicated, may hold values from -0.0034179688 to 0.0034179688
- vectors_second: float32 [11, 180], replicated, may hold values from 2.887409e-08 to 1.1549636e-07
- qkv_weight: float32 [180, 540], replicated, may hold values from -0.4375 to 0.4375
- qkv_first: float32 [180, 540], replicated, may hold values from -0.0008544922 to 0.0008544922
- qkv_second: float32 [180, 540], replicated, may hold values from 1.8046307e-09 to 7.2185227e-09
- proj_weight: float32 [180, 180], replicated, may hold values from -1.25 to 1.25
- proj_first: float32 [180, 180], replicated, may hold values from -0.0008544922 to 0.0008544922
- proj_second: float32 [180, 180], replicated, may hold values from 1.8046307e-09 to 7.2185227e-09
- rel_table: float32 [225, 6], replicated, may hold values from -2 to 2
- rel_first: float32 [225, 6], replicated, may hold values from -0.0034179688 to 0.0034179688
- rel_second: float32 [225, 6], replicated, may hold values from 3.6092615e-10 to 1.4437046e-09
- fc1_weight: float32 [180, 360], replicated, may hold values from -0.4375 to 0.4375
- fc1_first: float32 [180, 360], replicated, may hold values from -0.0008544922 to 0.0008544922
- fc1_second: float32 [180, 360], replicated, may hold values from 1.8046307e-09 to 7.2185227e-09
- fc2_weight: float32 [360, 180], replicated, may hold values from -0.3125 to 0.3125
- fc2_first: float32 [360, 180], replicated, may hold values from -0.0008544922 to 0.0008544922
- fc2_second: float32 [360, 180], replicated, may hold values from 1.8046307e-09 to 7.2185227e-09
- conv_weight: float32 [3, 3, 180, 180], replicated, may hold values from -0.15625 to 0.15625
- conv_first: float32 [3, 3, 180, 180], replicated, may hold values from -0.0008544922 to 0.0008544922
- conv_second: float32 [3, 3, 180, 180], replicated, may hold values from 1.8046307e-09 to 7.2185227e-09
- step: int32 [1], replicated, may hold values from 2 to 20
- sr_crops: float32 [64, 3, 96, 96], P(('dp', 'head')), may hold values from 0 to 1, as said below
- hr_crops: float32 [64, 3, 96, 96], P(('dp', 'head')), may hold values from 0 to 1, as said below
- psnr_running: float32 [1], replicated, may hold values from 0 to 1000
Outputs:
- output: bfloat16 [24, 96, 96, 180], P('dp', 'head')
- image_grad: float32 [24, 96, 96, 180], P('dp', 'head')
- grad_norm: float32 [1], replicated
- psnr_total: float32 [1], replicated
- new_vectors: float32 [11, 180], replicated
- new_vectors_first: float32 [11, 180], replicated
- new_vectors_second: float32 [11, 180], replicated
- new_qkv_weight: float32 [180, 540], replicated
- new_qkv_first: float32 [180, 540], replicated
- new_qkv_second: float32 [180, 540], replicated
- new_proj_weight: float32 [180, 180], replicated
- new_proj_first: float32 [180, 180], replicated
- new_proj_second: float32 [180, 180], replicated
- new_rel_table: float32 [225, 6], replicated
- new_rel_first: float32 [225, 6], replicated
- new_rel_second: float32 [225, 6], replicated
- new_fc1_weight: float32 [180, 360], replicated
- new_fc1_first: float32 [180, 360], replicated
- new_fc1_second: float32 [180, 360], replicated
- new_fc2_weight: float32 [360, 180], replicated
- new_fc2_first: float32 [360, 180], replicated
- new_fc2_second: float32 [360, 180], replicated
- new_conv_weight: float32 [3, 3, 180, 180], replicated
- new_conv_first: float32 [3, 3, 180, 180], replicated
- new_conv_second: float32 [3, 3, 180, 180], replicated
Inputs may be any that keep to these rules, and one draw needn't show every extreme that they name: `valid_size`: each image's valid side is one of 48, 64 and 96. `vectors`: rows 0 and 5 are gains near 1, the other rows biases near 0. `sr_crops`: intensities. `hr_crops`: intensities.
All inputs are finite; a program needn't handle non-finite values.
Results may differ from a plain program's by a relative error of at most 0.008.
The roundings to bfloat16 on the way count: a program that leaves them out, or rounds other values in their place, can miss the bound.
Values may be sent and summed in bfloat16 or wider, within the bound.
A program may use at most 384 MiB of HBM per device.

v0:
```python
import jax
import jax.numpy as jnp
from jax import lax
from jax.sharding import PartitionSpec as P

WIN = 8


eps_norm = 1e-05
neg_mask = -100.0
max_norm = 1.0
learn_rate = 0.03
vector_rate = 0.2
beta_one = 0.9
beta_two = 0.999
adam_eps = 1e-08
decay_rate = 0.01
highest = lax.Precision.HIGHEST


def with_halo(x, sides, width):
    for axis, dim in sides:
        peers, length = (lax.axis_size(axis), x.shape[dim])
        up = [(i, (i + 1) % peers) for i in range(peers - 1)]
        down = [(j, i) for i, j in up]
        last = lax.slice_in_dim(x, length - width, length, axis=dim)
        first = lax.slice_in_dim(x, 0, width, axis=dim)
        before = lax.ppermute(last, axis, up)
        after = lax.ppermute(first, axis, down)
        x = jnp.concatenate([before, x, after], axis=dim)
    return x


def to_windows(image, window):
    per_side = image.shape[0] // window
    channels = image.shape[-1]
    tiled = image.reshape(per_side, window, per_side, window, channels)
    return tiled.transpose(0, 2, 1, 3, 4).reshape(per_side * per_side, window * window, channels)


def from_windows(blocks, image_side, window):
    per_side = image_side // window
    channels = blocks.shape[-1]
    tiled = blocks.reshape(per_side, per_side, window, window, channels)
    return tiled.transpose(0, 2, 1, 3, 4).reshape(image_side, image_side, channels)


def region_mask(valid_len, image_side, window):
    shift_by = window // 2
    coords = jnp.arange(image_side)
    band_id = jnp.where(
        coords < image_side - window, 0, jnp.where(coords < image_side - shift_by, 1, 2)
    )
    region = band_id[:, None] * 3 + band_id[None, :]
    anchor = (coords + shift_by) % image_side
    outside = anchor >= valid_len
    masked_key = outside[:, None] | outside[None, :]
    region_win = to_windows(region[:, :, None], window)[:, :, 0]
    masked_win = to_windows(masked_key[:, :, None], window)[:, :, 0]
    apart = region_win[:, :, None] != region_win[:, None, :]
    additive = jnp.where(apart, neg_mask, 0.0) + jnp.where(masked_win[:, None, :], neg_mask, 0.0)
    return additive.astype(jnp.float32)


def relative_onehot(window):
    position = jnp.arange(window * window)
    pos_row = position // window
    pos_col = position % window
    span_rel = 2 * window - 1
    rel_index = (pos_row[:, None] - pos_row[None, :] + window - 1) * span_rel + (
        pos_col[:, None] - pos_col[None, :] + window - 1
    )
    return (rel_index.reshape(-1)[:, None] == jnp.arange(span_rel * span_rel)[None, :]).astype(
        jnp.float32
    )


def layer_norm_parts(values_in, gain, shift_vec):
    average = jnp.mean(values_in, axis=-1, keepdims=True)
    centered = values_in - average
    variance = jnp.mean(centered * centered, axis=-1, keepdims=True)
    inv_std = lax.rsqrt(variance + eps_norm)
    normal_part = centered * inv_std
    return (normal_part * gain + shift_vec, normal_part, inv_std)


def layer_norm_back(grad_out, normal_part, inv_std, gain):
    scaled = grad_out * gain
    return inv_std * (
        scaled
        - jnp.mean(scaled, axis=-1, keepdims=True)
        - normal_part * jnp.mean(scaled * normal_part, axis=-1, keepdims=True)
    )


def gelu_slope(hidden):
    return (
        0.5 * (1.0 + lax.erf(hidden * 0.7071067811865476))
        + hidden * jnp.exp(-0.5 * hidden * hidden) * 0.3989422804014327
    )


def add_into(total, grad_piece, offset, axis_num):
    current = lax.dynamic_slice_in_dim(total, offset, grad_piece.shape[axis_num], axis_num)
    return lax.dynamic_update_slice_in_dim(total, current + grad_piece, offset, axis_num)


def row_sums(values_in):
    return jnp.sum(values_in, axis=(0, 1, 2), dtype=jnp.float32)


def conv_apply(padded, kernel, out_rows, image_side):
    total = None
    for row_off in range(3):
        for col_off in range(3):
            term = jnp.einsum(
                "nhwc,cf->nhwf",
                padded[:, row_off : row_off + out_rows, col_off : col_off + image_side],
                kernel[row_off, col_off],
                preferred_element_type=jnp.float32,
            )
            total = term if total is None else total + term
    return total


def adam_update(
    weight, moment_one, moment_two, grad_item, clip_factor, first_fix, second_fix, step_rate
):
    clipped = grad_item * clip_factor
    moment_one = beta_one * moment_one + (1.0 - beta_one) * clipped
    moment_two = beta_two * moment_two + (1.0 - beta_two) * clipped * clipped
    update = moment_one / first_fix / (jnp.sqrt(moment_two / second_fix) + adam_eps)
    return (weight - step_rate * (update + decay_rate * weight), moment_one, moment_two)


def on_device(
    images,
    cotangent,
    valid_size,
    vectors,
    vectors_first,
    vectors_second,
    qkv_weight,
    qkv_first,
    qkv_second,
    proj_weight,
    proj_first,
    proj_second,
    rel_table,
    rel_first,
    rel_second,
    fc1_weight,
    fc1_first,
    fc1_second,
    fc2_weight,
    fc2_first,
    fc2_second,
    conv_weight,
    conv_first,
    conv_second,
    step,
    sr_crops,
    hr_crops,
    psnr_running,
):
    image_count, own_rows, image_side, channels = images.shape
    head_count = rel_table.shape[1]
    head_dim = channels // head_count
    shift_by = WIN // 2
    win_tokens = WIN * WIN
    slot_width = 2 * head_dim
    scale_q = head_dim ** (-0.5)
    head_place = lax.axis_index("head")
    slot_heads = jnp.array([[0, 1], [2, 3], [4, 4], [5, 5]], jnp.int32)[head_place]
    slot_scale = jnp.array([[1.0, 1.0], [1.0, 1.0], [1.0, 0.0], [1.0, 0.0]], jnp.float32)[
        head_place
    ]
    qkv_low = qkv_weight.astype(jnp.bfloat16)
    proj_low = proj_weight.astype(jnp.bfloat16)
    fc1_low = fc1_weight.astype(jnp.bfloat16)
    fc2_low = fc2_weight.astype(jnp.bfloat16)
    conv_low = conv_weight.astype(jnp.bfloat16)
    head_starts = [slot_heads[slot_index] * head_dim for slot_index in range(2)]
    own_columns = jnp.concatenate(
        [
            lax.dynamic_slice_in_dim(qkv_low, part_index * channels + head_start, head_dim, 1)
            for part_index in range(3)
            for head_start in head_starts
        ],
        axis=1,
    )
    query_bias = jnp.concatenate(
        [
            lax.dynamic_slice_in_dim(vectors[2], head_start, head_dim, 0)
            for head_start in head_starts
        ]
    )
    value_bias = jnp.concatenate(
        [
            lax.dynamic_slice_in_dim(vectors[3], head_start, head_dim, 0)
            for head_start in head_starts
        ]
    )
    proj_rows = jnp.concatenate(
        [lax.dynamic_slice_in_dim(proj_low, head_start, head_dim, 0) for head_start in head_starts],
        axis=0,
    )
    onehot = relative_onehot(WIN)
    table_bias = jnp.dot(onehot, rel_table, precision=highest)
    slot_bias = jnp.concatenate(
        [
            lax.dynamic_slice_in_dim(table_bias, slot_heads[slot_index], 1, 1)
            for slot_index in range(2)
        ],
        axis=1,
    )
    slot_bias = slot_bias.reshape(win_tokens, win_tokens, 2).transpose(2, 0, 1)

    def attend(image, valid_len):
        rolled = jnp.roll(image, (-shift_by, -shift_by), (0, 1))
        blocks = to_windows(rolled, WIN)
        win_count = blocks.shape[0]
        packed = jnp.einsum("wtc,cf->wtf", blocks, own_columns, preferred_element_type=jnp.float32)
        shape_slots = (win_count, win_tokens, 2, head_dim)
        queries = (
            ((packed[:, :, :slot_width] + query_bias) * scale_q)
            .astype(jnp.bfloat16)
            .reshape(shape_slots)
        )
        key_rows = (
            packed[:, :, slot_width : 2 * slot_width].astype(jnp.bfloat16).reshape(shape_slots)
        )
        value_rows = (
            (packed[:, :, 2 * slot_width :] + value_bias).astype(jnp.bfloat16).reshape(shape_slots)
        )
        scores = jnp.einsum(
            "wqsd,wksd->wsqk", queries, key_rows, preferred_element_type=jnp.float32
        )
        scores = scores + slot_bias[None] + region_mask(valid_len, image_side, WIN)[:, None]
        attn_probs = jax.nn.softmax(scores, axis=-1)
        mixed_rows = jnp.einsum(
            "wsqk,wksd->wqsd",
            attn_probs.astype(jnp.bfloat16),
            value_rows,
            preferred_element_type=jnp.float32,
        )
        mixed_rows = (mixed_rows.astype(jnp.bfloat16) * slot_scale[:, None]).astype(jnp.bfloat16)
        return (
            blocks,
            queries,
            key_rows,
            value_rows,
            attn_probs,
            mixed_rows.reshape(win_count, win_tokens, slot_width),
        )

    def forward_image(item_pair):
        blocks, queries, key_rows, value_rows, attn_probs, mixed_rows = attend(
            item_pair[0], item_pair[1]
        )
        projected = jnp.einsum(
            "wtf,fc->wtc", mixed_rows, proj_rows, preferred_element_type=jnp.float32
        )
        return jnp.roll(from_windows(projected, image_side, WIN), (shift_by, shift_by), (0, 1))

    def backward_image(totals, triple):
        blocks, queries, key_rows, value_rows, attn_probs, mixed_rows = attend(triple[0], triple[2])
        win_count = blocks.shape[0]
        dblocks = to_windows(jnp.roll(triple[1], (-shift_by, -shift_by), (0, 1)), WIN)
        grad_rows = jnp.einsum(
            "wtf,wtc->fc", mixed_rows, dblocks, preferred_element_type=jnp.float32
        )
        dmixed = jnp.einsum("wtc,fc->wtf", dblocks, proj_rows, preferred_element_type=jnp.float32)
        dmixed = (dmixed.reshape(win_count, win_tokens, 2, head_dim) * slot_scale[:, None]).astype(
            jnp.bfloat16
        )
        dvalues = jnp.einsum(
            "wsqk,wqsd->wksd",
            attn_probs.astype(jnp.bfloat16),
            dmixed,
            preferred_element_type=jnp.float32,
        ).astype(jnp.bfloat16)
        dprobs = jnp.einsum(
            "wqsd,wksd->wsqk", dmixed, value_rows, preferred_element_type=jnp.float32
        )
        dscores = (
            attn_probs * (dprobs - jnp.sum(attn_probs * dprobs, axis=-1, keepdims=True))
        ).astype(jnp.bfloat16)
        dqueries = jnp.einsum(
            "wsqk,wksd->wqsd", dscores, key_rows, preferred_element_type=jnp.float32
        ).astype(jnp.bfloat16)
        dkeys = jnp.einsum(
            "wsqk,wqsd->wksd", dscores, queries, preferred_element_type=jnp.float32
        ).astype(jnp.bfloat16)
        table_part = jnp.sum(dscores, axis=0, dtype=jnp.float32).reshape(2, win_tokens * win_tokens)
        grad_table = jnp.dot(table_part, onehot, precision=highest)
        dq_flat = dqueries.reshape(win_count, win_tokens, slot_width)
        dv_flat = dvalues.reshape(win_count, win_tokens, slot_width)
        dkv_flat = jnp.concatenate(
            [dkeys.reshape(win_count, win_tokens, slot_width), dv_flat], axis=-1
        )
        grad_qcols = (
            jnp.einsum("wtc,wtf->cf", blocks, dq_flat, preferred_element_type=jnp.float32) * scale_q
        )
        grad_kvcols = jnp.einsum(
            "wtc,wtf->cf", blocks, dkv_flat, preferred_element_type=jnp.float32
        )
        grad_qbias = jnp.sum(dq_flat, axis=(0, 1), dtype=jnp.float32) * scale_q
        grad_vbias = jnp.sum(dv_flat, axis=(0, 1), dtype=jnp.float32)
        dblk = (
            jnp.einsum(
                "wtf,cf->wtc",
                dq_flat,
                own_columns[:, :slot_width],
                preferred_element_type=jnp.float32,
            )
            * scale_q
        )
        dblk = dblk + jnp.einsum(
            "wtf,cf->wtc", dkv_flat, own_columns[:, slot_width:], preferred_element_type=jnp.float32
        )
        dpart = jnp.roll(from_windows(dblk, image_side, WIN), (shift_by, shift_by), (0, 1))
        fresh = (grad_qcols, grad_kvcols, grad_rows, grad_table, grad_qbias, grad_vbias)
        return (tuple((old + new for old, new in zip(totals, fresh))), dpart)

    image_f = images.astype(jnp.float32)
    normed_one, normal_one, inv_one = layer_norm_parts(image_f, vectors[0], vectors[1])
    normed_low = normed_one.astype(jnp.bfloat16)
    full_normed = lax.all_gather(normed_low, "head", axis=1, tiled=True)
    partials = lax.map(forward_image, (full_normed, valid_size))
    attn_out = lax.psum_scatter(partials, "head", scatter_dimension=1, tiled=True) + vectors[4]
    resid_one = image_f + attn_out
    normed_two_f, normal_two, inv_two = layer_norm_parts(resid_one, vectors[5], vectors[6])
    normed_two = normed_two_f.astype(jnp.bfloat16)
    hidden_bias = jnp.concatenate([vectors[7], vectors[8]])
    hidden = (
        jnp.einsum("nijc,cf->nijf", normed_two, fc1_low, preferred_element_type=jnp.float32)
        + hidden_bias
    )
    active = jax.nn.gelu(hidden, approximate=False).astype(jnp.bfloat16)
    branch = (
        jnp.einsum("nijf,fc->nijc", active, fc2_low, preferred_element_type=jnp.float32)
        + vectors[9]
    )
    resid_two = resid_one + branch
    conv_in = resid_two.astype(jnp.bfloat16)
    conv_pad = with_halo(conv_in, (("head", 1),), 1)
    conv_pad = jnp.pad(conv_pad, ((0, 0), (0, 0), (1, 1), (0, 0)))
    output = (conv_apply(conv_pad, conv_low, own_rows, image_side) + vectors[10] + image_f).astype(
        jnp.bfloat16
    )
    grad_pad = with_halo(cotangent, (("head", 1),), 1)
    grad_pad = jnp.pad(grad_pad, ((0, 0), (0, 0), (1, 1), (0, 0)))
    grad_conv = jnp.stack(
        [
            jnp.stack(
                [
                    jnp.einsum(
                        "nhwc,nhwf->cf",
                        conv_pad[:, row_off : row_off + own_rows, col_off : col_off + image_side],
                        cotangent,
                        preferred_element_type=jnp.float32,
                    )
                    for col_off in range(3)
                ]
            )
            for row_off in range(3)
        ]
    )
    flipped = jnp.flip(conv_low, (0, 1)).transpose(0, 1, 3, 2)
    dsecond = conv_apply(grad_pad, flipped, own_rows, image_side)
    dbranch = dsecond.astype(jnp.bfloat16)
    grad_fc2 = jnp.einsum("nijf,nijc->fc", active, dbranch, preferred_element_type=jnp.float32)
    dhidden = (
        jnp.einsum("nijc,fc->nijf", dbranch, fc2_low, preferred_element_type=jnp.float32)
        * gelu_slope(hidden)
    ).astype(jnp.bfloat16)
    grad_fc1 = jnp.einsum("nijc,nijf->cf", normed_two, dhidden, preferred_element_type=jnp.float32)
    dnormed_two = jnp.einsum("nijf,cf->nijc", dhidden, fc1_low, preferred_element_type=jnp.float32)
    grad_hidden_bias = row_sums(dhidden)
    dfirst = dsecond + layer_norm_back(dnormed_two, normal_two, inv_two, vectors[5])
    dattn_low = dfirst.astype(jnp.bfloat16)
    full_dattn = lax.all_gather(dattn_low, "head", axis=1, tiled=True)
    zero_totals = (
        jnp.zeros((channels, slot_width), jnp.float32),
        jnp.zeros((channels, 2 * slot_width), jnp.float32),
        jnp.zeros((slot_width, channels), jnp.float32),
        jnp.zeros((2, onehot.shape[1]), jnp.float32),
        jnp.zeros((slot_width,), jnp.float32),
        jnp.zeros((slot_width,), jnp.float32),
    )
    totals, dparts = lax.scan(backward_image, zero_totals, (full_normed, full_dattn, valid_size))
    dnormed_one = lax.psum_scatter(
        dparts.astype(jnp.bfloat16), "head", scatter_dimension=1, tiled=True
    ).astype(jnp.float32)
    grad_qcols, grad_kvcols, grad_rows, grad_table, grad_qbias, grad_vbias = totals
    grad_qkv = jnp.zeros((channels, 3 * channels), jnp.float32)
    grad_proj = jnp.zeros((channels, channels), jnp.float32)
    grad_rel = jnp.zeros(rel_table.shape, jnp.float32)
    grad_query_bias = jnp.zeros((channels,), jnp.float32)
    grad_value_bias = jnp.zeros((channels,), jnp.float32)
    for slot_index in range(2):
        lower = slot_index * head_dim
        upper = lower + head_dim
        head_start = head_starts[slot_index]
        grad_qkv = add_into(grad_qkv, grad_qcols[:, lower:upper], head_start, 1)
        grad_qkv = add_into(grad_qkv, grad_kvcols[:, lower:upper], channels + head_start, 1)
        grad_qkv = add_into(
            grad_qkv,
            grad_kvcols[:, slot_width + lower : slot_width + upper],
            2 * channels + head_start,
            1,
        )
        grad_proj = add_into(grad_proj, grad_rows[lower:upper], head_start, 0)
        grad_rel = add_into(grad_rel, grad_table[slot_index][:, None], slot_heads[slot_index], 1)
        grad_query_bias = add_into(grad_query_bias, grad_qbias[lower:upper], head_start, 0)
        grad_value_bias = add_into(grad_value_bias, grad_vbias[lower:upper], head_start, 0)
    image_grad = (
        cotangent.astype(jnp.float32)
        + dfirst
        + layer_norm_back(dnormed_one, normal_one, inv_one, vectors[0])
    )
    grad_vectors = jnp.stack(
        [
            row_sums(dnormed_one * normal_one),
            row_sums(dnormed_one),
            grad_query_bias,
            grad_value_bias,
            row_sums(dattn_low),
            row_sums(dnormed_two * normal_two),
            row_sums(dnormed_two),
            grad_hidden_bias[:channels],
            grad_hidden_bias[channels:],
            row_sums(dbranch),
            row_sums(cotangent),
        ]
    )
    difference = sr_crops - hr_crops
    luma_diff = (
        65.481 * difference[:, 0] + 128.553 * difference[:, 1] + 24.966 * difference[:, 2]
    ) / 255.0
    mean_error = jnp.mean(luma_diff * luma_diff, axis=(1, 2))
    local_psnr = jnp.sum(-10.0 * jnp.log10(mean_error + 1e-06))
    grads = lax.psum(
        (grad_vectors, grad_qkv, grad_proj, grad_rel, grad_fc1, grad_fc2, grad_conv), ("dp", "head")
    )
    psnr_sum_all = lax.psum(local_psnr, ("dp", "head"))
    total_sq = jnp.zeros((), jnp.float32)
    for grad_item in grads:
        total_sq = total_sq + jnp.sum(grad_item * grad_item)
    grad_norm = jnp.sqrt(total_sq)
    clip_factor = jnp.minimum(1.0, max_norm / (grad_norm + 1e-06))
    step_count = step[0].astype(jnp.float32)
    first_fix = 1.0 - beta_one**step_count
    second_fix = 1.0 - beta_two**step_count
    weights = (vectors, qkv_weight, proj_weight, rel_table, fc1_weight, fc2_weight, conv_weight)
    firsts = (vectors_first, qkv_first, proj_first, rel_first, fc1_first, fc2_first, conv_first)
    seconds = (
        vectors_second,
        qkv_second,
        proj_second,
        rel_second,
        fc1_second,
        fc2_second,
        conv_second,
    )
    rate_list = (
        vector_rate,
        learn_rate,
        learn_rate,
        learn_rate,
        learn_rate,
        learn_rate,
        learn_rate,
    )
    updated = []
    for weight, moment_one, moment_two, grad_item, step_rate in zip(
        weights, firsts, seconds, grads, rate_list
    ):
        updated.extend(
            adam_update(
                weight,
                moment_one,
                moment_two,
                grad_item,
                clip_factor,
                first_fix,
                second_fix,
                step_rate,
            )
        )
    psnr_total = psnr_running + psnr_sum_all
    return (
        output,
        image_grad,
        grad_norm.reshape(1),
        psnr_total,
        updated[0],
        updated[1],
        updated[2],
        updated[3],
        updated[4],
        updated[5],
        updated[6],
        updated[7],
        updated[8],
        updated[9],
        updated[10],
        updated[11],
        updated[12],
        updated[13],
        updated[14],
        updated[15],
        updated[16],
        updated[17],
        updated[18],
        updated[19],
        updated[20],
    )


def solution(mesh):
    placed = (
        P("dp", "head", None, None),
        P("dp", "head", None, None),
        P("dp"),
        P(),
        P(),
        P(),
        P(),
        P(),
        P(),
        P(),
        P(),
        P(),
        P(),
        P(),
        P(),
        P(),
        P(),
        P(),
        P(),
        P(),
        P(),
        P(),
        P(),
        P(),
        P(),
        P(("dp", "head"), None, None, None),
        P(("dp", "head"), None, None, None),
        P(),
    )
    return jax.shard_map(
        on_device,
        mesh=mesh,
        in_specs=placed,
        out_specs=(
            P("dp", "head", None, None),
            P("dp", "head", None, None),
            P(),
            P(),
            P(),
            P(),
            P(),
            P(),
            P(),
            P(),
            P(),
            P(),
            P(),
            P(),
            P(),
            P(),
            P(),
            P(),
            P(),
            P(),
            P(),
            P(),
            P(),
            P(),
            P(),
        ),
        check_vma=False,
    )
```

profile of v0, /device:TPU:0, one launch (start us, length us, event | category | flops | bytes accessed | tf_op | source)
XLA Modules:
  0.0 3282.5 jit_solution(9992957308359878413)
XLA Ops:
  28.7 225.5 %all-gather.3.cloned.1.call-done = bf16[3,96,96,180]{2,3,1,0:T(8,128)(2,1)} async-done(((bf16[3,24,96,180]{2,3,1,0:T(8,128)(2,1)}), bf16[3,96,96,180]{2,3,1,0:T(8,128)(2,1)}) %all-gather.3.cloned.1.call-update) | async-done | bytes 9953296 | tf_op jit(solution)/shard_map/all_gather | solution.py:329
  254.2 18.0 copy.486
  272.2 403.1 %while.38 = (s32[]{:T(128)}, f32[3,96,96,180]{2,3,1,0:T(8,128)}, bf16[3,96,96,180]{3,2,1,0:T(8,128)(2,1)}, bf16[180,180]{1,0:T(8,128)(2,1)S(1)}, f32[60]{0:T(128...) while((s32[]{:T(128)}, f32[3,96,96,180]{2,3,1,0:T(8,128)}, ...), condition=%wide.region_5.6_spmd, body=%wide.region_2.5_spmd.sunk | while | flops 968193216 | bytes 204096240 | solution.py:330
  298.9 10.3 fusion.435
  340.5 10.8 fusion.437
  433.1 10.3 fusion.435
  474.6 10.8 fusion.437
  608.8 10.8 fusion.437
  727.0 23.3 convert_reduce_fusion.9
  750.3 822.4 %all-reduce.10.cloned.1.call-done = f32[3,96,96,180]{2,3,1,0:T(8,128)} async-done(((f32[3,96,96,180]{2,3,1,0:T(8,128)}), f32[3,96,96,180]{2,3,1,0:T(8,128)}) %all-reduce.10.cloned.1.call-update) | async-done | bytes 19906576
  1608.8 25.6 fusion.102
  1682.3 162.7 %all-gather.5.cloned.1.call-done = bf16[3,96,96,180]{2,3,1,0:T(8,128)(2,1)} async-done(((bf16[3,24,96,180]{2,3,1,0:T(8,128)(2,1)}), bf16[3,96,96,180]{2,3,1,0:T(8,128)(2,1)}) %all-gather.5.cloned.1.call-update) | async-done | bytes 9953296 | tf_op jit(solution)/shard_map/all_gather | solution.py:383
  1845.0 731.6 %while.39 = (s32[]{:T(128)}, f32[180,60]{0,1:T(8,128)}, f32[180,120]{1,0:T(8,128)}, f32[60,180]{1,0:T(8,128)}, f32[2,225]{1,0:T(2,128)}, /*index=5*/f32[60]{0:T(...) while((s32[]{:T(128)}, f32[180,60]{0,1:T(8,128)}, ...), condition=%wide.wide.region_18.19_spmd.clone, body=%wide.wide.region_11.18_spmd.clone.sunk | while | flops 2715991808 | bytes 398493440 | solution.py:392
  1940.1 10.6 fusion.470
  1990.9 11.2 multiply_reduce_fusion.15
  2182.9 10.6 fusion.470
  2233.7 11.2 multiply_reduce_fusion.15
  2425.6 10.6 fusion.470
  2476.4 11.2 multiply_reduce_fusion.15
  2591.4 17.8 copy.509
  2644.9 20.1 fusion.131
  2670.1 59.4 %all-reduce.14.cloned.1.call-done = (f32[180,540]{1,0:T(8,128)}, f32[180,180]{1,0:T(8,128)}, f32[180,360]{1,0:T(8,128)}, f32[360,180]{0,1:T(8,128)}, f32[3,3,180,180]{3,2,1,0:T(8,128)}) async-done(((f32[180,540]{1,0:T(8,128)}, f32[180,180]{1,0:T(8,128)}, f32[180,360]{1,0:T(8,128)}, f32[360,180]{0,1:T(8,128)}, f32[3,3,180,180]{3,2,1,0:T(8,128)}), (f32[180,540]{1,0:T(8,128)}, f32[180,180]{1,0:T(8,128)}, ...) | async-done | bytes 2203216 | tf_op jit(solution)/shard_map/psum | solution.py:444
  2739.1 450.3 %all-reduce.12.cloned.1.call-done = bf16[3,96,96,180]{2,3,1,0:T(8,128)(2,1)} async-done(((bf16[3,96,96,180]{2,3,1,0:T(8,128)(2,1)}), bf16[3,96,96,180]{2,3,1,0:T(8,128)(2,1)}) %all-reduce.12.cloned.1.call-update) | async-done | bytes 9953296
  3205.8 40.1 %all-reduce.4 = (f32[11,180]{1,0:T(8,128)S(1)}, f32[225,6]{0,1:T(8,128)S(1)}, f32[1]{0:T(128)}) all-reduce(f32[11,180]{1,0:T(8,128)S(1)} %stack.101, f32[225,6]{0,1:T(8,128)S(1)} %dynamic_update_slice.70, f32[1]{0:T(128)} %bitcast.137), channel_id=1, replica_groups=mesh['dp'=8,'head'=4] {'dp','head'}, use_global_device_ids=true, to_apply=%region_30.31 | all-reduce | flops 3331 | bytes 26648 | tf_op jit(solution)/shard_map/psum | solution.py:444
  (806 shorter events, 1261.1 us)
Async XLA Ops:
  7.2 247.0 %all-gather.3.cloned.1.call-start = ((), (), s32[]{:S(2)}) async-start(), calls=%async_computation | async-start | bytes 16957440 | tf_op jit(solution)/shard_map/all_gather | solution.py:329
  17.0 1555.7 %all-reduce.10.cloned.1.call-start = ((), (), s32[]{:S(2)}) async-start(), calls=%async_computation.2 | async-start | bytes 54263808
  27.6 244.6 %copy-start.19 = (bf16[180,180]{0,1:T(8,128)(2,1)}, bf16[180,180]{0,1:T(8,128)(2,1)S(1)}, u32[]{:S(2)}) copy-start(bf16[180,180]{0,1:T(8,128)(2,1)S(1)} %concatenate.106) | copy-start | bytes 194404
  28.7 243.5 %copy-start.95 = (s32[3]{0:T(128)S(1)}, s32[3]{0:T(128)}, u32[]{:S(2)}) copy-start(s32[3]{0:T(128)} %param.36) | copy-start | bytes 40
  675.9 1169.1 %all-gather.5.cloned.1.call-start = ((), (), s32[]{:S(2)}) async-start(), calls=%async_computation.1 | async-start | bytes 16957440 | tf_op jit(solution)/shard_map/all_gather | solution.py:383
  679.1 14.2 collective-permute-start.2
  681.1 16.9 collective-permute-start.3
  727.0 845.7 %copy-start.11 = (bf16[3,24,96,180]{2,1,3,0:T(8,128)(2,1)S(1)}, bf16[3,24,96,180]{2,1,3,0:T(8,128)(2,1)}, u32[]{:S(2)}) copy-start(bf16[3,24,96,180]{2,1,3,0:T(8,128)(2,1)} %param.34) | copy-start | bytes 7464964
  727.0 845.7 %copy-start.87 = (f32[1,180]{1,0:T(1,128)S(1)}, f32[1,180]{1,0:T(1,128)}, u32[]{:S(2)}) copy-start(f32[1,180]{1,0:T(1,128)} %get-tuple-element.868) | copy-start | bytes 2164
  1576.9 24.6 copy-start.9
  1608.7 25.7 slice-start.7
  1608.7 1120.8 %all-reduce.14.cloned.1.call-start = ((), (), s32[]{:S(2)}) async-start(), calls=%async_computation.4 | async-start | bytes 5840896 | tf_op jit(solution)/shard_map/psum | solution.py:444
  1608.7 25.6 slice-start.8
  1608.7 25.6 copy-start.69
  1637.4 11.6 collective-permute-start
  1638.7 13.4 collective-permute-start.1
  1679.8 165.2 %copy-start.20 = (bf16[180,180]{0,1:T(8,128)(2,1)S(1)}, bf16[180,180]{0,1:T(8,128)(2,1)}, u32[]{:S(2)}) copy-start(bf16[180,180]{0,1:T(8,128)(2,1)} %copy-done.19) | copy-start | bytes 194404
  1679.8 165.2 %copy-start.64 = (f32[60]{0:T(128)S(1)}, f32[60]{0:T(128)}, u32[]{:S(2)}) copy-start(f32[60]{0:T(128)} %copy-done.63) | copy-start | bytes 724
  1679.8 165.2 %copy-start.66 = (f32[60]{0:T(128)S(1)}, f32[60]{0:T(128)}, u32[]{:S(2)}) copy-start(f32[60]{0:T(128)} %copy-done.65) | copy-start | bytes 724
  1679.8 165.2 %copy-start.76 = (f32[1,2]{1,0:T(1,128)S(1)}, f32[1,2]{1,0:T(1,128)}, u32[]{:S(2)}) copy-start(f32[1,2]{1,0:T(1,128)} %copy-done.75) | copy-start | bytes 28
  2591.4 598.1 %all-reduce.12.cloned.1.call-start = ((), (), s32[]{:S(2)}) async-start(), calls=%async_computation.3 | async-start | bytes 27131904
  2665.1 524.4 %copy-start.53 = (f32[3,24,96]{2,1,0:T(8,128)S(1)}, f32[3,24,96]{2,1,0:T(8,128)}, u32[]{:S(2)}) copy-start(f32[3,24,96]{2,1,0:T(8,128)} %copy-done.52) | copy-start | bytes 82948
  2665.1 524.4 %copy-start.57 = (f32[3,24,96]{2,1,0:T(8,128)S(1)}, f32[3,24,96]{2,1,0:T(8,128)}, u32[]{:S(2)}) copy-start(f32[3,24,96]{2,1,0:T(8,128)} %copy-done.56) | copy-start | bytes 82948
  2665.1 524.4 %copy-start.74 = (f32[1,180]{1,0:T(1,128)S(1)}, f32[1,180]{1,0:T(1,128)}, u32[]{:S(2)}) copy-start(f32[1,180]{1,0:T(1,128)} %copy-done.73) | copy-start | bytes 2164
  (150 other events, 1148.0 us)
Sparse Core Ops, SparseCore 0:
  17.1 236.9 all-gather.2
  675.5 897.1 all-reduce.9
  1608.8 236.1 all-gather.4
  2591.5 137.9 all-reduce.13
  2731.9 457.5 all-reduce.11
where the time goes:
time: 3300 us; the launch traced here: 3280 us
  waiting for transfers between devices  1720 us (52%)
  local copies, waits for them, and re-layouts  730 us (22%)
  matrix products  472 us (14%)
  other arithmetic  272 us (8%)
  blocking collectives  40.1 us (1%)
    unnamed x7, waiting for transfers between devices  1270 us
    all_gather x1, waiting for transfers between devices, on_device(): full_normed = lax.all_gather(normed_low, 'head', axis=1, tiled=True)  225 us
    all_gather x1, waiting for transfers between devices, on_device(): full_dattn = lax.all_gather(dattn_low, 'head', axis=1, tiled=True)  163 us
    while x189, local copies, waits for them, and re-layouts  128 us
    dot_general x18, matrix products, conv_apply(): jnp.einsum('nhwc,cf->nhwf', padded[:, row_off:row_off + out_rows, col_off...  110 us
    dynamic_update_slice x12, local copies, waits for them, and re-layouts, on_device(): partials = lax.map(forward_image, (full_normed, valid_size))  90.4 us
  transfers between devices with their start and end apart: 9, of which 6 were waited for; matrix products, arithmetic and copies ran while one was open for 7% of the time, Pallas kernels for 0%

commit v1 on v0

v1 whole, which is shorter than its diff:
```python
import functools

import jax
import jax.numpy as jnp
import numpy as np
from jax import lax
from jax.experimental import pallas as pl
from jax.experimental.pallas import tpu as pltpu
from jax.sharding import PartitionSpec as P

WIN = 8
TOK = WIN * WIN
SHIFT = WIN // 2
LANE = 128
TAP = 256

eps_norm = 1e-05
neg_mask = -100.0
max_norm = 1.0
learn_rate = 0.03
vector_rate = 0.2
beta_one = 0.9
beta_two = 0.999
adam_eps = 1e-08
decay_rate = 0.01
highest = lax.Precision.HIGHEST
f32 = jnp.float32
bf16 = jnp.bfloat16


def nn(a, b):
    return lax.dot_general(a, b, (((1,), (0,)), ((), ())), preferred_element_type=f32)


def nt(a, b):
    return lax.dot_general(a, b, (((1,), (1,)), ((), ())), preferred_element_type=f32)


def head_of(index):
    total = jnp.zeros(index.shape, jnp.int32)
    for k in range(1, 6):
        total = total + (index >= 30 * k).astype(jnp.int32)
    return total


def to_tokens(rows):
    side = rows.shape[1]
    return jnp.concatenate(
        [rows[:, w * WIN : (w + 1) * WIN, :].reshape(TOK, rows.shape[2]) for w in range(side // WIN)],
        axis=0,
    )


def from_tokens(tokens):
    count = tokens.shape[0] // TOK
    return jnp.concatenate(
        [tokens[w * TOK : (w + 1) * TOK].reshape(WIN, WIN, tokens.shape[1]) for w in range(count)],
        axis=1,
    )


def roll_cols(rows, by):
    side = rows.shape[1]
    by = by % side
    return jnp.concatenate([rows[:, by:, :], rows[:, :by, :]], axis=1)


def block_step(x_rows, gy_rows, first_step, edge, base_row, valid, image_side, wts, prep, acc, tmp, c_out, ig_out):
    (vec_ref, qkv_ref, proj_ref, fc1_ref, fc2_ref, conv_ref, bias_ref) = wts
    (vecT, wqT, wkT, wvT, wpT, w1T, w2T, wq, wk, wv, wp, w1, w2, wc, masks, pmask, colmask, rowmask, eye, b1T) = prep
    (acc_conv, acc_qkv, acc_proj, acc_fc1, acc_fc2, acc_ln, acc_rel) = acc
    (g9, a_aug, o_aug, m_aug, g_aug, c_aug, qeo_s, p_s, pb_s, kv_s, first_s, dat_s, dq_s, dkv_s, u2_s, xT_s, slope_s, vt_s, qt_s, kt_s) = tmp
    ch = x_rows.shape[2]
    hid = fc1_ref.shape[1]
    px = x_rows.shape[1] * WIN
    pairs = px // LANE

    @pl.when(first_step)
    def _():
        def split(ref, lo, hi):
            return ref[:, lo:hi]

        vecT[...] = jnp.transpose(vec_ref[...])
        b1T[...] = jnp.concatenate([vecT[:, 7:8], vecT[:, 8:9]], axis=0)
        for dst, dst_t, lo in ((wq, wqT, 0), (wk, wkT, ch), (wv, wvT, 2 * ch)):
            part = split(qkv_ref, lo, lo + ch)
            dst[...] = part.astype(bf16)
            dst_t[...] = jnp.transpose(part).astype(bf16)
        wp[...] = proj_ref[...].astype(bf16)
        wpT[...] = jnp.transpose(proj_ref[...]).astype(bf16)
        w1[...] = fc1_ref[...].astype(bf16)
        w1T[...] = jnp.transpose(fc1_ref[...]).astype(bf16)
        w2[...] = fc2_ref[...].astype(bf16)
        w2T[...] = jnp.transpose(fc2_ref[...]).astype(bf16)
        wc[...] = jnp.zeros_like(wc)
        g9[...] = jnp.zeros_like(g9)
        for tap in range(9):
            wc[:, tap * TAP : tap * TAP + ch] = conv_ref[tap // 3, tap % 3].astype(bf16)
        row = lax.broadcasted_iota(jnp.int32, (ch, LANE), 0)
        lane = lax.broadcasted_iota(jnp.int32, (ch, LANE), 1)
        head = head_of(row)
        low_half = lane < TOK
        odd = (head & 1) == 1
        pair = head >> 1
        one = lambda m: m.astype(f32)
        masks[0] = one(low_half & jnp.logical_not(odd))
        masks[1] = one(jnp.logical_not(low_half) & odd)
        masks[2] = one(low_half & (pair == 0))
        masks[3] = one(jnp.logical_not(low_half) & (pair == 1))
        masks[4] = one(pair == 2)
        lane_pair = head_of(lax.broadcasted_iota(jnp.int32, (TOK, ch), 1)) >> 1
        for p in range(3):
            pmask[p] = one(lane_pair == p)
        key = lax.broadcasted_iota(jnp.int32, (TOK, LANE), 0)
        query = lax.broadcasted_iota(jnp.int32, (TOK, LANE), 1) & (TOK - 1)
        colmask[...] = one(((key & 7) < SHIFT) != ((query & 7) < SHIFT))
        rowmask[...] = one(((key >> 3) < SHIFT) != ((query >> 3) < SHIFT))
        er = lax.broadcasted_iota(jnp.int32, (ch, ch), 0)
        ec = lax.broadcasted_iota(jnp.int32, (ch, ch), 1)
        eye[...] = (er == ec).astype(f32).astype(bf16)
        for ref in (a_aug, o_aug, m_aug, c_aug):
            pad = ref.shape[0] - ch
            ref[ch:, :] = (lax.broadcasted_iota(jnp.int32, (pad, px), 0) == 0).astype(f32).astype(bf16)
        pad = g_aug.shape[0] - hid
        g_aug[hid:, :] = (lax.broadcasted_iota(jnp.int32, (pad, px), 0) == 0).astype(f32).astype(bf16)

    def column(k):
        return vecT[:, k : k + 1]

    def natural(matrix_t):
        return jnp.transpose(matrix_t.astype(f32))

    def stats(v):
        mean = jnp.sum(v, axis=0, keepdims=True) * (1.0 / ch)
        cen = v - mean
        var = jnp.sum(cen * cen, axis=0, keepdims=True) * (1.0 / ch)
        inv = lax.rsqrt(var + eps_norm)
        return cen * inv, inv

    def ln_back(grad, u, inv, gain):
        t = grad * gain
        mean_t = jnp.sum(t, axis=0, keepdims=True) * (1.0 / ch)
        mean_tu = jnp.sum(t * u, axis=0, keepdims=True) * (1.0 / ch)
        return inv * (t - mean_t - u * mean_tu)

    def lane_fold(v):
        out = v[:, :LANE]
        for k in range(1, v.shape[1] // LANE):
            out = out + v[:, k * LANE : (k + 1) * LANE]
        return out

    gyf = gy_rows.astype(f32)
    keep = jnp.where(edge, 0.0, 1.0).astype(f32)
    col = lax.broadcasted_iota(jnp.int32, (1, image_side, ch), 1)
    for j in range(3):
        shifted = roll_cols(gyf, SHIFT + 1 - j)
        if j == 0:
            shifted = jnp.where(col == image_side - SHIFT - 1, 0.0, shifted)
        if j == 2:
            shifted = jnp.where(col == image_side - SHIFT, 0.0, shifted)
        for i in range(3):
            rows = [shifted[r + 2 - i : r + 3 - i] for r in range(WIN)]
            if i == 0:
                rows[SHIFT - 1] = rows[SHIFT - 1] * keep
            if i == 2:
                rows[SHIFT] = rows[SHIFT] * keep
            tap = 3 * i + j
            g9[:, tap * TAP : tap * TAP + ch] = to_tokens(jnp.concatenate(rows, axis=0)).astype(bf16)

    x_tok = to_tokens(roll_cols(x_rows.astype(f32), SHIFT)).astype(bf16)
    xT = nt(eye[...], x_tok)
    xT_s[...] = xT
    u1, inv1 = stats(xT)
    aT = (u1 * column(0) + column(1)).astype(bf16)
    a_aug[:ch, :] = aT
    scale = (ch // 6) ** (-0.5)
    qt_s[...] = ((nn(wqT[...], aT) + column(2)) * scale).astype(bf16).astype(f32)
    kT = nn(wkT[...], aT).astype(bf16).astype(f32)
    vT = (nn(wvT[...], aT) + column(3)).astype(bf16).astype(f32)
    kt_s[...] = kT
    vt_s[...] = vT
    kv_s[0] = jnp.transpose(kT).astype(bf16)
    kv_s[1] = jnp.transpose(vT).astype(bf16)

    def dup(slab):
        other = pltpu.roll(slab, TOK, 1)
        return (
            (slab * masks[0] + other * masks[1]).astype(bf16),
            (other * masks[0] + slab * masks[1]).astype(bf16),
        )

    def spread(slab):
        other = pltpu.roll(slab, TOK, 1)
        first = jnp.concatenate(
            [slab * masks[2] + other * masks[3], (slab * masks[4])[:, :TOK]], axis=1
        ).astype(bf16)
        second = jnp.concatenate(
            [other * masks[2] + slab * masks[3], (other * masks[4])[:, :TOK]], axis=1
        ).astype(bf16)
        return first, second

    def merge(one, two):
        lane = lax.broadcasted_iota(jnp.int32, (ch, LANE), 1)
        crossed = pltpu.roll(jnp.where(lane < TOK, two, one), TOK, 1)
        return jnp.where(masks[0] > 0.5, one, jnp.where(masks[1] > 0.5, two, crossed))

    def by_pair(rows):
        return jnp.concatenate([rows * pmask[p].astype(bf16) for p in range(3)], axis=0)

    def pick_pair(stacked):
        return (
            stacked[:TOK] * pmask[0] + stacked[TOK : 2 * TOK] * pmask[1] + stacked[2 * TOK :] * pmask[2]
        )

    key = lax.broadcasted_iota(jnp.int32, (TOK, LANE), 0)
    key_row = base_row + (key >> 3)
    key_row = jnp.where(key_row >= image_side, key_row - image_side, key_row)
    out_row = key_row >= valid
    edge_f = jnp.where(edge, neg_mask, 0.0).astype(f32)
    for pp in range(pairs):
        cols = slice(pp * LANE, (pp + 1) * LANE)
        q_pair = dup(qt_s[:, cols])
        v_pair = spread(vt_s[:, cols])
        mixed = []
        for half in range(2):
            w = 2 * pp + half
            qeo_s[w] = q_pair[half]
            s = nn(by_pair(kv_s[0, w * TOK : (w + 1) * TOK, :]), q_pair[half])
            key_col = (key & 7) + (w * WIN + SHIFT)
            if w == 2 * pairs - 1:
                key_col = jnp.where(key_col >= image_side, key_col - image_side, key_col)
                apart = rowmask[...] * edge_f
                apart = jnp.where(colmask[...] > 0.5, neg_mask, apart)
            else:
                apart = rowmask[...] * edge_f
            extra = apart + jnp.where(out_row | (key_col >= valid), neg_mask, 0.0)
            s = s.reshape(3, TOK, LANE) + bias_ref[...] + extra[None]
            top = jnp.max(s, axis=1, keepdims=True)
            e = jnp.exp(s - top)
            p = e / jnp.sum(e, axis=1, keepdims=True)
            p = p.reshape(3 * TOK, LANE)
            p_s[w] = p
            pb = p.astype(bf16)
            pb_s[w] = pb
            mixed.append(nn(v_pair[half], pb))
        o_aug[:ch, cols] = merge(*mixed).astype(bf16)

    first = xT_s[...] + (nn(wpT[...], o_aug[:ch, :]) + column(4))
    u2, inv2 = stats(first)
    u2_s[...] = u2
    mT = (u2 * column(5) + column(6)).astype(bf16)
    m_aug[:ch, :] = mT
    hidden = nn(w1T[...], mT) + b1T[...]
    cdf = 0.5 * (1.0 + lax.erf(hidden * 0.7071067811865476))
    g_aug[:hid, :] = (hidden * cdf).astype(bf16)
    slope_s[...] = cdf + hidden * jnp.exp(-0.5 * hidden * hidden) * 0.3989422804014327
    second = first + (nn(w2T[...], g_aug[:hid, :]) + column(9))
    cT = second.astype(bf16)
    c_aug[:ch, :] = cT
    c_out[0] = roll_cols(from_tokens(natural(cT)), -SHIFT).astype(bf16)

    dsecond = nt(wc[...], g9[...])
    acc_conv[...] += nn(c_aug[...], g9[...])
    dbT = dsecond.astype(bf16)
    acc_fc2[...] += nt(g_aug[...], dbT)
    dhT = (nn(w2[...], dbT) * slope_s[...]).astype(bf16)
    acc_fc1[...] += nt(m_aug[...], dhT)
    dm = nn(w1[...], dhT)
    u2 = u2_s[...]
    acc_ln[2] += lane_fold(dm * u2)
    acc_ln[3] += lane_fold(dm)
    dfirst = dsecond + ln_back(dm, u2, inv2, column(5))
    first_s[...] = dfirst
    datT = dfirst.astype(bf16)
    acc_proj[...] += nt(o_aug[...], datT)
    dat_s[...] = nn(wp[...], datT).astype(bf16).astype(f32)

    rel_sum = jnp.zeros((3 * TOK, LANE), f32)
    for pp in range(pairs):
        cols = slice(pp * LANE, (pp + 1) * LANE)
        do_pair = dup(dat_s[:, cols])
        k_pair = spread(kt_s[:, cols])
        dq = []
        for half in range(2):
            w = 2 * pp + half
            toks = slice(w * TOK, (w + 1) * TOK)
            dv = pick_pair(nt(pb_s[w], do_pair[half]))
            dp = nn(by_pair(kv_s[1, toks, :]), do_pair[half])
            p = p_s[w].reshape(3, TOK, LANE)
            dp = dp.reshape(3, TOK, LANE)
            ds = p * (dp - jnp.sum(p * dp, axis=1, keepdims=True))
            ds = ds.reshape(3 * TOK, LANE).astype(bf16)
            rel_sum = rel_sum + ds.astype(f32)
            dk = pick_pair(nt(ds, qeo_s[w]))
            dq.append(nn(k_pair[half], ds))
            dkv_s[0, toks, :] = dk.astype(bf16)
            dkv_s[1, toks, :] = dv.astype(bf16)
        dq_s[:, cols] = merge(*dq).astype(bf16)
    acc_rel[...] += rel_sum

    dqT = dq_s[...]
    acc_qkv[0] += nt(a_aug[...], dqT) * scale
    acc_qkv[1] += nn(a_aug[...], dkv_s[0])
    acc_qkv[2] += nn(a_aug[...], dkv_s[1])
    da = nn(wq[...], dqT) * scale + (nt(wk[...], dkv_s[0]) + nt(wv[...], dkv_s[1]))
    u1, inv1 = stats(xT_s[...])
    acc_ln[0] += lane_fold(da * u1)
    acc_ln[1] += lane_fold(da)
    ig = first_s[...] + ln_back(da, u1, inv1, column(0))
    ig_out[0] = roll_cols(from_tokens(jnp.transpose(ig)), -SHIFT) + gyf[1 : 1 + WIN]


N_ACC = 7
N_WTS = 7


def inner_kernel(image_side, own_rows, info, x_ref, gy_ref, *refs):
    wts, refs = refs[:N_WTS], refs[N_WTS:]
    c_out, ig_out, refs = refs[0], refs[1], refs[2:]
    acc, refs = refs[:N_ACC], refs[N_ACC:]
    prep, tmp = refs[:20], refs[20:]
    image, row_block = pl.program_id(0), pl.program_id(1)
    first_step = (image == 0) & (row_block == 0)

    @pl.when(first_step)
    def _():
        for ref in acc:
            ref[...] = jnp.zeros_like(ref)

    start = row_block * WIN + SHIFT
    x_rows = x_ref[0, pl.ds(start, WIN)]
    gy_rows = gy_ref[0, pl.ds(start - 1, WIN + 2)]
    base_row = info[0] * own_rows + start
    block_step(
        x_rows, gy_rows, first_step, False, base_row, info[2 + image], image_side, wts, prep, acc, tmp, c_out, ig_out
    )


def last_kernel(image_side, own_rows, info, x_ref, gy_ref, xh_ref, gyh_ref, *refs):
    wts, refs = refs[:N_WTS], refs[N_WTS:]
    acc_in, refs = refs[:N_ACC], refs[N_ACC:]
    c_out, ig_out, refs = refs[0], refs[1], refs[2:]
    acc, refs = refs[:N_ACC], refs[N_ACC:]
    prep, tmp = refs[:20], refs[20:]
    image = pl.program_id(0)
    first_step = image == 0

    @pl.when(first_step)
    def _():
        for ref, given in zip(acc, acc_in):
            ref[...] = given[...]

    x_rows = jnp.concatenate([x_ref[0, SHIFT:], xh_ref[0]], axis=0)
    gy_rows = jnp.concatenate([gy_ref[0, SHIFT - 1 :], gyh_ref[0]], axis=0)
    base_row = info[0] * own_rows + own_rows - SHIFT
    block_step(
        x_rows, gy_rows, first_step, info[1] == 1, base_row, info[2 + image], image_side, wts, prep, acc, tmp, c_out, ig_out
    )


def whole(shape):
    return pl.BlockSpec(shape, lambda *_: (0,) * len(shape))


def acc_shapes(ch, hid):
    up = lambda n: -(-(n + 1) // 16) * 16
    return [
        (up(ch), 9 * TAP),
        (3, up(ch), ch),
        (up(ch), ch),
        (up(ch), hid),
        (up(hid), ch),
        (4, ch, LANE),
        (3 * TOK, LANE),
    ]


def scratches(ch, hid, px, vec_rows):
    up = lambda n: -(-(n + 1) // 16) * 16
    v = pltpu.VMEM
    prep = [
        v((ch, vec_rows), f32),
        v((ch, ch), bf16), v((ch, ch), bf16), v((ch, ch), bf16), v((ch, ch), bf16),
        v((hid, ch), bf16), v((ch, hid), bf16),
        v((ch, ch), bf16), v((ch, ch), bf16), v((ch, ch), bf16), v((ch, ch), bf16),
        v((ch, hid), bf16), v((hid, ch), bf16),
        v((ch, 9 * TAP), bf16),
        v((5, ch, LANE), f32),
        v((3, TOK, ch), f32),
        v((TOK, LANE), f32),
        v((TOK, LANE), f32),
        v((ch, ch), bf16),
        v((hid, 1), f32),
    ]
    wins = px // TOK
    tmp = [
        v((px, 9 * TAP), bf16),
        v((up(ch), px), bf16), v((up(ch), px), bf16), v((up(ch), px), bf16), v((up(hid), px), bf16), v((up(ch), px), bf16),
        v((wins, ch, LANE), bf16),
        v((wins, 3 * TOK, LANE), f32),
        v((wins, 3 * TOK, LANE), bf16),
        v((2, px, ch), bf16),
        v((ch, px), f32),
        v((ch, px), f32),
        v((ch, px), bf16),
        v((2, px, ch), bf16),
        v((ch, px), f32),
        v((ch, px), f32),
        v((hid, px), f32),
        v((ch, px), f32),
        v((ch, px), f32),
        v((ch, px), f32),
    ]
    return prep + tmp


def conv_kernel(image_side, own_rows, info, hc_ref, c1_ref, c2_ref, hg_ref, g1_ref, g2_ref, x_ref, vec_ref, conv_ref, out_ref, ig_ref, cs, wc):
    ch = x_ref.shape[3]

    @pl.when(pl.program_id(0) == 0)
    def _():
        wc[...] = jnp.zeros_like(wc)
        cs[...] = jnp.zeros_like(cs)
        for tap in range(9):
            wc[tap * TAP : tap * TAP + ch, :] = conv_ref[tap // 3, tap % 3].astype(bf16)

    first = jnp.where(info[0] == 0, 0.0, 1.0).astype(f32)
    last = jnp.where(info[1] == 1, 0.0, 1.0).astype(f32)
    need = own_rows + 2
    col = lax.broadcasted_iota(jnp.int32, (1, image_side, ch), 1)
    halo = hc_ref.shape[1]
    for r in range(need):
        if r < halo:
            row = hc_ref[0, r : r + 1]
        elif r - halo < c1_ref.shape[1]:
            row = c1_ref[0, r - halo : r - halo + 1]
        else:
            at = r - halo - c1_ref.shape[1]
            row = c2_ref[0, at : at + 1]
        row = row.astype(f32)
        if r == 0:
            row = row * first
        if r == need - 1:
            row = row * last
        left = jnp.where(col == 0, 0.0, roll_cols(row, -1))
        right = jnp.where(col == image_side - 1, 0.0, roll_cols(row, 1))
        at = slice(r * image_side, (r + 1) * image_side)
        cs[at, 0:ch] = left[0].astype(bf16)
        cs[at, TAP : TAP + ch] = row[0].astype(bf16)
        cs[at, 2 * TAP : 2 * TAP + ch] = right[0].astype(bf16)
    group = 4
    bias = vec_ref[10:11, :]
    for r in range(0, own_rows, group):
        total = None
        for i in range(3):
            at = slice((r + i) * image_side, (r + i + group) * image_side)
            term = nn(cs[at, :], wc[i * 3 * TAP : (i + 1) * 3 * TAP, :])
            total = term if total is None else total + term
        total = total + bias
        total = total.reshape(group, image_side, ch) + x_ref[0, r : r + group].astype(f32)
        out_ref[0, r : r + group] = total.astype(bf16)
    head = hg_ref.shape[1]
    mid = g1_ref.shape[1]
    ig_ref[0, :head] = hg_ref[0]
    ig_ref[0, head : head + mid] = g1_ref[0]
    ig_ref[0, head + mid :] = g2_ref[0, : own_rows - head - mid]


def adam_kernel(scal, a_conv, a_qkv, a_proj, a_fc1, a_fc2, a_ln, a_rel, *refs):
    weights, firsts, seconds = refs[0:7], refs[7:14], refs[14:21]
    norm_ref, outs = refs[21], refs[22:43]
    ch = weights[2].shape[0]
    hid = weights[5].shape[0]
    g_vec = [
        a_ln[0:1, :],
        a_ln[1:2, :],
        a_qkv[0, ch : ch + 1, :],
        a_qkv[2, ch : ch + 1, :],
        a_proj[ch : ch + 1, :],
        a_ln[2:3, :],
        a_ln[3:4, :],
        a_fc1[ch : ch + 1, :ch],
        a_fc1[ch : ch + 1, ch:],
        a_fc2[hid : hid + 1, :],
        a_conv[ch : ch + 1, 4 * TAP : 4 * TAP + ch],
    ]
    vec = jnp.concatenate(g_vec, axis=0)
    qkv = jnp.concatenate([a_qkv[k, :ch, :] for k in range(3)], axis=1)
    small = [vec, qkv, a_proj[:ch, :], a_rel[...], a_fc1[:ch, :], a_fc2[:hid, :]]
    taps = [a_conv[:ch, t * TAP : t * TAP + ch] for t in range(9)]
    total = jnp.zeros((1, 1), f32)
    for g in small + taps:
        total = total + jnp.sum(jnp.sum(g * g, axis=0, keepdims=True), axis=1, keepdims=True)
    norm = jnp.sqrt(total)
    norm_ref[...] = norm
    clip = jnp.minimum(1.0, max_norm / (norm + 1e-06))
    fix_one, fix_two = scal[0], scal[1]

    def update(w, m1, m2, g, rate):
        g = g * clip
        m1 = beta_one * m1 + (1.0 - beta_one) * g
        m2 = beta_two * m2 + (1.0 - beta_two) * g * g
        step = (m1 / fix_one) / (jnp.sqrt(m2 / fix_two) + adam_eps)
        return w - rate * (step + decay_rate * w), m1, m2

    for k, g in enumerate(small):
        new = update(weights[k][...], firsts[k][...], seconds[k][...], g, vector_rate if k == 0 else learn_rate)
        for ref, value in zip(outs[3 * k : 3 * k + 3], new):
            ref[...] = value
    for t, g in enumerate(taps):
        at = (t // 3, t % 3)
        new = update(weights[6][at], firsts[6][at], seconds[6][at], g, learn_rate)
        for ref, value in zip(outs[18:21], new):
            ref[at] = value


def relative_onehot_keys_first():
    position = np.arange(TOK)
    pos_row, pos_col = position // WIN, position % WIN
    span = 2 * WIN - 1
    index = (pos_row[None, :] - pos_row[:, None] + WIN - 1) * span + (
        pos_col[None, :] - pos_col[:, None] + WIN - 1
    )
    return index.reshape(-1), span * span


def on_device(
    images, cotangent, valid_size,
    vectors, vectors_first, vectors_second,
    qkv_weight, qkv_first, qkv_second,
    proj_weight, proj_first, proj_second,
    rel_table, rel_first, rel_second,
    fc1_weight, fc1_first, fc1_second,
    fc2_weight, fc2_first, fc2_second,
    conv_weight, conv_first, conv_second,
    step, sr_crops, hr_crops, psnr_running,
):
    count, own_rows, image_side, ch = images.shape
    hid = fc1_weight.shape[1]
    px = image_side * WIN
    blocks = own_rows // WIN
    heads = lax.axis_size("head")
    place = lax.axis_index("head")
    to_lower = [((i + 1) % heads, i) for i in range(heads)]
    to_upper = [(i, (i + 1) % heads) for i in range(heads)]
    info = jnp.concatenate(
        [
            jnp.stack([place, (place == heads - 1).astype(jnp.int32)]).astype(jnp.int32),
            valid_size.astype(jnp.int32),
        ]
    )
    halo = lax.ppermute(
        jnp.concatenate([images[:, :SHIFT], cotangent[:, : SHIFT + 1]], axis=1), "head", to_lower
    )
    x_halo, gy_halo = halo[:, :SHIFT], halo[:, SHIFT:]

    index, span = relative_onehot_keys_first()
    onehot = (jnp.asarray(index)[:, None] == jnp.arange(span)[None, :]).astype(f32)
    bias = jnp.dot(onehot, rel_table, precision=highest)
    bias = bias.reshape(TOK, TOK, 3, 2).transpose(2, 0, 3, 1).reshape(3, TOK, LANE)

    wts = (vectors, qkv_weight, proj_weight, fc1_weight, fc2_weight, conv_weight, bias)
    wts_specs = [whole(w.shape) for w in wts]
    acc_dims = acc_shapes(ch, hid)
    acc_types = [jax.ShapeDtypeStruct(s, f32) for s in acc_dims]
    smem = pl.BlockSpec(memory_space=pltpu.SMEM)
    params = pltpu.CompilerParams(
        dimension_semantics=("arbitrary", "arbitrary"), vmem_limit_bytes=60 * 1024 * 1024
    )
    c1, ig1, *acc = pl.pallas_call(
        functools.partial(inner_kernel, image_side, own_rows),
        grid=(count, blocks - 1),
        in_specs=[
            smem,
            pl.BlockSpec((1, own_rows, image_side, ch), lambda n, r: (n, 0, 0, 0)),
            pl.BlockSpec((1, own_rows, image_side, ch), lambda n, r: (n, 0, 0, 0)),
            *wts_specs,
        ],
        out_specs=[
            pl.BlockSpec((1, WIN, image_side, ch), lambda n, r: (n, r, 0, 0)),
            pl.BlockSpec((1, WIN, image_side, ch), lambda n, r: (n, r, 0, 0)),
            *[whole(s) for s in acc_dims],
        ],
        out_shape=[
            jax.ShapeDtypeStruct((count, own_rows - WIN, image_side, ch), bf16),
            jax.ShapeDtypeStruct((count, own_rows - WIN, image_side, ch), f32),
            *acc_types,
        ],
        scratch_shapes=scratches(ch, hid, px, vectors.shape[0]),
        compiler_params=params,
        name="inner_windows",
    )(info, images, cotangent, *wts)
    c2, ig2, *acc = pl.pallas_call(
        functools.partial(last_kernel, image_side, own_rows),
        grid=(count,),
        in_specs=[
            smem,
            pl.BlockSpec((1, WIN, image_side, ch), lambda n: (n, blocks - 1, 0, 0)),
            pl.BlockSpec((1, WIN, image_side, ch), lambda n: (n, blocks - 1, 0, 0)),
            pl.BlockSpec((1, SHIFT, image_side, ch), lambda n: (n, 0, 0, 0)),
            pl.BlockSpec((1, SHIFT + 1, image_side, ch), lambda n: (n, 0, 0, 0)),
            *wts_specs,
            *[whole(s) for s in acc_dims],
        ],
        out_specs=[
            pl.BlockSpec((1, WIN, image_side, ch), lambda n: (n, 0, 0, 0)),
            pl.BlockSpec((1, WIN, image_side, ch), lambda n: (n, 0, 0, 0)),
            *[whole(s) for s in acc_dims],
        ],
        out_shape=[
            jax.ShapeDtypeStruct((count, WIN, image_side, ch), bf16),
            jax.ShapeDtypeStruct((count, WIN, image_side, ch), f32),
            *acc_types,
        ],
        scratch_shapes=scratches(ch, hid, px, vectors.shape[0]),
        compiler_params=pltpu.CompilerParams(
            dimension_semantics=("arbitrary",), vmem_limit_bytes=60 * 1024 * 1024
        ),
        name="last_windows",
    )(info, images, cotangent, x_halo, gy_halo, *wts, *acc)

    c_halo = lax.ppermute(c2[:, WIN - SHIFT - 1 :], "head", to_upper)
    ig_halo = lax.ppermute(ig2[:, WIN - SHIFT :], "head", to_upper)

    a_conv, a_qkv, a_proj, a_fc1, a_fc2, a_ln, a_rel = acc
    rel = a_rel.reshape(3, TOK, 2, TOK).transpose(0, 2, 1, 3).reshape(6, TOK * TOK)
    rel = jnp.dot(rel, onehot, precision=highest).T
    ln = jnp.sum(a_ln, axis=2)

    difference = sr_crops - hr_crops
    luma = (65.481 * difference[:, 0] + 128.553 * difference[:, 1] + 24.966 * difference[:, 2]) / 255.0
    mean_error = jnp.mean(luma * luma, axis=(1, 2))
    local_psnr = jnp.sum(-10.0 * jnp.log10(mean_error + 1e-06))
    a_conv, a_qkv, a_proj, a_fc1, a_fc2, ln, rel, psnr = lax.psum(
        (a_conv, a_qkv, a_proj, a_fc1, a_fc2, ln, rel, local_psnr), ("dp", "head")
    )
    psnr_total = psnr_running + psnr

    image_block = lambda rows: pl.BlockSpec((1, rows, image_side, ch), lambda n: (n, 0, 0, 0))
    output, image_grad = pl.pallas_call(
        functools.partial(conv_kernel, image_side, own_rows),
        grid=(count,),
        in_specs=[
            smem,
            image_block(SHIFT + 1), image_block(own_rows - WIN), image_block(WIN),
            image_block(SHIFT), image_block(own_rows - WIN), image_block(WIN),
            image_block(own_rows),
            whole(vectors.shape), whole(conv_weight.shape),
        ],
        out_specs=[image_block(own_rows), image_block(own_rows)],
        out_shape=[
            jax.ShapeDtypeStruct(images.shape, bf16),
            jax.ShapeDtypeStruct(images.shape, f32),
        ],
        scratch_shapes=[
            pltpu.VMEM(((own_rows + 2) * image_side, 3 * TAP), bf16),
            pltpu.VMEM((9 * TAP, ch), bf16),
        ],
        compiler_params=pltpu.CompilerParams(
            dimension_semantics=("arbitrary",), vmem_limit_bytes=60 * 1024 * 1024
        ),
        name="conv_output",
    )(info, c_halo, c1, c2, ig_halo, ig1, ig2, images, vectors, conv_weight)

    step_count = step[0].astype(f32)
    scal = jnp.stack([1.0 - beta_one**step_count, 1.0 - beta_two**step_count])
    weights = (vectors, qkv_weight, proj_weight, rel_table, fc1_weight, fc2_weight, conv_weight)
    firsts = (vectors_first, qkv_first, proj_first, rel_first, fc1_first, fc2_first, conv_first)
    seconds = (vectors_second, qkv_second, proj_second, rel_second, fc1_second, fc2_second, conv_second)
    vmem = pl.BlockSpec(memory_space=pltpu.VMEM)
    grad_norm, *updated = pl.pallas_call(
        adam_kernel,
        in_specs=[smem] + [vmem] * 28,
        out_specs=[vmem] * 22,
        out_shape=[jax.ShapeDtypeStruct((1, 1), f32)]
        + [jax.ShapeDtypeStruct(w.shape, f32) for w in weights for _ in range(3)],
        compiler_params=pltpu.CompilerParams(vmem_limit_bytes=60 * 1024 * 1024),
        name="adam",
    )(scal, a_conv, a_qkv, a_proj, a_fc1, a_fc2, ln, rel, *weights, *firsts, *seconds)
    return (output, image_grad, grad_norm.reshape(1), psnr_total, *updated)


def solution(mesh):
    pixels = P("dp", "head", None, None)
    crops = P(("dp", "head"), None, None, None)
    placed = (pixels, pixels, P("dp")) + (P(),) * 22 + (crops, crops, P())
    return jax.shard_map(
        on_device,
        mesh=mesh,
        in_specs=placed,
        out_specs=(pixels, pixels) + (P(),) * 23,
        check_vma=False,
    )
```

time: 3300 us -> 331 us (0.10)
  waiting for transfers between devices: 1720 us -> 37.1 us
  local copies, waits for them, and re-layouts: 730 us -> 59 us
  matrix products: 472 us -> 5.86 us
  other arithmetic: 272 us -> 4.43 us
  Pallas kernels: 0 us -> 132 us
    unnamed x7 -> x1, waiting for transfers between devices: 1270 us -> 0.02 us
    dot_general x82 -> x2, matrix products: 408 us -> 5.86 us  [the longest x1 3.3 us: on_device(): rel = jnp.dot(rel, onehot, precision=highest).T]
    all_gather x2 -> x0, waiting for transfers between devices: 388 us -> none  [the longest x1 225 us: on_device(): full_normed = lax.all_gather(normed_low, 'head', axis=1, tiled=True)]
    reshape x41 -> x6, local copies, waits for them, and re-layouts: 155 us -> 1.34 us  [the longest x3 1.06 us: on_device(): bias.reshape(TOK, TOK, 3, 2).transpose(2, 0, 3, 1).reshape(3, TOK, LANE)]
    while x192 -> x0, local copies, waits for them, and re-layouts: 147 us -> none
    slice x55 -> x9, local copies, waits for them, and re-layouts: 152 us -> 7.04 us  [the longest x2 2.26 us: on_device(): x_halo, gy_halo = (halo[:, :SHIFT], halo[:, SHIFT:])]
    pallas_call x0 -> x4, Pallas kernels: none -> 132 us  [the longest x1 67.4 us: on_device(): pl.pallas_call(functools.partial(inner_kernel, image_side, own_rows), gri...]
    convert_element_type x16 -> x0, local copies, waits for them, and re-layouts: 104 us -> none  [the longest x6 40.3 us: attend(): (mixed_rows.astype(jnp.bfloat16) * slot_scale[:, None]).astype(jnp.bfloat16)]
  transfers between devices with their start and end apart: 9 -> 4, of which waited for: 6 -> 1; matrix products, arithmetic and copies ran while one was open for 7% -> 15% of each run, Pallas kernels for 0% -> 25%
where the time goes in v1:
time: 331 us; the launch traced here: 328 us
  Pallas kernels  132 us (40%)
  blocking collectives  66.7 us (20%)
  local copies, waits for them, and re-layouts  59 us (18%)
  waiting for transfers between devices  37.1 us (11%)
  between operations  17.7 us (5%)
  matrix products  5.86 us (2%)
  starting transfers between devices  5.32 us (2%)
  other arithmetic  4.43 us (1%)
    pallas_call x1, Pallas kernels, on_device(): pl.pallas_call(functools.partial(inner_kernel, image_side, own_rows), gri...  67.4 us
    psum x1, blocking collectives, on_device(): lax.psum((a_conv, a_qkv, a_proj, a_fc1, a_fc2, ln, rel, local_psnr), ('dp...  66.7 us
    unnamed x46, local copies, waits for them, and re-layouts  47.6 us
    pallas_call x1, Pallas kernels, on_device(): pl.pallas_call(functools.partial(last_kernel, image_side, own_rows), grid...  37.1 us
    psum x1, waiting for transfers between devices, on_device(): lax.psum((a_conv, a_qkv, a_proj, a_fc1, a_fc2, ln, rel, local_psnr), ('dp...  37.1 us
    pallas_call x1, Pallas kernels, on_device(): pl.pallas_call(functools.partial(conv_kernel, image_side, own_rows), grid...  16.1 us
    pallas_call x1, Pallas kernels, on_device(): pl.pallas_call(adam_kernel, in_specs=[smem] + [vmem] * 28, out_specs=[vme...  11 us
  transfers between devices with their start and end apart: 4, of which 1 were waited for; matrix products, arithmetic and copies ran while one was open for 15% of the time, Pallas kernels for 25%

profile of v1, /device:TPU:0, one launch (start us, length us, event | category | flops | bytes accessed | tf_op | source)
XLA Modules:
  0.0 327.6 jit_solution(8380163727790059545)
XLA Ops:
  11.3 5.0 %collective-permute-start = (bf16[3,9,96,180]{2,3,1,0:T(8,128)(2,1)}, bf16[3,9,96,180]{2,3,1,0:T(8,128)(2,1)}, u32[]{:S(2)}, u32[]{:S(2)}) collective-permute-start(bf16[3,9,96,180]{2,3,1,0:T(8,128)(2,1)} %pad_maximum_fusion), channel_id=1, source_target_pairs={{1,0},{2,1},{3,2},{0,3},{5,4},{6,5},{7,6},{4,7},{9,8},{10,9},{11,1... | collective-permute-start | bytes 2799368 | tf_op jit(solution)/shard_map/ppermute | solution.py:552
  16.4 6.6 %copy.113.x_ref = bf16[3,24,96,180]{3,2,1,0:T(8,128)(2,1)} copy(bf16[3,24,96,180]{2,1,3,0:T(8,128)(2,1)} %param.29) | data formatting | bytes 4976640 | tf_op args[0]
  23.0 4.9 %copy.114.gy_ref = bf16[3,24,96,180]{3,2,1,0:T(8,128)(2,1)} copy(bf16[3,24,96,180]{2,1,3,0:T(8,128)(2,1)S(1)} %copy-done) | data formatting | bytes 4976640 | tf_op args[1]
  28.0 1.9 copy.115.refs_4_.refs_5_
  29.8 2.6 fusion.1
  34.0 67.4 %inner_windows.1 = (bf16[3,16,96,180]{3,2,1,0:T(8,128)(2,1)}, f32[3,16,96,180]{3,2,1,0:T(8,128)}, f32[192,2304]{1,0:T(8,128)}, f32[3,192,180]{2,1,0:T(8,128)}, f...) custom-call(s32[5]{0:T(128)} %pad_add_fusion.info, ...), custom_call_target="tpu_custom_call" | custom-call | tf_op jit(solution)/shard_map/inner_windows/pallas_call | solution.py:570
  106.0 37.1 %last_windows.1 = (bf16[3,8,96,180]{3,2,1,0:T(8,128)(2,1)}, f32[3,8,96,180]{3,2,1,0:T(8,128)}, f32[192,2304]{1,0:T(8,128)}, f32[3,192,180]{2,1,0:T(8,128)}, f32[...) custom-call(s32[5]{0:T(128)} %pad_add_fusion.info, ...), custom_call_target="tpu_custom_call" | custom-call | tf_op jit(solution)/shard_map/last_windows/pallas_call | solution.py:593
  143.2 1.6 copy-done.1
  144.9 1.7 copy.117
  150.2 1.9 copy.126.refs_12_
  153.0 1.9 copy.128.refs_19_
  157.8 3.3 %fusion.2 = f32[225,6]{1,0:T(8,128)S(1)} fusion(f32[6,4096]{1,0:T(8,128)S(1)} %reshape.90, s32[4096]{0:T(1024)S(1)} %copy-done.12), kind=kOutput, calls=%fused_computation.3 | convolution fusion | flops 68198400 | bytes 120088 | tf_op jit(solution)/shard_map/dot_general | solution.py:627
  161.1 66.7 %all-reduce = (f32[4,180]{1,0:T(4,128)}, f32[225,6]{1,0:T(8,128)}, f32[1]{0:T(128)}) all-reduce(f32[4,180]{1,0:T(4,128)S(1)} %reduce_sum.27, f32[225,6]{1,0:T(8,128)S(1)} %fusion.2, f32[1]{0:T(128)} %bitcast.5), channel_id=1, replica_groups=mesh['dp'=8,'head'=4] {'dp','head'}, use_global_device_ids=true, to_apply=%region_6.0 | all-reduce | flops 2071 | bytes 16568 | tf_op jit(solution)/shard_map/psum | solution.py:634
  229.7 1.7 copy.119.hg_ref
  231.4 16.1 %conv_output.1 = (bf16[3,24,96,180]{3,2,1,0:T(8,128)(2,1)}, f32[3,24,96,180]{3,2,1,0:T(8,128)}) custom-call(s32[5]{0:T(128)} %pad_add_fusion.info, bf16[3,5,96,180]{3,2,1,0:T(8,128)(2,1)} %copy.118.hc_ref, bf16[3,16,96,180]{3,2,1,0:T(8,128)(2,1)} %get-tuple-element.75.c1_ref, bf16[3,8,96,180]{3,2,1,0:T(8,128)(2,1)} %get-tuple-element.74.c2_ref, ...), custom_call_target="tpu_custom_call" | custom-call | tf_op jit(solution)/shard_map/conv_output/pallas_call | solution.py:640
  247.5 6.3 %copy.129 = bf16[3,24,96,180]{2,1,3,0:T(8,128)(2,1)} copy(bf16[3,24,96,180]{3,2,1,0:T(8,128)(2,1)} %get-tuple-element.159) | data formatting | bytes 4976640
  253.8 8.2 %copy.130 = f32[3,24,96,180]{2,1,3,0:T(8,128)} copy(f32[3,24,96,180]{3,2,1,0:T(8,128)} %get-tuple-element.160) | data formatting | bytes 9953280
  262.0 37.1 %all-reduce.4.cloned.1.call-done = (f32[192,2304]{1,0:T(8,128)}, f32[3,192,180]{2,1,0:T(8,128)}, f32[192,180]{1,0:T(8,128)}, f32[192,360]{1,0:T(8,128)}, f32[368,180]{1,0:T(8,128)}) async-done(((f32[192,2304]{1,0:T(8,128)}, f32[3,192,180]{2,1,0:T(8,128)}, f32[192,180]{1,0:T(8,128)}, f32[192,360]{1,0:T(8,128)}, f32[368,180]{1,0:T(8,128)}), (f32[192,2304]{1,0:T(8,128)}, f32[3,192,180]{2,1,0:T(8,128)}, ...) | async-done | bytes 2863888 | tf_op jit(solution)/shard_map/psum | solution.py:634
  299.1 11.0 %adam.1 = (f32[1,1]{1,0:T(1,128)}, f32[11,180]{1,0:T(8,128)}, f32[11,180]{1,0:T(8,128)}, f32[11,180]{1,0:T(8,128)}, f32[180,540]{1,0:T(8,128)}, /*index=5*/f32[1...) custom-call(f32[2]{0:T(128)} %pad_maximum_fusion.1.scal, ...), custom_call_target="tpu_custom_call" | custom-call | tf_op jit(solution)/shard_map/adam/pallas_call | solution.py:671
  310.1 1.6 copy.131
  311.8 1.6 copy.132
  313.3 1.6 copy.133
  314.9 1.8 copy.134
  316.8 1.8 copy.135
  (62 shorter events, 18.4 us)
Async XLA Ops:
  7.2 1.2 slice-start
  7.2 291.9 %all-reduce.4.cloned.1.call-start = ((), (), s32[]{:S(2)}) async-start(), calls=%async_computation | async-start | bytes 6455296 | tf_op jit(solution)/shard_map/psum | solution.py:634
  11.3 90.1 %collective-permute-start = (bf16[3,9,96,180]{2,3,1,0:T(8,128)(2,1)}, bf16[3,9,96,180]{2,3,1,0:T(8,128)(2,1)}, u32[]{:S(2)}, u32[]{:S(2)}) collective-permute-start(bf16[3,9,96,180]{2,3,1,0:T(8,128)(2,1)} %pad_maximum_fusion), channel_id=1, source_target_pairs={{1,0},{2,1},{3,2},{0,3},{5,4},{6,5},{7,6},{4,7},{9,8},{10,9},{11,1... | collective-permute-start | bytes 2799368 | tf_op jit(solution)/shard_map/ppermute | solution.py:552
  16.4 6.6 %copy-start = (bf16[3,24,96,180]{2,1,3,0:T(8,128)(2,1)S(1)}, bf16[3,24,96,180]{2,1,3,0:T(8,128)(2,1)}, u32[]{:S(2)}) copy-start(bf16[3,24,96,180]{2,1,3,0:T(8,128)(2,1)} %param.30) | copy-start | bytes 7464964
  23.0 6.8 %copy-start.7 = (f32[225,6]{0,1:T(8,128)S(1)}, f32[225,6]{0,1:T(8,128)}, u32[]{:S(2)}) copy-start(f32[225,6]{0,1:T(8,128)} %param.41) | copy-start | bytes 16204
  23.0 6.8 %copy-start.11 = (s32[4096]{0:T(1024)S(1)}, s32[4096]{0:T(1024)}, u32[]{:S(2)}) copy-start(s32[4096]{0:T(1024)} %constant.38.clone) | copy-start | bytes 49156
  28.0 5.5 %copy-start.10 = (s32[3]{0:T(128)S(1)}, s32[3]{0:T(128)}, u32[]{:S(2)}) copy-start(s32[3]{0:T(128)} %param.31) | copy-start | bytes 40
  143.1 1.7 copy-start.1
  144.9 2.4 copy-start.2
  146.6 2.9 copy-start.8
  146.6 83.1 %collective-permute-start.2 = (f32[3,4,96,180]{2,1,3,0:T(4,128)}, f32[3,4,96,180]{2,1,3,0:T(4,128)S(1)}, u32[]{:S(2)}, u32[]{:S(2)}) collective-permute-start(f32[3,4,96,180]{2,1,3,0:T(4,128)} %copy.117), channel_id=1, source_target_pairs={{0,1},{1,2},{2,3},{3,0},{4,5},{5,6},{6,7},{7,4},{8,9},{9,10},{10,1... | collective-permute-start | bytes 2488328 | tf_op jit(solution)/shard_map/ppermute | solution.py:623
  147.3 4.9 %copy-start.9 = (f32[225,6]{0,1:T(8,128)S(1)}, f32[225,6]{0,1:T(8,128)}, u32[]{:S(2)}) copy-start(f32[225,6]{0,1:T(8,128)} %param.43) | copy-start | bytes 16204
  147.4 8.1 %copy-start.5 = (f32[2,3,96,96]{3,2,1,0:T(8,128)S(1)}, f32[2,3,96,96]{3,2,1,0:T(8,128)}, u32[]{:S(2)}) copy-start(f32[2,3,96,96]{3,2,1,0:T(8,128)} %param.54) | copy-start | bytes 663556
  147.8 9.4 %copy-start.6 = (f32[192,128]{1,0:T(8,128)S(1)}, f32[192,128]{1,0:T(8,128)}, u32[]{:S(2)}) copy-start(f32[192,128]{1,0:T(8,128)} %get-tuple-element.86) | copy-start | bytes 294916
  147.8 80.6 %collective-permute-start.1 = (bf16[3,5,96,180]{2,3,1,0:T(8,128)(2,1)S(1)}, bf16[3,5,96,180]{2,3,1,0:T(8,128)(2,1)S(1)}, u32[]{:S(2)}, u32[]{:S(2)}) collective-permute-start(bf16[3,5,96,180]{2,3,1,0:T(8,128)(2,1)S(1)} %copy.116), channel_id=1, source_target_pairs={{0,1},{1,2},{2,3},{3,0},{4,5},{5,6},{6,7},{7,4},{8,9},{9,10},{10,1... | collective-permute-start | bytes 1555208 | tf_op jit(solution)/shard_map/ppermute | solution.py:622
  150.2 7.3 %copy-start.3 = (f32[4,180,128]{2,1,0:T(8,128)S(1)}, f32[4,180,128]{2,1,0:T(8,128)}, u32[]{:S(2)}) copy-start(f32[4,180,128]{2,1,0:T(8,128)} %get-tuple-element.85) | copy-start | bytes 1105924
  152.2 5.6 %copy-start.12 = (s32[4096]{0:T(1024)S(1)}, s32[4096]{0:T(1024)}, u32[]{:S(2)}) copy-start(s32[4096]{0:T(1024)} %constant.38.clone) | copy-start | bytes 49156
  310.1 8.5 %copy-start.4 = (f32[360,180]{1,0:T(8,128)S(1)}, f32[360,180]{1,0:T(8,128)}, u32[]{:S(2)}) copy-start(f32[360,180]{1,0:T(8,128)} %get-tuple-element.180) | copy-start | bytes 777604
Sparse Core Ops, SparseCore 0:
  143.3 155.7 all-reduce.3

commit v2 on v1

--- a/solution.py
+++ b/solution.py
@@ -90,8 +90,8 @@
         wpT[...] = jnp.transpose(proj_ref[...]).astype(bf16)
         w1[...] = fc1_ref[...].astype(bf16)
         w1T[...] = jnp.transpose(fc1_ref[...]).astype(bf16)
-        w2[...] = fc2_ref[...].astype(bf16)
-        w2T[...] = jnp.transpose(fc2_ref[...]).astype(bf16)
+        w2T[...] = fc2_ref[...].astype(bf16)
+        w2[...] = jnp.transpose(fc2_ref[...]).astype(bf16)
         wc[...] = jnp.zeros_like(wc)
         g9[...] = jnp.zeros_like(g9)
         for tap in range(9):
@@ -121,8 +121,6 @@
         for ref in (a_aug, o_aug, m_aug, c_aug):
             pad = ref.shape[0] - ch
             ref[ch:, :] = (lax.broadcasted_iota(jnp.int32, (pad, px), 0) == 0).astype(f32).astype(bf16)
-        pad = g_aug.shape[0] - hid
-        g_aug[hid:, :] = (lax.broadcasted_iota(jnp.int32, (pad, px), 0) == 0).astype(f32).astype(bf16)
 
     def column(k):
         return vecT[:, k : k + 1]
@@ -252,9 +250,9 @@
     m_aug[:ch, :] = mT
     hidden = nn(w1T[...], mT) + b1T[...]
     cdf = 0.5 * (1.0 + lax.erf(hidden * 0.7071067811865476))
-    g_aug[:hid, :] = (hidden * cdf).astype(bf16)
+    g_aug[...] = (hidden * cdf).astype(bf16)
     slope_s[...] = cdf + hidden * jnp.exp(-0.5 * hidden * hidden) * 0.3989422804014327
-    second = first + (nn(w2T[...], g_aug[:hid, :]) + column(9))
+    second = first + (nn(w2T[...], g_aug[...]) + column(9))
     cT = second.astype(bf16)
     c_aug[:ch, :] = cT
     c_out[0] = roll_cols(from_tokens(natural(cT)), -SHIFT).astype(bf16)
@@ -262,7 +260,8 @@
     dsecond = nt(wc[...], g9[...])
     acc_conv[...] += nn(c_aug[...], g9[...])
     dbT = dsecond.astype(bf16)
-    acc_fc2[...] += nt(g_aug[...], dbT)
+    acc_fc2[...] += nt(dbT, g_aug[...])
+    acc_ln[4] += lane_fold(dbT.astype(f32))
     dhT = (nn(w2[...], dbT) * slope_s[...]).astype(bf16)
     acc_fc1[...] += nt(m_aug[...], dhT)
     dm = nn(w1[...], dhT)
@@ -339,7 +338,7 @@
 def last_kernel(image_side, own_rows, info, x_ref, gy_ref, xh_ref, gyh_ref, *refs):
     wts, refs = refs[:N_WTS], refs[N_WTS:]
     acc_in, refs = refs[:N_ACC], refs[N_ACC:]
-    c_out, ig_out, refs = refs[0], refs[1], refs[2:]
+    sr_ref, hr_ref, c_out, ig_out, pack_out, refs = *refs[:5], refs[5:]
     acc, refs = refs[:N_ACC], refs[N_ACC:]
     prep, tmp = refs[:20], refs[20:]
     image = pl.program_id(0)
@@ -356,6 +355,65 @@
     block_step(
         x_rows, gy_rows, first_step, info[1] == 1, base_row, info[2 + image], image_side, wts, prep, acc, tmp, c_out, ig_out
     )
+
+    @pl.when(image == pl.num_programs(0) - 1)
+    def _():
+        pack_gradients(info[2 + pl.num_programs(0)], acc, sr_ref, hr_ref, pack_out)
+
+
+def pack_rows(ch):
+    up = -(-ch // 8) * 8
+    blocks = 17
+    vec_at = (blocks + (blocks + 1) // 2) * up
+    return up, blocks, vec_at, vec_at + 32, vec_at + 32 + 3 * TOK
+
+
+def pack_gradients(device, acc, sr_ref, hr_ref, out):
+    (acc_conv, acc_qkv, acc_proj, acc_fc1, acc_fc2, acc_ln, acc_rel) = acc
+    ch = acc_fc2.shape[0]
+    up, count, vec_at, rel_at, used = pack_rows(ch)
+    rest = ch - LANE
+    out[used:, :] = jnp.zeros((out.shape[0] - used, LANE), f32)
+    out[rel_at:used, :] = acc_rel[...]
+    blocks = [acc_conv[:ch, t * TAP : t * TAP + ch] for t in range(9)]
+    blocks += [acc_qkv[k, :ch, :] for k in range(3)]
+    blocks += [acc_proj[:ch, :]]
+    blocks += [acc_fc1[:ch, :ch], acc_fc1[:ch, ch:]]
+    blocks += [acc_fc2[:, :ch], acc_fc2[:, ch:]]
+    out[:vec_at, :] = jnp.zeros((vec_at, LANE), f32)
+    for k, block in enumerate(blocks):
+        out[k * up : k * up + ch, :] = block[:, :LANE]
+        at = (count + k // 2) * up
+        half = (k % 2) * TOK
+        out[at : at + ch, half : half + rest] = block[:, LANE:]
+    ln = [jnp.sum(jnp.transpose(acc_ln[k]), axis=0, keepdims=True) for k in range(5)]
+    vec = [
+        ln[0],
+        ln[1],
+        acc_qkv[0, ch : ch + 1, :],
+        acc_qkv[2, ch : ch + 1, :],
+        acc_proj[ch : ch + 1, :],
+        ln[2],
+        ln[3],
+        acc_fc1[ch : ch + 1, :ch],
+        acc_fc1[ch : ch + 1, ch:],
+        ln[4],
+        acc_conv[ch : ch + 1, 4 * TAP : 4 * TAP + ch],
+    ]
+    vec = jnp.concatenate(vec, axis=0)
+    diff = sr_ref[...] - hr_ref[...]
+    luma = (65.481 * diff[:, 0] + 128.553 * diff[:, 1] + 24.966 * diff[:, 2]) / 255.0
+    square = jnp.sum(luma * luma, axis=1, keepdims=True)
+    mse = jnp.sum(square, axis=2, keepdims=True) * (1.0 / (luma.shape[1] * luma.shape[2]))
+    psnr = jnp.sum(jnp.log(mse + 1e-06) * (-10.0 / 2.302585092994046), axis=0)
+    out[vec_at : vec_at + 32, :] = jnp.zeros((32, LANE), f32)
+    out[vec_at : vec_at + 11, :] = vec[:, :LANE]
+    lane = lax.broadcasted_iota(jnp.int32, (1, LANE), 1)
+    for k in range(3):
+        piece = psnr.astype(bf16).astype(f32)
+        out[vec_at + 11 + k : vec_at + 12 + k, :] = jnp.where(lane == device, piece, 0.0)
+        psnr = psnr - piece
+    out[vec_at + 16 : vec_at + 27, :rest] = vec[:, LANE:]
 
 
 def whole(shape):
@@ -369,8 +427,8 @@
         (3, up(ch), ch),
         (up(ch), ch),
         (up(ch), hid),
-        (up(hid), ch),
-        (4, ch, LANE),
+        (ch, hid),
+        (5, ch, LANE),
         (3 * TOK, LANE),
     ]
 
@@ -395,7 +453,7 @@
     wins = px // TOK
     tmp = [
         v((px, 9 * TAP), bf16),
-        v((up(ch), px), bf16), v((up(ch), px), bf16), v((up(ch), px), bf16), v((up(hid), px), bf16), v((up(ch), px), bf16),
+        v((up(ch), px), bf16), v((up(ch), px), bf16), v((up(ch), px), bf16), v((hid, px), bf16), v((up(ch), px), bf16),
         v((wins, ch, LANE), bf16),
         v((wins, 3 * TOK, LANE), f32),
         v((wins, 3 * TOK, LANE), bf16),
@@ -466,28 +524,150 @@
     ig_ref[0, head + mid :] = g2_ref[0, : own_rows - head - mid]
 
 
-def adam_kernel(scal, a_conv, a_qkv, a_proj, a_fc1, a_fc2, a_ln, a_rel, *refs):
+def split_bits(size):
+    return [b for b in range(size.bit_length() - 1)]
+
+
+def exchange_kernel(stages, g_ref, out_ref, work, given, low, send_sem, recv_sem):
+    rows = g_ref.shape[0]
+
+    def meet(stage):
+        axis, b = stage
+        me = lax.axis_index(axis)
+        step = 2**b
+        bit = (me // step) % 2
+        return {axis: me + (1 - 2 * bit) * step}, bit
+
+    barrier = pltpu.get_barrier_semaphore()
+    for stage in stages:
+        other, _ = meet(stage)
+        pl.semaphore_signal(barrier, inc=1, device_id=other, device_id_type=pl.DeviceIdType.MESH)
+    pl.semaphore_wait(barrier, len(stages))
+
+    def span(start, size):
+        return pl.ds(pl.multiple_of(start, 16), size)
+
+    start = 0
+    size = rows
+    starts = []
+    taken = 0
+    for s, stage in enumerate(stages):
+        other, bit = meet(stage)
+        size = size // 2
+        starts.append(start)
+        keep = start + bit * size
+        give = start + (1 - bit) * size
+        source = g_ref if s == 0 else work
+        copy = pltpu.make_async_remote_copy(
+            src_ref=source.at[span(give, size)],
+            dst_ref=given.at[pl.ds(taken, size)],
+            send_sem=send_sem.at[s],
+            recv_sem=recv_sem.at[s],
+            device_id=other,
+            device_id_type=pl.DeviceIdType.MESH,
+        )
+        copy.start()
+        copy.wait()
+        total = source[span(keep, size), :] + given[taken : taken + size, :]
+        if s < len(stages) - 1:
+            work[span(keep, size), :] = total
+        else:
+            low[span(keep, size), :] = total.astype(bf16)
+        taken += size
+        start = keep
+    for s in reversed(range(len(stages))):
+        other, bit = meet(stages[s])
+        n = len(stages) + s
+        copy = pltpu.make_async_remote_copy(
+            src_ref=low.at[span(start, size)],
+            dst_ref=low.at[span(start, size)],
+            send_sem=send_sem.at[n],
+            recv_sem=recv_sem.at[n],
+            device_id=other,
+            device_id_type=pl.DeviceIdType.MESH,
+        )
+        copy.start()
+        copy.wait()
+        start = starts[s]
+        size = size * 2
+    out_ref[...] = low[...]
+
+
+def reduce_all(packed, sizes):
+    stages = [(axis, b) for axis, size in sizes for b in split_bits(size)]
+    rows = packed.shape[0]
+    vmem = pl.BlockSpec(memory_space=pltpu.VMEM)
+    return pl.pallas_call(
+        functools.partial(exchange_kernel, stages),
+        in_specs=[vmem],
+        out_specs=vmem,
+        out_shape=jax.ShapeDtypeStruct(packed.shape, bf16),
+        scratch_shapes=[
+            pltpu.VMEM(packed.shape, f32),
+            pltpu.VMEM(packed.shape, f32),
+            pltpu.VMEM(packed.shape, bf16),
+            pltpu.SemaphoreType.DMA((2 * len(stages),)),
+            pltpu.SemaphoreType.DMA((2 * len(stages),)),
+        ],
+        compiler_params=pltpu.CompilerParams(
+            collective_id=0, has_side_effects=True, vmem_limit_bytes=40 * 1024 * 1024
+        ),
+        name="sum_gradients",
+    )(packed)
+
+
+def adam_kernel(scal, g_ref, *refs):
     weights, firsts, seconds = refs[0:7], refs[7:14], refs[14:21]
-    norm_ref, outs = refs[21], refs[22:43]
+    norm_ref, psnr_ref, outs = refs[21], refs[22], refs[23:44]
     ch = weights[2].shape[0]
-    hid = weights[5].shape[0]
-    g_vec = [
-        a_ln[0:1, :],
-        a_ln[1:2, :],
-        a_qkv[0, ch : ch + 1, :],
-        a_qkv[2, ch : ch + 1, :],
-        a_proj[ch : ch + 1, :],
-        a_ln[2:3, :],
-        a_ln[3:4, :],
-        a_fc1[ch : ch + 1, :ch],
-        a_fc1[ch : ch + 1, ch:],
-        a_fc2[hid : hid + 1, :],
-        a_conv[ch : ch + 1, 4 * TAP : 4 * TAP + ch],
-    ]
-    vec = jnp.concatenate(g_vec, axis=0)
-    qkv = jnp.concatenate([a_qkv[k, :ch, :] for k in range(3)], axis=1)
-    small = [vec, qkv, a_proj[:ch, :], a_rel[...], a_fc1[:ch, :], a_fc2[:hid, :]]
-    taps = [a_conv[:ch, t * TAP : t * TAP + ch] for t in range(9)]
+    up, count, vec_at, rel_at, used = pack_rows(ch)
+    rest = ch - LANE
+
+    def block(k):
+        left = g_ref[k * up : (k + 1) * up, :].astype(f32)
+        at = (count + k // 2) * up
+        right = g_ref[at : at + up, :].astype(f32)
+        if k % 2:
+            right = pltpu.roll(right, TOK, 1)
+        return jnp.concatenate([left, right[:, :rest]], axis=1)[:ch]
+
+    vec_rows = g_ref[vec_at : vec_at + 32, :].astype(f32)
+    vec = jnp.concatenate([vec_rows[:11], vec_rows[16:27, :rest]], axis=1)
+    psnr = vec_rows[11:12] + vec_rows[12:13] + vec_rows[13:14]
+    psnr_ref[...] = jnp.sum(psnr, axis=1, keepdims=True)
+
+    span = 2 * WIN
+    wide = span * span
+    at = lax.broadcasted_iota(jnp.int32, (TOK, wide), 0)
+    to = lax.broadcasted_iota(jnp.int32, (TOK, wide), 1)
+    place = ((at >> 3) + (WIN - 1)) * span + (at & 7) + (WIN - 1)
+    expand = (to == place).astype(f32).astype(bf16)
+    pairs = g_ref[rel_at:used, :]
+    rel_rows = []
+    for p in range(3):
+        for parity in range(2):
+            part = pairs[p * TOK : (p + 1) * TOK, :].astype(f32)
+            if parity:
+                part = pltpu.roll(part, TOK, 1)
+            spread = nn(part[:, :TOK].astype(bf16), expand)
+            total = jnp.zeros((WIN, wide), f32)
+            for row in range(WIN):
+                piece = spread[row * WIN : (row + 1) * WIN]
+                piece = pltpu.roll(piece, (wide - span * row) % wide, 1)
+                total = total + piece
+            line = total[0:1]
+            for c in range(1, WIN):
+                line = line + pltpu.roll(total, wide - c, 1)[c : c + 1]
+            rel_rows.append(line)
+    rel = jnp.concatenate(rel_rows, axis=0)
+    rel = jnp.concatenate(
+        [rel[:, k * span : k * span + span - 1] for k in range(span - 1)], axis=1
+    )
+    qkv = jnp.concatenate([block(9), block(10), block(11)], axis=1)
+    fc1 = jnp.concatenate([block(13), block(14)], axis=1)
+    fc2 = jnp.concatenate([block(15), block(16)], axis=1)
+    small = [vec, qkv, block(12), rel, fc1, fc2]
+    taps = [block(t) for t in range(9)]
     total = jnp.zeros((1, 1), f32)
     for g in small + taps:
         total = total + jnp.sum(jnp.sum(g * g, axis=0, keepdims=True), axis=1, keepdims=True)
@@ -547,6 +727,7 @@
         [
             jnp.stack([place, (place == heads - 1).astype(jnp.int32)]).astype(jnp.int32),
             valid_size.astype(jnp.int32),
+            ((lax.axis_index("dp") * heads + place) % LANE)[None].astype(jnp.int32),
         ]
     )
     halo = lax.ppermute(
@@ -559,7 +740,7 @@
     bias = jnp.dot(onehot, rel_table, precision=highest)
     bias = bias.reshape(TOK, TOK, 3, 2).transpose(2, 0, 3, 1).reshape(3, TOK, LANE)
 
-    wts = (vectors, qkv_weight, proj_weight, fc1_weight, fc2_weight, conv_weight, bias)
+    wts = (vectors, qkv_weight, proj_weight, fc1_weight, fc2_weight.T, conv_weight, bias)
     wts_specs = [whole(w.shape) for w in wts]
     acc_dims = acc_shapes(ch, hid)
     acc_types = [jax.ShapeDtypeStruct(s, f32) for s in acc_dims]
@@ -590,7 +771,10 @@
         compiler_params=params,
         name="inner_windows",
     )(info, images, cotangent, *wts)
-    c2, ig2, *acc = pl.pallas_call(
+    device_count = lax.axis_size("dp") * heads
+    unit = 16 * device_count
+    rows = -(-pack_rows(ch)[-1] // unit) * unit
+    c2, ig2, packed = pl.pallas_call(
         functools.partial(last_kernel, image_side, own_rows),
         grid=(count,),
         in_specs=[
@@ -601,42 +785,32 @@
             pl.BlockSpec((1, SHIFT + 1, image_side, ch), lambda n: (n, 0, 0, 0)),
             *wts_specs,
             *[whole(s) for s in acc_dims],
+            whole(sr_crops.shape),
+            whole(hr_crops.shape),
         ],
         out_specs=[
             pl.BlockSpec((1, WIN, image_side, ch), lambda n: (n, 0, 0, 0)),
             pl.BlockSpec((1, WIN, image_side, ch), lambda n: (n, 0, 0, 0)),
-            *[whole(s) for s in acc_dims],
+            whole((rows, LANE)),
         ],
         out_shape=[
             jax.ShapeDtypeStruct((count, WIN, image_side, ch), bf16),
             jax.ShapeDtypeStruct((count, WIN, image_side, ch), f32),
-            *acc_types,
-        ],
-        scratch_shapes=scratches(ch, hid, px, vectors.shape[0]),
+            jax.ShapeDtypeStruct((rows, LANE), f32),
+        ],
+        scratch_shapes=[pltpu.VMEM(s, f32) for s in acc_dims] + scratches(ch, hid, px, vectors.shape[0]),
         compiler_params=pltpu.CompilerParams(
             dimension_semantics=("arbitrary",), vmem_limit_bytes=60 * 1024 * 1024
         ),
         name="last_windows",
-    )(info, images, cotangent, x_halo, gy_halo, *wts, *acc)
+    )(info, images, cotangent, x_halo, gy_halo, *wts, *acc, sr_crops, hr_crops)
 
     c_halo = lax.ppermute(c2[:, WIN - SHIFT - 1 :], "head", to_upper)
     ig_halo = lax.ppermute(ig2[:, WIN - SHIFT :], "head", to_upper)
 
-    a_conv, a_qkv, a_proj, a_fc1, a_fc2, a_ln, a_rel = acc
-    rel = a_rel.reshape(3, TOK, 2, TOK).transpose(0, 2, 1, 3).reshape(6, TOK * TOK)
-    rel = jnp.dot(rel, onehot, precision=highest).T
-    ln = jnp.sum(a_ln, axis=2)
-
-    difference = sr_crops - hr_crops
-    luma = (65.481 * difference[:, 0] + 128.553 * difference[:, 1] + 24.966 * difference[:, 2]) / 255.0
-    mean_error = jnp.mean(luma * luma, axis=(1, 2))
-    local_psnr = jnp.sum(-10.0 * jnp.log10(mean_error + 1e-06))
-    a_conv, a_qkv, a_proj, a_fc1, a_fc2, ln, rel, psnr = lax.psum(
-        (a_conv, a_qkv, a_proj, a_fc1, a_fc2, ln, rel, local_psnr), ("dp", "head")
-    )
-    psnr_total = psnr_running + psnr
-
-    image_block = lambda rows: pl.BlockSpec((1, rows, image_side, ch), lambda n: (n, 0, 0, 0))
+    summed = reduce_all(packed, (("dp", lax.axis_size("dp")), ("head", heads)))
+
+    image_block = lambda size: pl.BlockSpec((1, size, image_side, ch), lambda n: (n, 0, 0, 0))
     output, image_grad = pl.pallas_call(
         functools.partial(conv_kernel, image_side, own_rows),
         grid=(count,),
@@ -664,19 +838,22 @@
 
     step_count = step[0].astype(f32)
     scal = jnp.stack([1.0 - beta_one**step_count, 1.0 - beta_two**step_count])
-    weights = (vectors, qkv_weight, proj_weight, rel_table, fc1_weight, fc2_weight, conv_weight)
-    firsts = (vectors_first, qkv_first, proj_first, rel_first, fc1_first, fc2_first, conv_first)
-    seconds = (vectors_second, qkv_second, proj_second, rel_second, fc1_second, fc2_second, conv_second)
+    weights = (vectors, qkv_weight, proj_weight, rel_table.T, fc1_weight, fc2_weight.T, conv_weight)
+    firsts = (vectors_first, qkv_first, proj_first, rel_first.T, fc1_first, fc2_first.T, conv_first)
+    seconds = (vectors_second, qkv_second, proj_second, rel_second.T, fc1_second, fc2_second.T, conv_second)
     vmem = pl.BlockSpec(memory_space=pltpu.VMEM)
-    grad_norm, *updated = pl.pallas_call(
+    grad_norm, psnr, *updated = pl.pallas_call(
         adam_kernel,
-        in_specs=[smem] + [vmem] * 28,
-        out_specs=[vmem] * 22,
-        out_shape=[jax.ShapeDtypeStruct((1, 1), f32)]
+        in_specs=[smem] + [vmem] * 22,
+        out_specs=[vmem] * 23,
+        out_shape=[jax.ShapeDtypeStruct((1, 1), f32)] * 2
         + [jax.ShapeDtypeStruct(w.shape, f32) for w in weights for _ in range(3)],
         compiler_params=pltpu.CompilerParams(vmem_limit_bytes=60 * 1024 * 1024),
         name="adam",
-    )(scal, a_conv, a_qkv, a_proj, a_fc1, a_fc2, ln, rel, *weights, *firsts, *seconds)
+    )(scal, summed, *weights, *firsts, *seconds)
+    for k in (9, 10, 11, 15, 16, 17):
+        updated[k] = updated[k].T
+    psnr_total = psnr_running + psnr.reshape(1)
     return (output, image_grad, grad_norm.reshape(1), psnr_total, *updated)
 
 

time: 331 us -> 260 us (0.79)
  blocking collectives: 66.7 us -> 0 us
  Pallas kernels: 132 us -> 198 us
  waiting for transfers between devices: 37.1 us -> 0.01 us
  local copies, waits for them, and re-layouts: 59 us -> 44.8 us
  between operations: 17.7 us -> 4.35 us
    psum x1 -> x0, blocking collectives: 66.7 us -> none  [on_device(): lax.psum((a_conv, a_qkv, a_proj, a_fc1, a_fc2, ln, rel, local_psnr), ('dp...]
    pallas_call x1 -> x2, Pallas kernels: 11 us -> 76.2 us  [the longest x1 65.5 us: reduce_all(): pl.pallas_call(functools.partial(exchange_kernel, stages), in_specs=[vmem...]
    psum x1 -> x0, waiting for transfers between devices: 37.1 us -> none  [on_device(): lax.psum((a_conv, a_qkv, a_proj, a_fc1, a_fc2, ln, rel, local_psnr), ('dp...]
    unnamed x46 -> x20, local copies, waits for them, and re-layouts: 47.6 us -> 29.6 us
  transfers between devices with their start and end apart: 4 -> 3, of which waited for: 1 -> 0; matrix products, arithmetic and copies ran while one was open for 15% -> 8% of each run, Pallas kernels for 25% -> 56%
where the time goes in v2:
time: 260 us; the launch traced here: 257 us
  Pallas kernels  198 us (76%)
  local copies, waits for them, and re-layouts  44.8 us (17%)
  starting transfers between devices  5.29 us (2%)
  between operations  4.35 us (2%)
    pallas_call x1, Pallas kernels, on_device(): pl.pallas_call(functools.partial(inner_kernel, image_side, own_rows), gri...  67.2 us
    pallas_call x1, Pallas kernels, reduce_all(): pl.pallas_call(functools.partial(exchange_kernel, stages), in_specs=[vmem...  65.5 us
    pallas_call x1, Pallas kernels, on_device(): pl.pallas_call(functools.partial(last_kernel, image_side, own_rows), grid...  38.4 us
    unnamed x20, local copies, waits for them, and re-layouts  29.6 us
    pallas_call x1, Pallas kernels, on_device(): pl.pallas_call(functools.partial(conv_kernel, image_side, own_rows), grid...  15.9 us
    pallas_call x1, Pallas kernels, on_device(): pl.pallas_call(adam_kernel, in_specs=[smem] + [vmem] * 22, out_specs=[vme...  10.7 us
  transfers between devices with their start and end apart: 3, of which 0 were waited for; matrix products, arithmetic and copies ran while one was open for 8% of the time, Pallas kernels for 56%

profile of v2, /device:TPU:0, one launch (start us, length us, event | category | flops | bytes accessed | tf_op | source)
XLA Modules:
  0.0 257.3 jit_solution(17016152544763193958)
XLA Ops:
  0.7 1.4 slice.18
  2.2 1.2 slice-done
  3.4 1.3 pad_maximum_fusion
  4.7 5.0 %collective-permute-start = (bf16[3,9,96,180]{2,3,1,0:T(8,128)(2,1)}, bf16[3,9,96,180]{2,3,1,0:T(8,128)(2,1)}, u32[]{:S(2)}, u32[]{:S(2)}) collective-permute-start(bf16[3,9,96,180]{2,3,1,0:T(8,128)(2,1)} %pad_maximum_fusion), channel_id=1, source_target_pairs={{1,0},{2,1},{3,2},{0,3},{5,4},{6,5},{7,6},{4,7},{9,8},{10,9},{11,1... | collective-permute-start | bytes 2799368 | tf_op jit(solution)/shard_map/ppermute | solution.py:733
  9.8 6.6 %copy.71.x_ref = bf16[3,24,96,180]{3,2,1,0:T(8,128)(2,1)} copy(bf16[3,24,96,180]{2,1,3,0:T(8,128)(2,1)} %param.29) | data formatting | bytes 4976640 | tf_op args[0]
  16.4 4.9 %copy.72.gy_ref = bf16[3,24,96,180]{3,2,1,0:T(8,128)(2,1)} copy(bf16[3,24,96,180]{2,1,3,0:T(8,128)(2,1)S(1)} %copy-done.2) | data formatting | bytes 4976640 | tf_op args[1]
  21.3 2.6 fusion
  25.6 67.2 %inner_windows.1 = (bf16[3,16,96,180]{3,2,1,0:T(8,128)(2,1)}, f32[3,16,96,180]{3,2,1,0:T(8,128)}, f32[192,2304]{1,0:T(8,128)}, f32[3,192,180]{2,1,0:T(8,128)}, f...) custom-call(s32[6]{0:T(128)} %pad_add_fusion.info, ...), custom_call_target="tpu_custom_call" | custom-call | tf_op jit(solution)/shard_map/inner_windows/pallas_call | solution.py:751
  92.9 1.1 slice.24
  94.0 1.1 copy.82.xh_ref
  95.1 1.2 slice.25
  96.2 1.2 copy.83.gyh_ref
  97.4 38.4 %last_windows.1 = (bf16[3,8,96,180]{3,2,1,0:T(8,128)(2,1)}, f32[3,8,96,180]{3,2,1,0:T(8,128)}, f32[5120,128]{1,0:T(8,128)}) custom-call(s32[6]{0:T(128)} %pad_add_fusion.info, bf16[3,24,96,180]{3,2,1,0:T(8,128)(2,1)} %copy.71.x_ref, bf16[3,24,96,180]{3,2,1,0:T(8,128)(2,1)} %copy.72.gy_ref, bf16[3,4,96,180]{3,2,1,0:T(8,128)(2,1)} %copy.82.xh_ref, ...), custom_call_target="tpu_custom_call" | custom-call | tf_op jit(solution)/shard_map/last_windows/pallas_call | solution.py:777
  135.8 1.4 slice.23
  137.2 1.7 copy.74
  139.1 1.3 slice.22
  140.4 1.3 copy.73
  143.7 65.5 %sum_gradients.1.g_ref = bf16[5120,128]{1,0:T(8,128)(2,1)S(1)} custom-call(f32[5120,128]{1,0:T(8,128)S(1)} %copy-done.1), custom_call_target="tpu_custom_call" | custom-call | tf_op jit(solution)/shard_map/sum_gradients/pallas_call | solution.py:600
  210.2 10.7 %adam.1 = (f32[1,1]{1,0:T(1,128)}, f32[1,1]{1,0:T(1,128)}, f32[11,180]{1,0:T(8,128)}, f32[11,180]{1,0:T(8,128)}, f32[11,180]{1,0:T(8,128)}, /*index=5*/f32[180,5...) custom-call(f32[2]{0:T(128)} %pad_maximum_fusion.1.scal, ...), custom_call_target="tpu_custom_call" | custom-call | tf_op jit(solution)/shard_map/adam/pallas_call | solution.py:845
  221.5 1.2 copy.75.hc_ref
  222.7 2.5 copy.76.hg_ref
  225.2 15.9 %conv_output.1 = (bf16[3,24,96,180]{3,2,1,0:T(8,128)(2,1)}, f32[3,24,96,180]{3,2,1,0:T(8,128)}) custom-call(s32[6]{0:T(128)} %pad_add_fusion.info, bf16[3,5,96,180]{3,2,1,0:T(8,128)(2,1)} %copy.75.hc_ref, bf16[3,16,96,180]{3,2,1,0:T(8,128)(2,1)} %get-tuple-element.70.c1_ref, bf16[3,8,96,180]{3,2,1,0:T(8,128)(2,1)} %get-tuple-element.69.c2_ref, ...), custom_call_target="tpu_custom_call" | custom-call | tf_op jit(solution)/shard_map/conv_output/pallas_call | solution.py:814
  241.2 6.3 %copy.78 = bf16[3,24,96,180]{2,1,3,0:T(8,128)(2,1)} copy(bf16[3,24,96,180]{3,2,1,0:T(8,128)(2,1)} %get-tuple-element.124) | data formatting | bytes 4976640
  247.5 8.2 %copy.79 = f32[3,24,96,180]{2,1,3,0:T(8,128)} copy(f32[3,24,96,180]{3,2,1,0:T(8,128)} %get-tuple-element.125) | data formatting | bytes 9953280
  (25 shorter events, 3.8 us)
Async XLA Ops:
  2.1 1.2 slice-start
  4.7 88.2 %collective-permute-start = (bf16[3,9,96,180]{2,3,1,0:T(8,128)(2,1)}, bf16[3,9,96,180]{2,3,1,0:T(8,128)(2,1)}, u32[]{:S(2)}, u32[]{:S(2)}) collective-permute-start(bf16[3,9,96,180]{2,3,1,0:T(8,128)(2,1)} %pad_maximum_fusion), channel_id=1, source_target_pairs={{1,0},{2,1},{3,2},{0,3},{5,4},{6,5},{7,6},{4,7},{9,8},{10,9},{11,1... | collective-permute-start | bytes 2799368 | tf_op jit(solution)/shard_map/ppermute | solution.py:733
  9.8 6.6 %copy-start.2 = (bf16[3,24,96,180]{2,1,3,0:T(8,128)(2,1)S(1)}, bf16[3,24,96,180]{2,1,3,0:T(8,128)(2,1)}, u32[]{:S(2)}) copy-start(bf16[3,24,96,180]{2,1,3,0:T(8,128)(2,1)} %param.30) | copy-start | bytes 7464964
  16.4 5.0 %copy-start.3 = (f32[225,6]{0,1:T(8,128)S(1)}, f32[225,6]{0,1:T(8,128)}, u32[]{:S(2)}) copy-start(f32[225,6]{0,1:T(8,128)} %param.41) | copy-start | bytes 16204
  16.4 5.0 %copy-start.5 = (s32[4096]{0:T(1024)S(1)}, s32[4096]{0:T(1024)}, u32[]{:S(2)}) copy-start(s32[4096]{0:T(1024)} %constant.38.clone) | copy-start | bytes 49156
  21.3 3.6 %copy-start.4 = (s32[3]{0:T(128)S(1)}, s32[3]{0:T(128)}, u32[]{:S(2)}) copy-start(s32[3]{0:T(128)} %param.31) | copy-start | bytes 40
  138.9 4.8 %copy-start.1 = (f32[5120,128]{1,0:T(8,128)S(1)}, f32[5120,128]{1,0:T(8,128)}, u32[]{:S(2)}) copy-start(f32[5120,128]{1,0:T(8,128)} %get-tuple-element.75.g_ref) | copy-start | bytes 7864324
  138.9 83.9 %collective-permute-start.2 = (f32[3,4,96,180]{2,1,3,0:T(4,128)}, f32[3,4,96,180]{2,1,3,0:T(4,128)}, u32[]{:S(2)}, u32[]{:S(2)}) collective-permute-start(f32[3,4,96,180]{2,1,3,0:T(4,128)} %copy.74), channel_id=1, source_target_pairs={{0,1},{1,2},{2,3},{3,0},{4,5},{5,6},{6,7},{7,4},{8,9},{9,10},{10,1... | collective-permute-start | bytes 2488328 | tf_op jit(solution)/shard_map/ppermute | solution.py:809
  141.7 79.8 %collective-permute-start.1 = (bf16[3,5,96,180]{2,3,1,0:T(8,128)(2,1)}, bf16[3,5,96,180]{2,3,1,0:T(8,128)(2,1)S(1)}, u32[]{:S(2)}, u32[]{:S(2)}) collective-permute-start(bf16[3,5,96,180]{2,3,1,0:T(8,128)(2,1)} %copy.73), channel_id=1, source_target_pairs={{0,1},{1,2},{2,3},{3,0},{4,5},{5,6},{6,7},{7,4},{8,9},{9,10},{10,1... | collective-permute-start | bytes 1555208 | tf_op jit(solution)/shard_map/ppermute | solution.py:808
  209.2 1.1 copy-start

commit v3 on v2

v3 whole, which is shorter than its diff:
```python
import functools

import jax
import jax.numpy as jnp
import numpy as np
from jax import lax
from jax.experimental import pallas as pl
from jax.experimental.pallas import tpu as pltpu
from jax.sharding import PartitionSpec as P

WIN = 8
TOK = WIN * WIN
SHIFT = WIN // 2
LANE = 128
TAP = 256
HPAD = 32
HEADS = 6
CPAD = HEADS * HPAD

eps_norm = 1e-05
neg_mask = -100.0
max_norm = 1.0
learn_rate = 0.03
vector_rate = 0.2
beta_one = 0.9
beta_two = 0.999
adam_eps = 1e-08
decay_rate = 0.01
highest = lax.Precision.HIGHEST
f32 = jnp.float32
bf16 = jnp.bfloat16


def nn(a, b):
    return lax.dot_general(a, b, (((1,), (0,)), ((), ())), preferred_element_type=f32)


def nt(a, b):
    return lax.dot_general(a, b, (((1,), (1,)), ((), ())), preferred_element_type=f32)


def pad_heads(rows, heads):
    dim = rows.shape[0] // heads
    gap = jnp.zeros((HPAD - dim, rows.shape[1]), rows.dtype)
    parts = []
    for h in range(heads):
        parts += [rows[h * dim : (h + 1) * dim], gap]
    return jnp.concatenate(parts, axis=0)


def drop_rows(rows, heads, dim):
    return jnp.concatenate([rows[h * HPAD : h * HPAD + dim] for h in range(heads)], axis=0)


def drop_lanes(rows, heads, dim):
    return jnp.concatenate([rows[:, h * HPAD : h * HPAD + dim] for h in range(heads)], axis=1)


def to_tokens(rows):
    side = rows.shape[1]
    return jnp.concatenate(
        [rows[:, w * WIN : (w + 1) * WIN, :].reshape(TOK, rows.shape[2]) for w in range(side // WIN)],
        axis=0,
    )


def from_tokens(tokens):
    count = tokens.shape[0] // TOK
    return jnp.concatenate(
        [tokens[w * TOK : (w + 1) * TOK].reshape(WIN, WIN, tokens.shape[1]) for w in range(count)],
        axis=1,
    )


def roll_cols(rows, by):
    side = rows.shape[1]
    by = by % side
    return jnp.concatenate([rows[:, by:, :], rows[:, :by, :]], axis=1)


def block_step(x_rows, gy_rows, first_step, edge, base_row, valid, image_side, wts, prep, acc, tmp, c_out):
    (vec_ref, qkv_ref, proj_ref, fc1_ref, fc2_ref, conv_ref, bias_ref) = wts
    (vecT, wqkvT, wpT, w1T, w2T, wq, wk, wv, wp, w1, w2, wcT, colmask, rowmask, b1T, wide_vec, head_vec) = prep
    (acc_conv, acc_qkv, acc_proj, acc_fc1, acc_fc2, acc_ln, acc_rel) = acc
    (g9, a_aug, o_aug, m_aug, g_aug, c_aug, qeo_s, p_s, pb_s, kv_s, first_s, do_s, dq_s, dkv_s, u2_s, xT_s, slope_s, vt_s, qt_s, kt_s, inv_s, db_s, dh_s, ds_s) = tmp
    ch = x_rows.shape[2]
    dim = ch // HEADS
    hid = fc1_ref.shape[1]
    px = x_rows.shape[1] * WIN
    pairs = px // LANE
    ones_row = dim

    @pl.when(first_step)
    def _():
        vecT[...] = jnp.transpose(vec_ref[...])
        for k in range(10):
            wide_vec[k] = jnp.broadcast_to(vecT[:, k : k + 1], (ch, LANE))
        for k in range(2):
            head_vec[k] = pad_heads(wide_vec[2 + k], HEADS)
        b1T[:ch, :] = wide_vec[7]
        b1T[ch:, :] = wide_vec[8]
        for k, dst in enumerate((wq, wk, wv)):
            part = pad_heads(jnp.transpose(qkv_ref[:, k * ch : (k + 1) * ch]), HEADS)
            wqkvT[k * CPAD : (k + 1) * CPAD, :] = part.astype(bf16)
            dst[...] = jnp.transpose(part).astype(bf16)
        padded = pad_heads(proj_ref[...], HEADS)
        wp[...] = padded.astype(bf16)
        wpT[...] = jnp.transpose(padded).astype(bf16)
        w1[...] = fc1_ref[...].astype(bf16)
        w1T[...] = jnp.transpose(fc1_ref[...]).astype(bf16)
        w2T[...] = fc2_ref[...].astype(bf16)
        w2[...] = jnp.transpose(fc2_ref[...]).astype(bf16)
        wcT[...] = jnp.zeros_like(wcT)
        g9[...] = jnp.zeros_like(g9)
        for tap in range(9):
            wcT[tap * CPAD : tap * CPAD + ch, :] = jnp.transpose(conv_ref[tap // 3, tap % 3]).astype(bf16)
        key = lax.broadcasted_iota(jnp.int32, (TOK, LANE), 0)
        query = lax.broadcasted_iota(jnp.int32, (TOK, LANE), 1) & (TOK - 1)
        one = lambda m: m.astype(f32)
        colmask[...] = one(((key & 7) < SHIFT) != ((query & 7) < SHIFT))
        rowmask[...] = one(((key >> 3) < SHIFT) != ((query >> 3) < SHIFT))
        for ref in (a_aug, m_aug, c_aug):
            pad = ref.shape[0] - ch
            ref[ch:, :] = (lax.broadcasted_iota(jnp.int32, (pad, px), 0) == 0).astype(f32).astype(bf16)

    def column(k):
        return wide_vec[k]

    def stats(v):
        mean = jnp.sum(v, axis=0, keepdims=True) * (1.0 / ch)
        cen = v - mean
        var = jnp.sum(cen * cen, axis=0, keepdims=True) * (1.0 / ch)
        inv = lax.rsqrt(var + eps_norm)
        return cen * inv, inv

    def ln_back(grad, u, inv, gain):
        t = grad * gain
        mean_t = jnp.sum(t, axis=0, keepdims=True) * (1.0 / ch)
        mean_tu = jnp.sum(t * u, axis=0, keepdims=True) * (1.0 / ch)
        return inv * (t - mean_t - u * mean_tu)

    chunks = [slice(k * LANE, (k + 1) * LANE) for k in range(px // LANE)]
    third = hid // 3
    bands = [slice(k * third, (k + 1) * third) for k in range(3)]

    keep = jnp.where(edge, 0.0, 1.0).astype(f32)
    col = lax.broadcasted_iota(jnp.int32, (1, image_side, ch), 1)
    moved = {}

    def build_tap(tap):
        i, j = tap % 3, tap // 3
        if i == 0:
            shifted = roll_cols(gy_rows, SHIFT + 1 - j)
            if j == 0:
                shifted = jnp.where(col == image_side - SHIFT - 1, 0.0, shifted)
            if j == 2:
                shifted = jnp.where(col == image_side - SHIFT, 0.0, shifted)
            moved[j] = shifted
        rows = [moved[j][r + 2 - i : r + 3 - i] for r in range(WIN)]
        if i == 0:
            rows[SHIFT - 1] = rows[SHIFT - 1] * keep
        if i == 2:
            rows[SHIFT] = rows[SHIFT] * keep
        at = (3 * i + j) * CPAD
        g9[:, at : at + ch] = to_tokens(jnp.concatenate(rows, axis=0)).astype(bf16)

    x_tok = to_tokens(roll_cols(x_rows, SHIFT))
    for at in chunks:
        xT = jnp.transpose(x_tok[at])
        xT_s[:, at] = xT
        u1, _ = stats(xT)
        a_aug[:ch, at] = (u1 * column(0) + column(1)).astype(bf16)
    scale = dim ** (-0.5)
    qkv_all = nn(wqkvT[...], a_aug[:ch, :])
    for at in chunks:
        qt_s[:, at] = ((qkv_all[:CPAD, at] + head_vec[0]) * scale).astype(bf16)
        kT = qkv_all[CPAD : 2 * CPAD, at].astype(bf16)
        vT = (qkv_all[2 * CPAD :, at] + head_vec[1]).astype(bf16)
        kt_s[:, at] = kT
        vt_s[:, at] = vT
        kv_s[0, at, :] = jnp.transpose(kT.astype(f32)).astype(bf16)
        kv_s[1, at, :] = jnp.transpose(vT.astype(f32)).astype(bf16)

    def low_lanes(rows):
        return lax.broadcasted_iota(jnp.int32, (rows, LANE), 1) < TOK

    def swap(slab):
        return pltpu.roll(slab, TOK, 1)

    def only_low(v):
        return jnp.where(low_lanes(v.shape[0]), v, jnp.zeros_like(v))

    def only_high(v):
        return jnp.where(low_lanes(v.shape[0]), jnp.zeros_like(v), v)

    def head_rows(v, h):
        return v[h * HPAD : (h + 1) * HPAD]

    def dup(slab):
        slab = slab.astype(f32)
        other = swap(slab)
        out = []
        for low, high in ((slab, other), (other, slab)):
            rows = [
                only_high(head_rows(high, h)) if h % 2 else only_low(head_rows(low, h)) for h in range(HEADS)
            ]
            out.append(jnp.concatenate(rows, axis=0).astype(bf16))
        return out

    def spread(slab):
        slab = slab.astype(f32)
        other = swap(slab)
        two = 2 * HPAD
        gap = jnp.zeros((two, TOK), f32)
        wide = jnp.zeros((two, LANE), f32)
        out = []
        for low, high in ((slab, other), (other, slab)):
            rows = [
                jnp.concatenate([only_low(low[:two]), gap], axis=1),
                jnp.concatenate([only_high(high[two : 2 * two]), gap], axis=1),
                jnp.concatenate([wide, low[2 * two :, :TOK]], axis=1),
            ]
            out.append(jnp.concatenate(rows, axis=0).astype(bf16))
        return out

    def merge(one, two):
        rows = []
        for h in range(HEADS):
            first, second = head_rows(one, h), head_rows(two, h)
            if h % 2:
                rows.append(jnp.where(low_lanes(HPAD), swap(first), second))
            else:
                rows.append(jnp.where(low_lanes(HPAD), first, swap(second)))
        return jnp.concatenate(rows, axis=0)

    def by_pair(rows):
        front, back = rows[:, :LANE], rows[:, LANE:]
        zero_back = jnp.zeros_like(back)
        return jnp.concatenate(
            [
                jnp.concatenate([only_low(front), zero_back], axis=1),
                jnp.concatenate([only_high(front), zero_back], axis=1),
                jnp.concatenate([jnp.zeros_like(front), back], axis=1),
            ],
            axis=0,
        )

    def pick_pair(stacked):
        front = jnp.where(low_lanes(TOK), stacked[:TOK, :LANE], stacked[TOK : 2 * TOK, :LANE])
        return jnp.concatenate([front, stacked[2 * TOK :, LANE:]], axis=1)

    key = lax.broadcasted_iota(jnp.int32, (TOK, LANE), 0)
    key_row = base_row + (key >> 3)
    key_row = jnp.where(key_row >= image_side, key_row - image_side, key_row)
    out_row = key_row >= valid
    edge_f = jnp.where(edge, neg_mask, 0.0).astype(f32)

    def scores_of(pp):
        q_pair = dup(qt_s[:, chunks[pp]])
        raw = []
        for half in range(2):
            w = 2 * pp + half
            qeo_s[w] = q_pair[half]
            raw.append(nn(by_pair(kv_s[0, w * TOK : (w + 1) * TOK, :]), q_pair[half]))
        return raw

    def soften(pp, raw):
        for half in range(2):
            w = 2 * pp + half
            key_col = (key & 7) + (w * WIN + SHIFT)
            apart = rowmask[...] * edge_f
            if w == 2 * pairs - 1:
                key_col = jnp.where(key_col >= image_side, key_col - image_side, key_col)
                apart = jnp.where(colmask[...] > 0.5, neg_mask, apart)
            extra = apart + jnp.where(out_row | (key_col >= valid), neg_mask, 0.0)
            s = raw[half].reshape(3, TOK, LANE) + bias_ref[...] + extra[None]
            top = jnp.max(s, axis=1, keepdims=True)
            e = jnp.exp(s - top)
            p = e / jnp.sum(e, axis=1, keepdims=True)
            p = p.reshape(3 * TOK, LANE)
            p_s[w] = p
            pb_s[w] = p.astype(bf16)

    def mix(pp):
        v_pair = spread(vt_s[:, chunks[pp]])
        return [nn(v_pair[half], pb_s[2 * pp + half]) for half in range(2)]

    def place(pp, mixed):
        o_aug[:, chunks[pp]] = merge(*mixed).astype(bf16)

    raws, mixes = {}, {}
    for t in range(pairs + 3):
        if 0 <= t - 2 < pairs:
            mixes[t - 2] = mix(t - 2)
        if t < pairs:
            raws[t] = scores_of(t)
        if 0 <= t - 1 < pairs:
            soften(t - 1, raws.pop(t - 1))
        if 0 <= t - 3 < pairs:
            place(t - 3, mixes.pop(t - 3))
        if t < 9:
            build_tap(t)
    o_aug[ones_row : ones_row + 1, :] = jnp.ones((1, px), bf16)

    attn = nn(wpT[...], o_aug[...])
    part = px // 3
    conv_back = [nn(g9[:part, :], wcT[...])]
    for at in chunks:
        first = xT_s[:, at] + (attn[:, at] + column(4))
        first_s[:, at] = first
        u2, inv2 = stats(first)
        u2_s[:, at] = u2
        inv_s[0:1, at] = inv2
        m_aug[:ch, at] = (u2 * column(5) + column(6)).astype(bf16)
    hidden_all = nn(w1T[...], m_aug[:ch, :])
    conv_back.append(nn(g9[part : 2 * part, :], wcT[...]))
    for at in chunks:
        for band in bands:
            hidden = hidden_all[band, at] + b1T[band, :]
            cdf = 0.5 * (1.0 + lax.erf(hidden * 0.7071067811865476))
            g_aug[band, at] = (hidden * cdf).astype(bf16)
            slope_s[band, at] = cdf + hidden * jnp.exp(-0.5 * hidden * hidden) * 0.3989422804014327
    branch = nn(w2T[...], g_aug[...])
    conv_back.append(nn(g9[2 * part :, :], wcT[...]))
    c_rows = []
    for at in chunks:
        cT = (first_s[:, at] + (branch[:, at] + column(9))).astype(bf16)
        c_aug[:ch, at] = cT
        c_rows.append(jnp.transpose(cT.astype(f32)))
    c_out[0] = roll_cols(from_tokens(jnp.concatenate(c_rows, axis=0)), -SHIFT).astype(bf16)

    dsecond = jnp.concatenate(conv_back, axis=0)
    for at in chunks:
        ds_chunk = jnp.transpose(dsecond[at])
        ds_s[:, at] = ds_chunk
        dbT = ds_chunk.astype(bf16)
        db_s[:, at] = dbT
        acc_ln[4] += dbT.astype(f32)
    dg = nn(w2[...], db_s[...])
    acc_fc2[...] += nt(g_aug[...], db_s[...])
    for at in chunks:
        for band in bands:
            dh_s[band, at] = (dg[band, at] * slope_s[band, at]).astype(bf16)
    dm_all = nn(w1[...], dh_s[...])
    acc_fc1[...] += nt(dh_s[...], m_aug[...])
    for at in chunks:
        u2 = u2_s[:, at]
        dm = dm_all[:, at]
        acc_ln[2] += dm * u2
        acc_ln[3] += dm
        dfirst = ds_s[:, at] + ln_back(dm, u2, inv_s[0:1, at], column(5))
        first_s[:, at] = dfirst
        db_s[:, at] = dfirst.astype(bf16)
    do_all = nn(wp[...], db_s[...])
    acc_proj[...] += nt(o_aug[...], db_s[...])
    for at in chunks:
        do_s[:, at] = do_all[:, at].astype(bf16)

    rel_sum = jnp.zeros((3 * TOK, LANE), f32)

    def probs_grad(pp):
        do_pair = dup(do_s[:, chunks[pp]])
        dps, dvs = [], []
        for half in range(2):
            w = 2 * pp + half
            dps.append(nn(by_pair(kv_s[1, w * TOK : (w + 1) * TOK, :]), do_pair[half]))
            dvs.append(nt(pb_s[w], do_pair[half]))
        return dps, dvs

    def scores_grad(pp, dps, dvs, rel_sum):
        out = []
        for half in range(2):
            w = 2 * pp + half
            p = p_s[w].reshape(3, TOK, LANE)
            dp = dps[half].reshape(3, TOK, LANE)
            ds = p * (dp - jnp.sum(p * dp, axis=1, keepdims=True))
            ds = ds.reshape(3 * TOK, LANE).astype(bf16)
            rel_sum = rel_sum + ds.astype(f32)
            out.append(ds)
            dkv_s[1, w * TOK : (w + 1) * TOK, :] = pick_pair(dvs[half]).astype(bf16)
        return out, rel_sum

    def inner_grads(pp, ds):
        k_pair = spread(kt_s[:, chunks[pp]])
        dks = [nt(ds[half], qeo_s[2 * pp + half]) for half in range(2)]
        dqs = [nn(k_pair[half], ds[half]) for half in range(2)]
        return dks, dqs

    def place_grads(pp, dks, dqs):
        for half in range(2):
            w = 2 * pp + half
            dkv_s[0, w * TOK : (w + 1) * TOK, :] = pick_pair(dks[half]).astype(bf16)
        dq_s[:, chunks[pp]] = merge(*dqs).astype(bf16)

    first_part, second_part, third_part = {}, {}, {}
    for t in range(pairs + 3):
        if 0 <= t - 2 < pairs:
            third_part[t - 2] = inner_grads(t - 2, second_part.pop(t - 2))
        if t < pairs:
            first_part[t] = probs_grad(t)
        if 0 <= t - 1 < pairs:
            second_part[t - 1], rel_sum = scores_grad(t - 1, *first_part.pop(t - 1), rel_sum)
        if 0 <= t - 3 < pairs:
            place_grads(t - 3, *third_part.pop(t - 3))
        at = slice(t * TAP, min((t + 1) * TAP, 9 * CPAD))
        if at.start < at.stop:
            acc_conv[:, at] += nn(c_aug[...], g9[:, at])
    acc_rel[...] += rel_sum

    dqT = dq_s[...]
    da_q = nn(wq[...], dqT)
    da_kv = nt(wk[...], dkv_s[0]) + nt(wv[...], dkv_s[1])
    acc_qkv[0] += nt(a_aug[...], dqT) * scale
    acc_qkv[1] += nn(a_aug[...], dkv_s[0])
    acc_qkv[2] += nn(a_aug[...], dkv_s[1])
    ig_rows = []
    for at in chunks:
        da = da_q[:, at] * scale + da_kv[:, at]
        u1, inv1 = stats(xT_s[:, at])
        acc_ln[0] += da * u1
        acc_ln[1] += da
        ig_rows.append(jnp.transpose(first_s[:, at] + ln_back(da, u1, inv1, column(0))))
    return roll_cols(from_tokens(jnp.concatenate(ig_rows, axis=0)), -SHIFT) + gy_rows[1 : 1 + WIN]


N_ACC = 7
N_PREP = 17
N_WTS = 7


def natural_rows(ref, start, count):
    return jnp.concatenate([jnp.transpose(ref[start + r])[None] for r in range(count)], axis=0)


def inner_kernel(image_side, own_rows, info, x_ref, gy_ref, *refs):
    wts, refs = refs[:N_WTS], refs[N_WTS:]
    c_out, ig_out, refs = refs[0], refs[1], refs[2:]
    acc, refs = refs[:N_ACC], refs[N_ACC:]
    x_s, gy_s, ig_s, refs = *refs[:3], refs[3:]
    prep, tmp = refs[:N_PREP], refs[N_PREP:]
    image, row_block = pl.program_id(0), pl.program_id(1)
    first_step = (image == 0) & (row_block == 0)

    @pl.when(first_step)
    def _():
        for ref in acc:
            ref[...] = jnp.zeros_like(ref)
        ig_s[...] = jnp.zeros_like(ig_s)

    @pl.when(row_block == 0)
    def _():
        x_s[...] = jnp.swapaxes(x_ref[0].astype(f32), 0, 1)
        gy_s[...] = jnp.swapaxes(gy_ref[0].astype(f32), 0, 1)

    start = row_block * WIN + SHIFT
    x_rows = natural_rows(x_s, start, WIN)
    gy_rows = natural_rows(gy_s, start - 1, WIN + 2)
    base_row = info[0] * own_rows + start
    ig = block_step(
        x_rows, gy_rows, first_step, False, base_row, info[2 + image], image_side, wts, prep, acc, tmp, c_out
    )
    for r in range(WIN):
        ig_s[start + r] = jnp.transpose(ig[r])

    @pl.when(row_block == pl.num_programs(1) - 1)
    def _():
        ig_out[0] = jnp.swapaxes(ig_s[...], 0, 1)


def last_kernel(image_side, own_rows, info, x_ref, gy_ref, halo_ref, ig_ref, *refs):
    wts, refs = refs[:N_WTS], refs[N_WTS:]
    acc_in, refs = refs[:N_ACC], refs[N_ACC:]
    sr_ref, hr_ref, c_out, ig_out, ig_halo, pack_out, refs = *refs[:6], refs[6:]
    acc, refs = refs[:N_ACC], refs[N_ACC:]
    prep, tmp = refs[:N_PREP], refs[N_PREP:]
    image = pl.program_id(0)
    first_step = image == 0

    @pl.when(first_step)
    def _():
        for ref, given in zip(acc, acc_in):
            ref[...] = given[...]

    def rows_of(ref):
        return jnp.swapaxes(ref[0].astype(f32), 0, 1)

    x_own, gy_own, halo = rows_of(x_ref), rows_of(gy_ref), rows_of(halo_ref)
    natural = lambda rows: jnp.concatenate([jnp.transpose(r)[None] for r in rows], axis=0)
    x_rows = natural([x_own[SHIFT + r] for r in range(SHIFT)] + [halo[r] for r in range(SHIFT)])
    gy_rows = natural(
        [gy_own[SHIFT - 1 + r] for r in range(SHIFT + 1)] + [halo[SHIFT + r] for r in range(SHIFT + 1)]
    )
    base_row = info[0] * own_rows + own_rows - SHIFT
    ig = block_step(
        x_rows, gy_rows, first_step, info[1] == 1, base_row, info[2 + image], image_side, wts, prep, acc, tmp, c_out
    )
    kept = rows_of(ig_ref)
    new = [kept[r] for r in range(SHIFT)] + [jnp.transpose(ig[r]) for r in range(SHIFT)]
    ig_out[0] = jnp.swapaxes(jnp.stack(new), 0, 1)
    for r in range(SHIFT):
        ig_halo[0, r] = jnp.transpose(ig[SHIFT + r]).astype(bf16)

    @pl.when(image == pl.num_programs(0) - 1)
    def _():
        pack_gradients(info[2 + pl.num_programs(0)], acc, sr_ref, hr_ref, pack_out)


def pack_rows(ch):
    up = -(-ch // 8) * 8
    blocks = 17
    vec_at = (blocks + (blocks + 1) // 2) * up
    return up, blocks, vec_at, vec_at + 32, vec_at + 32 + 3 * TOK


def pack_gradients(device, acc, sr_ref, hr_ref, out):
    (acc_conv, acc_qkv, acc_proj, acc_fc1, acc_fc2, acc_ln, acc_rel) = acc
    ch = acc_fc2.shape[1]
    dim = ch // HEADS
    up, count, vec_at, rel_at, used = pack_rows(ch)
    rest = ch - LANE
    out[used:, :] = jnp.zeros((out.shape[0] - used, LANE), f32)
    out[rel_at:used, :] = acc_rel[...]
    blocks = [acc_conv[:ch, t * CPAD : t * CPAD + ch] for t in range(9)]
    qkv = [drop_lanes(acc_qkv[k], HEADS, dim) for k in range(3)]
    blocks += [qkv[k][:ch] for k in range(3)]
    blocks += [drop_rows(acc_proj[...], HEADS, dim)]
    fc1 = jnp.transpose(acc_fc1[...])
    fc2 = jnp.transpose(acc_fc2[...])
    blocks += [fc1[:ch, :ch], fc1[:ch, ch:]]
    blocks += [fc2[:, :ch], fc2[:, ch:]]
    out[:vec_at, :] = jnp.zeros((vec_at, LANE), f32)
    for k, block in enumerate(blocks):
        out[k * up : k * up + ch, :] = block[:, :LANE]
        at = (count + k // 2) * up
        half = (k % 2) * TOK
        out[at : at + ch, half : half + rest] = block[:, LANE:]
    ln = [jnp.sum(jnp.transpose(acc_ln[k]), axis=0, keepdims=True) for k in range(5)]
    vec = [
        ln[0],
        ln[1],
        qkv[0][ch : ch + 1, :],
        qkv[2][ch : ch + 1, :],
        acc_proj[dim : dim + 1, :],
        ln[2],
        ln[3],
        fc1[ch : ch + 1, :ch],
        fc1[ch : ch + 1, ch:],
        ln[4],
        acc_conv[ch : ch + 1, 4 * CPAD : 4 * CPAD + ch],
    ]
    vec = jnp.concatenate(vec, axis=0)
    diff = sr_ref[...] - hr_ref[...]
    luma = (65.481 * diff[:, 0] + 128.553 * diff[:, 1] + 24.966 * diff[:, 2]) / 255.0
    square = jnp.sum(luma * luma, axis=1, keepdims=True)
    mse = jnp.sum(square, axis=2, keepdims=True) * (1.0 / (luma.shape[1] * luma.shape[2]))
    psnr = jnp.sum(jnp.log(mse + 1e-06) * (-10.0 / 2.302585092994046), axis=0)
    out[vec_at : vec_at + 32, :] = jnp.zeros((32, LANE), f32)
    out[vec_at : vec_at + 11, :] = vec[:, :LANE]
    lane = lax.broadcasted_iota(jnp.int32, (1, LANE), 1)
    for k in range(3):
        piece = psnr.astype(bf16).astype(f32)
        out[vec_at + 11 + k : vec_at + 12 + k, :] = jnp.where(lane == device, piece, 0.0)
        psnr = psnr - piece
    out[vec_at + 16 : vec_at + 27, :rest] = vec[:, LANE:]


def whole(shape):
    return pl.BlockSpec(shape, lambda *_: (0,) * len(shape))


def acc_shapes(ch, hid):
    return [
        (CPAD, 9 * CPAD),
        (3, CPAD, CPAD),
        (CPAD, ch),
        (hid, CPAD),
        (hid, ch),
        (5, ch, LANE),
        (3 * TOK, LANE),
    ]


def scratches(ch, hid, px, vec_rows):
    v = pltpu.VMEM
    prep = [
        v((ch, vec_rows), f32),
        v((3 * CPAD, ch), bf16), v((ch, CPAD), bf16), v((hid, ch), bf16), v((ch, hid), bf16),
        v((ch, CPAD), bf16), v((ch, CPAD), bf16), v((ch, CPAD), bf16), v((CPAD, ch), bf16),
        v((ch, hid), bf16), v((hid, ch), bf16),
        v((9 * CPAD, ch), bf16),
        v((TOK, LANE), f32),
        v((TOK, LANE), f32),
        v((hid, LANE), f32),
        v((10, ch, LANE), f32),
        v((2, CPAD, LANE), f32),
    ]
    wins = px // TOK
    tmp = [
        v((px, 9 * CPAD), bf16),
        v((CPAD, px), bf16), v((CPAD, px), bf16), v((CPAD, px), bf16), v((hid, px), bf16), v((CPAD, px), bf16),
        v((wins, CPAD, LANE), bf16),
        v((wins, 3 * TOK, LANE), f32),
        v((wins, 3 * TOK, LANE), bf16),
        v((2, px, CPAD), bf16),
        v((ch, px), f32),
        v((CPAD, px), bf16),
        v((CPAD, px), bf16),
        v((2, px, CPAD), bf16),
        v((ch, px), f32),
        v((ch, px), f32),
        v((hid, px), f32),
        v((CPAD, px), bf16),
        v((CPAD, px), bf16),
        v((CPAD, px), bf16),
        v((8, px), f32),
        v((ch, px), bf16),
        v((hid, px), bf16),
        v((ch, px), f32),
    ]
    return prep + tmp


def conv_kernel(image_side, own_rows, info, hc_ref, c1_ref, c2_ref, hg_ref, ig_ref, x_ref, vec_ref, conv_ref, out_ref, ig_out, cs, wc):
    ch = x_ref.shape[1]

    @pl.when(pl.program_id(0) == 0)
    def _():
        wc[...] = jnp.zeros_like(wc)
        cs[...] = jnp.zeros_like(cs)
        for tap in range(9):
            wc[tap * TAP : tap * TAP + ch, :] = conv_ref[tap // 3, tap % 3].astype(bf16)

    first = jnp.where(info[0] == 0, 0.0, 1.0).astype(f32)
    last = jnp.where(info[1] == 1, 0.0, 1.0).astype(f32)
    need = own_rows + 2
    col = lax.broadcasted_iota(jnp.int32, (1, image_side, ch), 1)
    halo = hc_ref.shape[1]
    for r in range(need):
        if r < halo:
            row = hc_ref[0, r : r + 1]
        elif r - halo < c1_ref.shape[1]:
            row = c1_ref[0, r - halo : r - halo + 1]
        else:
            at = r - halo - c1_ref.shape[1]
            row = c2_ref[0, at : at + 1]
        row = row.astype(f32)
        if r == 0:
            row = row * first
        if r == need - 1:
            row = row * last
        left = jnp.where(col == 0, 0.0, roll_cols(row, -1))
        right = jnp.where(col == image_side - 1, 0.0, roll_cols(row, 1))
        at = slice(r * image_side, (r + 1) * image_side)
        cs[at, 0:ch] = left[0].astype(bf16)
        cs[at, TAP : TAP + ch] = row[0].astype(bf16)
        cs[at, 2 * TAP : 2 * TAP + ch] = right[0].astype(bf16)
    bias = vec_ref[10:11, :]
    x_rows = jnp.swapaxes(x_ref[0].astype(f32), 0, 1)
    done = []
    for r in range(0, own_rows, WIN):
        total = None
        for i in range(3):
            at = slice((r + i) * image_side, (r + i + WIN) * image_side)
            term = nn(cs[at, :], wc[i * 3 * TAP : (i + 1) * 3 * TAP, :])
            total = term if total is None else total + term
        total = total + bias
        for k in range(WIN):
            done.append(jnp.transpose(total[k * image_side : (k + 1) * image_side]) + x_rows[r + k])
    out_ref[0] = jnp.swapaxes(jnp.stack(done), 0, 1).astype(bf16)
    kept = jnp.swapaxes(ig_ref[0], 0, 1)
    new = [hg_ref[0, r].astype(f32) for r in range(SHIFT)] + [kept[r] for r in range(SHIFT, WIN)]
    ig_out[0] = jnp.swapaxes(jnp.stack(new), 0, 1)


def split_bits(size):
    return [b for b in range(size.bit_length() - 1)]


def exchange_kernel(stages, g_ref, out_ref, work, given, low, send_sem, recv_sem):
    rows = g_ref.shape[0]

    def meet(stage):
        axis, b = stage
        me = lax.axis_index(axis)
        step = 2**b
        bit = (me // step) % 2
        return {axis: me + (1 - 2 * bit) * step}, bit

    barrier = pltpu.get_barrier_semaphore()
    for stage in stages:
        other, _ = meet(stage)
        pl.semaphore_signal(barrier, inc=1, device_id=other, device_id_type=pl.DeviceIdType.MESH)
    pl.semaphore_wait(barrier, len(stages))

    def span(start, size):
        return pl.ds(pl.multiple_of(start, 16), size)

    start = 0
    size = rows
    starts = []
    taken = 0
    for s, stage in enumerate(stages):
        other, bit = meet(stage)
        size = size // 2
        starts.append(start)
        keep = start + bit * size
        give = start + (1 - bit) * size
        source = g_ref if s == 0 else work
        copy = pltpu.make_async_remote_copy(
            src_ref=source.at[span(give, size)],
            dst_ref=given.at[pl.ds(taken, size)],
            send_sem=send_sem.at[s],
            recv_sem=recv_sem.at[s],
            device_id=other,
            device_id_type=pl.DeviceIdType.MESH,
        )
        copy.start()
        copy.wait()
        total = source[span(keep, size), :] + given[taken : taken + size, :]
        if s < len(stages) - 1:
            work[span(keep, size), :] = total
        else:
            low[span(keep, size), :] = total.astype(bf16)
        taken += size
        start = keep
    for s in reversed(range(len(stages))):
        other, bit = meet(stages[s])
        n = len(stages) + s
        copy = pltpu.make_async_remote_copy(
            src_ref=low.at[span(start, size)],
            dst_ref=low.at[span(start, size)],
            send_sem=send_sem.at[n],
            recv_sem=recv_sem.at[n],
            device_id=other,
            device_id_type=pl.DeviceIdType.MESH,
        )
        copy.start()
        copy.wait()
        start = starts[s]
        size = size * 2
    out_ref[...] = low[...]


def reduce_all(packed, sizes):
    stages = [(axis, b) for axis, size in sizes for b in split_bits(size)]
    rows = packed.shape[0]
    vmem = pl.BlockSpec(memory_space=pltpu.VMEM)
    return pl.pallas_call(
        functools.partial(exchange_kernel, stages),
        in_specs=[vmem],
        out_specs=vmem,
        out_shape=jax.ShapeDtypeStruct(packed.shape, bf16),
        scratch_shapes=[
            pltpu.VMEM(packed.shape, f32),
            pltpu.VMEM(packed.shape, f32),
            pltpu.VMEM(packed.shape, bf16),
            pltpu.SemaphoreType.DMA((2 * len(stages),)),
            pltpu.SemaphoreType.DMA((2 * len(stages),)),
        ],
        compiler_params=pltpu.CompilerParams(
            collective_id=0, has_side_effects=True, vmem_limit_bytes=40 * 1024 * 1024
        ),
        name="sum_gradients",
    )(packed)


def adam_kernel(scal, g_ref, *refs):
    weights, firsts, seconds = refs[0:7], refs[7:14], refs[14:21]
    norm_ref, psnr_ref, outs = refs[21], refs[22], refs[23:44]
    ch = weights[2].shape[0]
    up, count, vec_at, rel_at, used = pack_rows(ch)
    rest = ch - LANE

    def block(k):
        left = g_ref[k * up : (k + 1) * up, :].astype(f32)
        at = (count + k // 2) * up
        right = g_ref[at : at + up, :].astype(f32)
        if k % 2:
            right = pltpu.roll(right, TOK, 1)
        return jnp.concatenate([left, right[:, :rest]], axis=1)[:ch]

    vec_rows = g_ref[vec_at : vec_at + 32, :].astype(f32)
    vec = jnp.concatenate([vec_rows[:11], vec_rows[16:27, :rest]], axis=1)
    psnr = vec_rows[11:12] + vec_rows[12:13] + vec_rows[13:14]
    psnr_ref[...] = jnp.sum(psnr, axis=1, keepdims=True)

    span = 2 * WIN
    wide = span * span
    at = lax.broadcasted_iota(jnp.int32, (TOK, wide), 0)
    to = lax.broadcasted_iota(jnp.int32, (TOK, wide), 1)
    place = ((at >> 3) + (WIN - 1)) * span + (at & 7) + (WIN - 1)
    expand = (to == place).astype(f32).astype(bf16)
    pairs = g_ref[rel_at:used, :]
    rel_rows = []
    for p in range(3):
        for parity in range(2):
            part = pairs[p * TOK : (p + 1) * TOK, :].astype(f32)
            if parity:
                part = pltpu.roll(part, TOK, 1)
            spread = nn(part[:, :TOK].astype(bf16), expand)
            total = jnp.zeros((WIN, wide), f32)
            for row in range(WIN):
                piece = spread[row * WIN : (row + 1) * WIN]
                piece = pltpu.roll(piece, (wide - span * row) % wide, 1)
                total = total + piece
            line = total[0:1]
            for c in range(1, WIN):
                line = line + pltpu.roll(total, wide - c, 1)[c : c + 1]
            rel_rows.append(line)
    rel = jnp.concatenate(rel_rows, axis=0)
    rel = jnp.concatenate(
        [rel[:, k * span : k * span + span - 1] for k in range(span - 1)], axis=1
    )
    qkv = jnp.concatenate([block(9), block(10), block(11)], axis=1)
    fc1 = jnp.concatenate([block(13), block(14)], axis=1)
    fc2 = jnp.concatenate([block(15), block(16)], axis=1)
    small = [vec, qkv, block(12), rel, fc1, fc2]
    taps = [block(t) for t in range(9)]
    total = jnp.zeros((1, 1), f32)
    for g in small + taps:
        total = total + jnp.sum(jnp.sum(g * g, axis=0, keepdims=True), axis=1, keepdims=True)
    norm = jnp.sqrt(total)
    norm_ref[...] = norm
    clip = jnp.minimum(1.0, max_norm / (norm + 1e-06))
    fix_one, fix_two = scal[0], scal[1]

    def update(w, m1, m2, g, rate):
        g = g * clip
        m1 = beta_one * m1 + (1.0 - beta_one) * g
        m2 = beta_two * m2 + (1.0 - beta_two) * g * g
        step = (m1 / fix_one) / (jnp.sqrt(m2 / fix_two) + adam_eps)
        return w - rate * (step + decay_rate * w), m1, m2

    for k, g in enumerate(small):
        new = update(weights[k][...], firsts[k][...], seconds[k][...], g, vector_rate if k == 0 else learn_rate)
        for ref, value in zip(outs[3 * k : 3 * k + 3], new):
            ref[...] = value
    for t, g in enumerate(taps):
        at = (t // 3, t % 3)
        new = update(weights[6][at], firsts[6][at], seconds[6][at], g, learn_rate)
        for ref, value in zip(outs[18:21], new):
            ref[at] = value


def relative_onehot_keys_first():
    position = np.arange(TOK)
    pos_row, pos_col = position // WIN, position % WIN
    span = 2 * WIN - 1
    index = (pos_row[None, :] - pos_row[:, None] + WIN - 1) * span + (
        pos_col[None, :] - pos_col[:, None] + WIN - 1
    )
    return index.reshape(-1), span * span


def on_device(
    images, cotangent, valid_size,
    vectors, vectors_first, vectors_second,
    qkv_weight, qkv_first, qkv_second,
    proj_weight, proj_first, proj_second,
    rel_table, rel_first, rel_second,
    fc1_weight, fc1_first, fc1_second,
    fc2_weight, fc2_first, fc2_second,
    conv_weight, conv_first, conv_second,
    step, sr_crops, hr_crops, psnr_running,
):
    count, own_rows, image_side, ch = images.shape
    out_shape = (count, ch, own_rows, image_side)
    hid = fc1_weight.shape[1]
    px = image_side * WIN
    blocks = own_rows // WIN
    heads = lax.axis_size("head")
    place = lax.axis_index("head")
    to_lower = [((i + 1) % heads, i) for i in range(heads)]
    to_upper = [(i, (i + 1) % heads) for i in range(heads)]
    info = jnp.concatenate(
        [
            jnp.stack([place, (place == heads - 1).astype(jnp.int32)]).astype(jnp.int32),
            valid_size.astype(jnp.int32),
            ((lax.axis_index("dp") * heads + place) % LANE)[None].astype(jnp.int32),
        ]
    )
    images = images.transpose(0, 3, 1, 2)
    cotangent = cotangent.transpose(0, 3, 1, 2)
    halo = lax.ppermute(
        jnp.concatenate([images[:, :, :SHIFT], cotangent[:, :, : SHIFT + 1]], axis=2), "head", to_lower
    )

    index, span = relative_onehot_keys_first()
    onehot = (jnp.asarray(index)[:, None] == jnp.arange(span)[None, :]).astype(f32)
    bias = jnp.dot(onehot, rel_table, precision=highest)
    bias = bias.reshape(TOK, TOK, 3, 2).transpose(2, 0, 3, 1).reshape(3, TOK, LANE)

    wts = (vectors, qkv_weight, proj_weight, fc1_weight, fc2_weight.T, conv_weight, bias)
    wts_specs = [whole(w.shape) for w in wts]
    acc_dims = acc_shapes(ch, hid)
    acc_types = [jax.ShapeDtypeStruct(s, f32) for s in acc_dims]
    smem = pl.BlockSpec(memory_space=pltpu.SMEM)
    params = pltpu.CompilerParams(
        dimension_semantics=("arbitrary", "arbitrary"), vmem_limit_bytes=60 * 1024 * 1024
    )
    view = lambda rows, at, dims: pl.BlockSpec((1, ch, rows, image_side), lambda n, *_: (n, 0, at, 0))
    c_block = lambda size: pl.BlockSpec((1, size, image_side, ch), lambda n, *_: (n, 0, 0, 0))
    row_view = pltpu.VMEM((own_rows, ch, image_side), f32)
    c1, ig, *acc = pl.pallas_call(
        functools.partial(inner_kernel, image_side, own_rows),
        grid=(count, blocks - 1),
        in_specs=[smem, view(own_rows, 0, 2), view(own_rows, 0, 2), *wts_specs],
        out_specs=[
            pl.BlockSpec((1, WIN, image_side, ch), lambda n, r: (n, r, 0, 0)),
            view(own_rows, 0, 2),
            *[whole(s) for s in acc_dims],
        ],
        out_shape=[
            jax.ShapeDtypeStruct((count, own_rows - WIN, image_side, ch), bf16),
            jax.ShapeDtypeStruct(out_shape, f32),
            *acc_types,
        ],
        scratch_shapes=[row_view] * 3 + scratches(ch, hid, px, vectors.shape[0]),
        compiler_params=params,
        name="inner_windows",
    )(info, images, cotangent, *wts)
    device_count = lax.axis_size("dp") * heads
    unit = 16 * device_count
    rows = -(-pack_rows(ch)[-1] // unit) * unit
    c2, ig, ig_halo, packed = pl.pallas_call(
        functools.partial(last_kernel, image_side, own_rows),
        grid=(count,),
        in_specs=[
            smem,
            view(WIN, blocks - 1, 1),
            view(WIN, blocks - 1, 1),
            view(2 * SHIFT + 1, 0, 1),
            view(WIN, blocks - 1, 1),
            *wts_specs,
            *[whole(s) for s in acc_dims],
            whole(sr_crops.shape),
            whole(hr_crops.shape),
        ],
        out_specs=[
            c_block(WIN),
            view(WIN, blocks - 1, 1),
            pl.BlockSpec((1, SHIFT, ch, image_side), lambda n: (n, 0, 0, 0)),
            whole((rows, LANE)),
        ],
        out_shape=[
            jax.ShapeDtypeStruct((count, WIN, image_side, ch), bf16),
            jax.ShapeDtypeStruct(out_shape, f32),
            jax.ShapeDtypeStruct((count, SHIFT, ch, image_side), bf16),
            jax.ShapeDtypeStruct((rows, LANE), f32),
        ],
        input_output_aliases={4: 1},
        scratch_shapes=[pltpu.VMEM(s, f32) for s in acc_dims] + scratches(ch, hid, px, vectors.shape[0]),
        compiler_params=pltpu.CompilerParams(
            dimension_semantics=("arbitrary",), vmem_limit_bytes=60 * 1024 * 1024
        ),
        name="last_windows",
    )(info, images, cotangent, halo, ig, *wts, *acc, sr_crops, hr_crops)

    c_halo = lax.ppermute(c2[:, WIN - SHIFT - 1 :], "head", to_upper)
    ig_halo = lax.ppermute(ig_halo, "head", to_upper)

    summed = reduce_all(packed, (("dp", lax.axis_size("dp")), ("head", heads)))

    output, image_grad = pl.pallas_call(
        functools.partial(conv_kernel, image_side, own_rows),
        grid=(count,),
        in_specs=[
            smem,
            c_block(SHIFT + 1), c_block(own_rows - WIN), c_block(WIN),
            pl.BlockSpec((1, SHIFT, ch, image_side), lambda n: (n, 0, 0, 0)),
            view(WIN, 0, 1),
            view(own_rows, 0, 1),
            whole(vectors.shape), whole(conv_weight.shape),
        ],
        out_specs=[view(own_rows, 0, 1), view(WIN, 0, 1)],
        out_shape=[jax.ShapeDtypeStruct(out_shape, bf16), jax.ShapeDtypeStruct(out_shape, f32)],
        input_output_aliases={5: 1},
        scratch_shapes=[
            pltpu.VMEM(((own_rows + 2) * image_side, 3 * TAP), bf16),
            pltpu.VMEM((9 * TAP, ch), bf16),
        ],
        compiler_params=pltpu.CompilerParams(
            dimension_semantics=("arbitrary",), vmem_limit_bytes=60 * 1024 * 1024
        ),
        name="conv_output",
    )(info, c_halo, c1, c2, ig_halo, ig, images, vectors, conv_weight)
    output, image_grad = output.transpose(0, 2, 3, 1), image_grad.transpose(0, 2, 3, 1)

    step_count = step[0].astype(f32)
    scal = jnp.stack([1.0 - beta_one**step_count, 1.0 - beta_two**step_count])
    weights = (vectors, qkv_weight, proj_weight, rel_table.T, fc1_weight, fc2_weight.T, conv_weight)
    firsts = (vectors_first, qkv_first, proj_first, rel_first.T, fc1_first, fc2_first.T, conv_first)
    seconds = (vectors_second, qkv_second, proj_second, rel_second.T, fc1_second, fc2_second.T, conv_second)
    vmem = pl.BlockSpec(memory_space=pltpu.VMEM)
    grad_norm, psnr, *updated = pl.pallas_call(
        adam_kernel,
        in_specs=[smem] + [vmem] * 22,
        out_specs=[vmem] * 23,
        out_shape=[jax.ShapeDtypeStruct((1, 1), f32)] * 2
        + [jax.ShapeDtypeStruct(w.shape, f32) for w in weights for _ in range(3)],
        compiler_params=pltpu.CompilerParams(vmem_limit_bytes=60 * 1024 * 1024),
        name="adam",
    )(scal, summed, *weights, *firsts, *seconds)
    for k in (9, 10, 11, 15, 16, 17):
        updated[k] = updated[k].T
    psnr_total = psnr_running + psnr.reshape(1)
    return (output, image_grad, grad_norm.reshape(1), psnr_total, *updated)


def solution(mesh):
    pixels = P("dp", "head", None, None)
    crops = P(("dp", "head"), None, None, None)
    placed = (pixels, pixels, P("dp")) + (P(),) * 22 + (crops, crops, P())
    return jax.shard_map(
        on_device,
        mesh=mesh,
        in_specs=placed,
        out_specs=(pixels, pixels) + (P(),) * 23,
        check_vma=False,
    )
```

time: 260 us -> 220 us (0.85)
  local copies, waits for them, and re-layouts: 44.8 us -> 13.8 us
  Pallas kernels: 198 us -> 188 us
    unnamed x20 -> x10, local copies, waits for them, and re-layouts: 29.6 us -> 1.08 us
    slice x7 -> x2, local copies, waits for them, and re-layouts: 7.87 us -> 2.71 us  [the longest x1 1.39 us: on_device(): images[:, :, :SHIFT]]
    pallas_call x1, Pallas kernels: 65.5 us -> 61.6 us  [reduce_all(): pl.pallas_call(functools.partial(exchange_kernel, stages), in_specs=[vmem...]
    pallas_call x1, Pallas kernels: 67.2 us -> 64 us  [on_device(): pl.pallas_call(functools.partial(inner_kernel, image_side, own_rows), gri...]
    pallas_call x1, Pallas kernels: 38.4 us -> 35.4 us  [on_device(): pl.pallas_call(functools.partial(last_kernel, image_side, own_rows), grid...]
  transfers between devices with their start and end apart: 3 -> 3, of which waited for: 0 -> 0; matrix products, arithmetic and copies ran while one was open for 8% -> 4% of each run, Pallas kernels for 56% -> 63%
where the time goes in v3:
time: 220 us; the launch traced here: 217 us
  Pallas kernels  188 us (85%)
  local copies, waits for them, and re-layouts  13.8 us (6%)
  starting transfers between devices  5.42 us (2%)
  between operations  4.42 us (2%)
  matrix products  2.55 us (1%)
    pallas_call x1, Pallas kernels, on_device(): pl.pallas_call(functools.partial(inner_kernel, image_side, own_rows), gri...  64 us
    pallas_call x1, Pallas kernels, reduce_all(): pl.pallas_call(functools.partial(exchange_kernel, stages), in_specs=[vmem...  61.6 us
    pallas_call x1, Pallas kernels, on_device(): pl.pallas_call(functools.partial(last_kernel, image_side, own_rows), grid...  35.4 us
    pallas_call x1, Pallas kernels, on_device(): pl.pallas_call(functools.partial(conv_kernel, image_side, own_rows), grid...  16.7 us
    pallas_call x1, Pallas kernels, on_device(): pl.pallas_call(adam_kernel, in_specs=[smem] + [vmem] * 22, out_specs=[vme...  10.7 us
    ppermute x1, starting transfers between devices, on_device(): lax.ppermute(jnp.concatenate([images[:, :, :SHIFT], cotangent[:, :, :SHIF...  5.1 us
  transfers between devices with their start and end apart: 3, of which 0 were waited for; matrix products, arithmetic and copies ran while one was open for 4% of the time, Pallas kernels for 63%

profile of v3, /device:TPU:0, one launch (start us, length us, event | category | flops | bytes accessed | tf_op | source)
XLA Modules:
  0.0 216.8 jit_solution(13385307128814768444)
XLA Ops:
  0.7 1.4 slice.12
  2.1 1.3 slice.13
  3.4 1.0 pad_maximum_fusion
  4.4 0.3 copy.57
  4.7 5.1 %collective-permute-start = (bf16[3,180,9,96]{3,1,2,0:T(8,128)(2,1)S(1)}, bf16[3,180,9,96]{3,1,2,0:T(8,128)(2,1)S(1)}, u32[]{:S(2)}, u32[]{:S(2)}) collective-permute-start(bf16[3,180,9,96]{3,1,2,0:T(8,128)(2,1)S(1)} %copy.57), channel_id=1, source_target_pairs={{1,0},{2,1},{3,2},{0,3},{5,4},{6,5},{7,6},{4,7},{9,8},{10,9},{11,1... | collective-permute-start | bytes 2799368 | tf_op jit(solution)/shard_map/ppermute | solution.py:884
  9.9 2.6 %fusion = f32[4096,6]{0,1:T(8,128)S(1)} fusion(f32[225,6]{0,1:T(8,128)S(1)} %copy-done.2, s32[4096]{0:T(1024)S(1)} %copy-done.4), kind=kOutput, calls=%fused_computation.1 | convolution fusion | flops 67276800 | bytes 120088 | tf_op jit(solution)/shard_map/dot_general | solution.py:890
  12.4 0.1 reshape.74
  12.5 0.2 copy.65
  12.7 0.8 reshape.75.refs_6_
  13.5 0.6 pad_add_fusion.info
  14.1 64.0 %inner_windows.1 = (bf16[3,16,96,180]{3,2,1,0:T(8,128)(2,1)}, f32[3,180,24,96]{3,2,1,0:T(8,128)}, f32[192,1728]{1,0:T(8,128)}, f32[3,192,192]{2,1,0:T(8,128)}, f...) custom-call(s32[6]{0:T(128)} %pad_add_fusion.info, ...), custom_call_target="tpu_custom_call" | custom-call | tf_op jit(solution)/shard_map/inner_windows/pallas_call | solution.py:904
  78.1 1.7 copy.59.halo_ref
  79.8 35.4 %last_windows.1 = (bf16[3,8,96,180]{3,2,1,0:T(8,128)(2,1)}, f32[3,180,24,96]{3,2,1,0:T(8,128)}, bf16[3,4,180,96]{3,2,1,0:T(8,128)(2,1)}, f32[5120,128]{1,0:T(8,128)}) custom-call(s32[6]{0:T(128)} %pad_add_fusion.info, bf16[3,180,24,96]{3,2,1,0:T(8,128)(2,1)} %bitcast.29, bf16[3,180,24,96]{3,2,1,0:T(8,128)(2,1)} %bitcast.34, ...), custom_call_target="tpu_custom_call", output_to_operand_aliasing={{1}: (4, {})} | custom-call | tf_op jit(solution)/shard_map/last_windows/pallas_call | solution.py:925
  115.2 1.3 slice.11
  116.5 1.2 copy.60
  117.7 1.3 copy.61
  119.0 0.3 collective-permute-start.2
  120.7 0.6 pad_maximum_fusion.1.scal
  121.3 61.6 %sum_gradients.1.g_ref = bf16[5120,128]{1,0:T(8,128)(2,1)S(1)} custom-call(f32[5120,128]{1,0:T(8,128)S(1)} %copy-done.1), custom_call_target="tpu_custom_call" | custom-call | tf_op jit(solution)/shard_map/sum_gradients/pallas_call | solution.py:748
  182.9 1.0 copy-done
  184.0 10.7 %adam.1 = (f32[1,1]{1,0:T(1,128)}, f32[1,1]{1,0:T(1,128)}, f32[11,180]{1,0:T(8,128)}, f32[11,180]{1,0:T(8,128)}, f32[11,180]{1,0:T(8,128)}, /*index=5*/f32[180,5...) custom-call(f32[2]{0:T(128)} %pad_maximum_fusion.1.scal, ...), custom_call_target="tpu_custom_call" | custom-call | tf_op jit(solution)/shard_map/adam/pallas_call | solution.py:995
  195.3 1.9 copy.63.hg_ref
  197.3 1.2 copy.62.hc_ref
  198.5 16.7 %conv_output.1 = (bf16[3,180,24,96]{3,2,1,0:T(8,128)(2,1)}, f32[3,180,24,96]{3,2,1,0:T(8,128)}) custom-call(s32[6]{0:T(128)} %pad_add_fusion.info, bf16[3,5,96,180]{3,2,1,0:T(8,128)(2,1)} %copy.62.hc_ref, bf16[3,16,96,180]{3,2,1,0:T(8,128)(2,1)} %get-tuple-element.72.c1_ref, ...), custom_call_target="tpu_custom_call", output_to_operand_aliasing={{1}: (5, {})} | custom-call | tf_op jit(solution)/shard_map/conv_output/pallas_call | solution.py:964
  (13 shorter events, 0.0 us)
Async XLA Ops:
  4.4 5.5 %copy-start.2 = (f32[225,6]{0,1:T(8,128)S(1)}, f32[225,6]{0,1:T(8,128)}, u32[]{:S(2)}) copy-start(f32[225,6]{0,1:T(8,128)} %param.41) | copy-start | bytes 16204
  4.4 5.5 %copy-start.4 = (s32[4096]{0:T(1024)S(1)}, s32[4096]{0:T(1024)}, u32[]{:S(2)}) copy-start(s32[4096]{0:T(1024)} %constant.38.clone) | copy-start | bytes 49156
  4.4 9.1 %copy-start.3 = (s32[3]{0:T(128)S(1)}, s32[3]{0:T(128)}, u32[]{:S(2)}) copy-start(s32[3]{0:T(128)} %param.31) | copy-start | bytes 40
  4.7 73.3 %collective-permute-start = (bf16[3,180,9,96]{3,1,2,0:T(8,128)(2,1)S(1)}, bf16[3,180,9,96]{3,1,2,0:T(8,128)(2,1)S(1)}, u32[]{:S(2)}, u32[]{:S(2)}) collective-permute-start(bf16[3,180,9,96]{3,1,2,0:T(8,128)(2,1)S(1)} %copy.57), channel_id=1, source_target_pairs={{1,0},{2,1},{3,2},{0,3},{5,4},{6,5},{7,6},{4,7},{9,8},{10,9},{11,1... | collective-permute-start | bytes 2799368 | tf_op jit(solution)/shard_map/ppermute | solution.py:884
  115.2 6.1 %copy-start.1 = (f32[5120,128]{1,0:T(8,128)S(1)}, f32[5120,128]{1,0:T(8,128)}, u32[]{:S(2)}) copy-start(f32[5120,128]{1,0:T(8,128)} %get-tuple-element.77.g_ref) | copy-start | bytes 7864324
  117.7 79.5 %collective-permute-start.1 = (bf16[3,5,96,180]{2,3,1,0:T(8,128)(2,1)}, bf16[3,5,96,180]{2,3,1,0:T(8,128)(2,1)S(1)}, u32[]{:S(2)}, u32[]{:S(2)}) collective-permute-start(bf16[3,5,96,180]{2,3,1,0:T(8,128)(2,1)} %copy.60), channel_id=1, source_target_pairs={{0,1},{1,2},{2,3},{3,0},{4,5},{5,6},{6,7},{7,4},{8,9},{9,10},{10,1... | collective-permute-start | bytes 1555208 | tf_op jit(solution)/shard_map/ppermute | solution.py:959
  119.0 76.3 %collective-permute-start.2 = (bf16[3,4,180,96]{3,1,2,0:T(4,128)(2,1)S(1)}, bf16[3,4,180,96]{3,1,2,0:T(4,128)(2,1)}, u32[]{:S(2)}, u32[]{:S(2)}) collective-permute-start(bf16[3,4,180,96]{3,1,2,0:T(4,128)(2,1)S(1)} %copy.61), channel_id=1, source_target_pairs={{0,1},{1,2},{2,3},{3,0},{4,5},{5,6},{6,7},{7,4},{8,9},{9,10},{10,1... | collective-permute-start | bytes 1244168 | tf_op jit(solution)/shard_map/ppermute | solution.py:960
  182.9 1.1 copy-start

commit v4 on v3

--- a/solution.py
+++ b/solution.py
@@ -620,64 +620,51 @@
     return prep + tmp
 
 
-def conv_kernel(image_side, own_rows, info, hc_ref, c1_ref, c2_ref, hg_ref, ig_ref, x_ref, vec_ref, conv_ref, out_ref, ig_out, cs, wc):
-    ch = x_ref.shape[1]
-
-    @pl.when(pl.program_id(0) == 0)
-    def _():
-        wc[...] = jnp.zeros_like(wc)
-        cs[...] = jnp.zeros_like(cs)
-        for tap in range(9):
-            wc[tap * TAP : tap * TAP + ch, :] = conv_ref[tap // 3, tap % 3].astype(bf16)
-
-    first = jnp.where(info[0] == 0, 0.0, 1.0).astype(f32)
-    last = jnp.where(info[1] == 1, 0.0, 1.0).astype(f32)
-    need = own_rows + 2
-    col = lax.broadcasted_iota(jnp.int32, (1, image_side, ch), 1)
-    halo = hc_ref.shape[1]
-    for r in range(need):
-        if r < halo:
-            row = hc_ref[0, r : r + 1]
-        elif r - halo < c1_ref.shape[1]:
-            row = c1_ref[0, r - halo : r - halo + 1]
-        else:
-            at = r - halo - c1_ref.shape[1]
-            row = c2_ref[0, at : at + 1]
-        row = row.astype(f32)
-        if r == 0:
-            row = row * first
-        if r == need - 1:
-            row = row * last
-        left = jnp.where(col == 0, 0.0, roll_cols(row, -1))
-        right = jnp.where(col == image_side - 1, 0.0, roll_cols(row, 1))
-        at = slice(r * image_side, (r + 1) * image_side)
-        cs[at, 0:ch] = left[0].astype(bf16)
-        cs[at, TAP : TAP + ch] = row[0].astype(bf16)
-        cs[at, 2 * TAP : 2 * TAP + ch] = right[0].astype(bf16)
-    bias = vec_ref[10:11, :]
-    x_rows = jnp.swapaxes(x_ref[0].astype(f32), 0, 1)
-    done = []
-    for r in range(0, own_rows, WIN):
-        total = None
-        for i in range(3):
-            at = slice((r + i) * image_side, (r + i + WIN) * image_side)
-            term = nn(cs[at, :], wc[i * 3 * TAP : (i + 1) * 3 * TAP, :])
-            total = term if total is None else total + term
-        total = total + bias
-        for k in range(WIN):
-            done.append(jnp.transpose(total[k * image_side : (k + 1) * image_side]) + x_rows[r + k])
-    out_ref[0] = jnp.swapaxes(jnp.stack(done), 0, 1).astype(bf16)
+def halo_kernel(halo_ref, ig_ref, ig_out):
     kept = jnp.swapaxes(ig_ref[0], 0, 1)
-    new = [hg_ref[0, r].astype(f32) for r in range(SHIFT)] + [kept[r] for r in range(SHIFT, WIN)]
+    new = [halo_ref[0, r].astype(f32) for r in range(SHIFT)] + [kept[r] for r in range(SHIFT, WIN)]
     ig_out[0] = jnp.swapaxes(jnp.stack(new), 0, 1)
 
 
-def split_bits(size):
-    return [b for b in range(size.bit_length() - 1)]
-
-
-def exchange_kernel(stages, g_ref, out_ref, work, given, low, send_sem, recv_sem):
-    rows = g_ref.shape[0]
+def bits_of(size):
+    return list(range(size.bit_length() - 1))
+
+
+def exchange_plan(sizes):
+    (dp_axis, dp_size), (head_axis, head_size) = sizes
+    first = (dp_axis, 0)
+    rest = [(dp_axis, b) for b in bits_of(dp_size)[1:]]
+    last = [(head_axis, b) for b in bits_of(head_size)]
+    half = len(rest) // 2
+    return first, [rest + last, rest[half:] + rest[:half] + last]
+
+
+def exchange_kernel(
+    first, orders, head_size,
+    g_in, c1_in, c2_in, x_in, halo_in, conv_in, vec_ref,
+    sum_ref, out_ref, halo_out,
+    g, work, given, low, c1, c2, c_halo, x, conv, wc, cs, rows_s, out_s,
+    send_sem, recv_sem, local_sem,
+):
+    count, ch, own_rows, image_side = x.shape
+    rows = g.shape[0]
+    mesh_id = pl.DeviceIdType.MESH
+    here = lax.axis_index("head")
+    upper = {"head": (here + 1) % head_size}
+    lower = {"head": (here + head_size - 1) % head_size}
+
+    def load(k, src, dst):
+        copy = pltpu.make_async_copy(src, dst, local_sem.at[k])
+        copy.start()
+        return copy
+
+    loads = [
+        load(0, g_in, g),
+        load(1, conv_in, conv),
+        load(2, c1_in, c1),
+        load(3, c2_in, c2),
+        load(4, x_in, x),
+    ]
 
     def meet(stage):
         axis, b = stage
@@ -687,81 +674,199 @@
         return {axis: me + (1 - 2 * bit) * step}, bit
 
     barrier = pltpu.get_barrier_semaphore()
-    for stage in stages:
-        other, _ = meet(stage)
-        pl.semaphore_signal(barrier, inc=1, device_id=other, device_id_type=pl.DeviceIdType.MESH)
-    pl.semaphore_wait(barrier, len(stages))
+    friends = [meet(stage)[0] for stage in [first] + orders[0]] + [upper, lower]
+    for other in friends:
+        pl.semaphore_signal(barrier, inc=1, device_id=other, device_id_type=mesh_id)
+    pl.semaphore_wait(barrier, len(friends))
+
+    used = [0]
+
+    def send(src, dst, other):
+        k = used[0]
+        used[0] += 1
+        copy = pltpu.make_async_remote_copy(
+            src_ref=src,
+            dst_ref=dst,
+            send_sem=send_sem.at[k],
+            recv_sem=recv_sem.at[k],
+            device_id=other,
+            device_id_type=mesh_id,
+        )
+        copy.start()
+        return copy
 
     def span(start, size):
         return pl.ds(pl.multiple_of(start, 16), size)
 
-    start = 0
-    size = rows
-    starts = []
-    taken = 0
-    for s, stage in enumerate(stages):
-        other, bit = meet(stage)
-        size = size // 2
-        starts.append(start)
-        keep = start + bit * size
-        give = start + (1 - bit) * size
-        source = g_ref if s == 0 else work
-        copy = pltpu.make_async_remote_copy(
-            src_ref=source.at[span(give, size)],
-            dst_ref=given.at[pl.ds(taken, size)],
-            send_sem=send_sem.at[s],
-            recv_sem=recv_sem.at[s],
-            device_id=other,
-            device_id_type=pl.DeviceIdType.MESH,
-        )
-        copy.start()
+    col = lax.broadcasted_iota(jnp.int32, (1, image_side, ch), 1)
+    top = jnp.where(here == 0, 0.0, 1.0).astype(f32)
+    bottom = jnp.where(here == head_size - 1, 0.0, 1.0).astype(f32)
+
+    def prepare():
+        loads[1].wait()
+        wc[...] = jnp.zeros_like(wc)
+        cs[...] = jnp.zeros_like(cs)
+        for tap in range(9):
+            wc[tap * TAP : tap * TAP + ch, :] = conv[tap // 3, tap % 3].astype(bf16)
+
+    def conv_rows(image, block):
+        for k in range(WIN + 2):
+            r = block * WIN + k - 1 - SHIFT
+            if r < 0:
+                row = c_halo[image, r + SHIFT + 1 : r + SHIFT + 2]
+            elif r < c1.shape[1]:
+                row = c1[image, r : r + 1]
+            else:
+                row = c2[image, r - c1.shape[1] : r - c1.shape[1] + 1]
+            row = row.astype(f32)
+            if block == 0 and k == 0:
+                row = row * top
+            if block == own_rows // WIN - 1 and k == WIN + 1:
+                row = row * bottom
+            left = jnp.where(col == 0, 0.0, roll_cols(row, -1))
+            right = jnp.where(col == image_side - 1, 0.0, roll_cols(row, 1))
+            at = slice(k * image_side, (k + 1) * image_side)
+            cs[at, 0:ch] = left[0].astype(bf16)
+            cs[at, TAP : TAP + ch] = row[0].astype(bf16)
+            cs[at, 2 * TAP : 2 * TAP + ch] = right[0].astype(bf16)
+        total = vec_ref[10:11, :]
+        for i in range(3):
+            at = slice(i * image_side, (i + WIN) * image_side)
+            total = total + nn(cs[at, :], wc[i * 3 * TAP : (i + 1) * 3 * TAP, :])
+        for k in range(WIN):
+            rows_s[image, block * WIN + k] = jnp.transpose(total[k * image_side : (k + 1) * image_side])
+
+    stores = []
+
+    def finish(image):
+        out_s[image] = (jnp.swapaxes(rows_s[image], 0, 1) + x[image].astype(f32)).astype(bf16)
+        stores.append(load(5 + image, out_s.at[image], out_ref.at[image]))
+
+    blocks = own_rows // WIN
+    inner = [(n, b) for n in range(count) for b in range(1, blocks)]
+    outer = [(n, 0) for n in range(count)]
+    stage_count = 2 * (1 + len(orders[0]))
+    jobs = [[] for _ in range(stage_count)]
+    for k, job in enumerate(inner + outer):
+        jobs[min(1 + k * (stage_count - 2) // len(inner + outer), stage_count - 2)].append(job)
+
+    halos = []
+
+    def work_on(stage):
+        if stage == 0:
+            prepare()
+        if stage == 1:
+            for k in (2, 3, 4):
+                loads[k].wait()
+        for image, block in jobs[stage]:
+            if block == 0 and image == 0:
+                halos[0].wait()
+            conv_rows(image, block)
+            if block == 0:
+                finish(image)
+
+    loads[0].wait()
+    other, bit = meet(first)
+    half = rows // 2
+    copy = send(g.at[span((1 - bit) * half, half)], given.at[pl.ds(0, half)], other)
+    halos.append(send(c2_in.at[:, WIN - SHIFT - 1 :], c_halo, upper))
+    halos.append(send(halo_in, halo_out, upper))
+    work_on(0)
+    copy.wait()
+    keep = bit * half
+    work[span(keep, half), :] = g[span(keep, half), :] + given[:half, :]
+    unit = 16 * 2 ** len(orders[0])
+    parts = half // unit
+    cut = (parts + 1) // 2 * unit
+    begin = [keep, keep + cut]
+    size = [cut, half - cut]
+    taken = half
+    trail = [[], []]
+    for s in range(len(orders[0])):
+        flying = []
+        for p in range(2):
+            if size[p] == 0:
+                continue
+            other, bit = meet(orders[p][s])
+            size[p] //= 2
+            trail[p].append(begin[p])
+            give = begin[p] + (1 - bit) * size[p]
+            begin[p] = begin[p] + bit * size[p]
+            flying.append((p, taken, send(work.at[span(give, size[p])], given.at[pl.ds(taken, size[p])], other)))
+            taken += size[p]
+        work_on(1 + s)
+        for p, at, copy in flying:
+            copy.wait()
+            total = work[span(begin[p], size[p]), :] + given[at : at + size[p], :]
+            if s < len(orders[0]) - 1:
+                work[span(begin[p], size[p]), :] = total
+            else:
+                low[span(begin[p], size[p]), :] = total.astype(bf16)
+
+    for s in reversed(range(len(orders[0]))):
+        flying = []
+        for p in range(2):
+            if size[p] == 0:
+                continue
+            other, _ = meet(orders[p][s])
+            here_now = low.at[span(begin[p], size[p])]
+            flying.append(send(here_now, here_now, other))
+            begin[p] = trail[p][s]
+            size[p] *= 2
+        work_on(2 * len(orders[0]) - s)
+        for copy in flying:
+            copy.wait()
+    other, _ = meet(first)
+    here_now = low.at[span(keep, half)]
+    copy = send(here_now, here_now, other)
+    work_on(stage_count - 1)
+    copy.wait()
+    sum_ref[...] = low[...]
+    halos[1].wait()
+    for copy in stores:
         copy.wait()
-        total = source[span(keep, size), :] + given[taken : taken + size, :]
-        if s < len(stages) - 1:
-            work[span(keep, size), :] = total
-        else:
-            low[span(keep, size), :] = total.astype(bf16)
-        taken += size
-        start = keep
-    for s in reversed(range(len(stages))):
-        other, bit = meet(stages[s])
-        n = len(stages) + s
-        copy = pltpu.make_async_remote_copy(
-            src_ref=low.at[span(start, size)],
-            dst_ref=low.at[span(start, size)],
-            send_sem=send_sem.at[n],
-            recv_sem=recv_sem.at[n],
-            device_id=other,
-            device_id_type=pl.DeviceIdType.MESH,
-        )
-        copy.start()
-        copy.wait()
-        start = starts[s]
-        size = size * 2
-    out_ref[...] = low[...]
-
-
-def reduce_all(packed, sizes):
-    stages = [(axis, b) for axis, size in sizes for b in split_bits(size)]
+
+
+def exchange(packed, c1, c2, images, ig_halo, conv_weight, vectors, sizes):
+    first, orders = exchange_plan(sizes)
     rows = packed.shape[0]
+    count, ch, own_rows, image_side = images.shape
     vmem = pl.BlockSpec(memory_space=pltpu.VMEM)
+    hbm = pl.BlockSpec(memory_space=pl.ANY)
+    v = pltpu.VMEM
+    sends = 2 + 2 + 4 * len(orders[0])
     return pl.pallas_call(
-        functools.partial(exchange_kernel, stages),
-        in_specs=[vmem],
-        out_specs=vmem,
-        out_shape=jax.ShapeDtypeStruct(packed.shape, bf16),
+        functools.partial(exchange_kernel, first, orders, sizes[1][1]),
+        in_specs=[hbm] * 6 + [vmem],
+        out_specs=[vmem, hbm, hbm],
+        out_shape=[
+            jax.ShapeDtypeStruct(packed.shape, bf16),
+            jax.ShapeDtypeStruct(images.shape, bf16),
+            jax.ShapeDtypeStruct(ig_halo.shape, bf16),
+        ],
         scratch_shapes=[
-            pltpu.VMEM(packed.shape, f32),
-            pltpu.VMEM(packed.shape, f32),
-            pltpu.VMEM(packed.shape, bf16),
-            pltpu.SemaphoreType.DMA((2 * len(stages),)),
-            pltpu.SemaphoreType.DMA((2 * len(stages),)),
+            v(packed.shape, f32),
+            v(packed.shape, f32),
+            v(packed.shape, f32),
+            v(packed.shape, bf16),
+            v(c1.shape, bf16),
+            v(c2.shape, bf16),
+            v((count, SHIFT + 1, image_side, ch), bf16),
+            v(images.shape, bf16),
+            v(conv_weight.shape, f32),
+            v((9 * TAP, ch), bf16),
+            v(((WIN + 2) * image_side, 3 * TAP), bf16),
+            v((count, own_rows, ch, image_side), f32),
+            v(images.shape, bf16),
+            pltpu.SemaphoreType.DMA((sends,)),
+            pltpu.SemaphoreType.DMA((sends,)),
+            pltpu.SemaphoreType.DMA((5 + count,)),
         ],
         compiler_params=pltpu.CompilerParams(
-            collective_id=0, has_side_effects=True, vmem_limit_bytes=40 * 1024 * 1024
+            collective_id=0, has_side_effects=True, vmem_limit_bytes=60 * 1024 * 1024
         ),
         name="sum_gradients",
-    )(packed)
+    )(packed, c1, c2, images, ig_halo, conv_weight, vectors)
 
 
 def adam_kernel(scal, g_ref, *refs):
@@ -871,7 +976,6 @@
     heads = lax.axis_size("head")
     place = lax.axis_index("head")
     to_lower = [((i + 1) % heads, i) for i in range(heads)]
-    to_upper = [(i, (i + 1) % heads) for i in range(heads)]
     info = jnp.concatenate(
         [
             jnp.stack([place, (place == heads - 1).astype(jnp.int32)]).astype(jnp.int32),
@@ -956,34 +1060,18 @@
         name="last_windows",
     )(info, images, cotangent, halo, ig, *wts, *acc, sr_crops, hr_crops)
 
-    c_halo = lax.ppermute(c2[:, WIN - SHIFT - 1 :], "head", to_upper)
-    ig_halo = lax.ppermute(ig_halo, "head", to_upper)
-
-    summed = reduce_all(packed, (("dp", lax.axis_size("dp")), ("head", heads)))
-
-    output, image_grad = pl.pallas_call(
-        functools.partial(conv_kernel, image_side, own_rows),
+    summed, output, ig_halo = exchange(
+        packed, c1, c2, images, ig_halo, conv_weight, vectors, (("dp", lax.axis_size("dp")), ("head", heads))
+    )
+    image_grad = pl.pallas_call(
+        halo_kernel,
         grid=(count,),
-        in_specs=[
-            smem,
-            c_block(SHIFT + 1), c_block(own_rows - WIN), c_block(WIN),
-            pl.BlockSpec((1, SHIFT, ch, image_side), lambda n: (n, 0, 0, 0)),
-            view(WIN, 0, 1),
-            view(own_rows, 0, 1),
-            whole(vectors.shape), whole(conv_weight.shape),
-        ],
-        out_specs=[view(own_rows, 0, 1), view(WIN, 0, 1)],
-        out_shape=[jax.ShapeDtypeStruct(out_shape, bf16), jax.ShapeDtypeStruct(out_shape, f32)],
-        input_output_aliases={5: 1},
-        scratch_shapes=[
-            pltpu.VMEM(((own_rows + 2) * image_side, 3 * TAP), bf16),
-            pltpu.VMEM((9 * TAP, ch), bf16),
-        ],
-        compiler_params=pltpu.CompilerParams(
-            dimension_semantics=("arbitrary",), vmem_limit_bytes=60 * 1024 * 1024
-        ),
-        name="conv_output",
-    )(info, c_halo, c1, c2, ig_halo, ig, images, vectors, conv_weight)
+        in_specs=[pl.BlockSpec((1, SHIFT, ch, image_side), lambda n: (n, 0, 0, 0)), view(WIN, 0, 1)],
+        out_specs=view(WIN, 0, 1),
+        out_shape=jax.ShapeDtypeStruct(out_shape, f32),
+        input_output_aliases={1: 0},
+        name="halo_rows",
+    )(ig_halo, ig)
     output, image_grad = output.transpose(0, 2, 3, 1), image_grad.transpose(0, 2, 3, 1)
 
     step_count = step[0].astype(f32)

time: 220 us -> 200 us (0.909)
  Pallas kernels: 188 us -> 176 us
  local copies, waits for them, and re-layouts: 13.8 us -> 7.58 us
    pallas_call x2, Pallas kernels: 78.3 us -> 65.4 us  [the longest x1 61.2 us: exchange(): pl.pallas_call(functools.partial(exchange_kernel, first, orders, sizes[1]...]
    ppermute x2 -> x0, local copies, waits for them, and re-layouts: 3.15 us -> none  [the longest x1 1.95 us: on_device(): ig_halo = lax.ppermute(ig_halo, 'head', to_upper)]
    slice x2 -> x0, local copies, waits for them, and re-layouts: 2.51 us -> none  [on_device(): c_halo = lax.ppermute(c2[:, WIN - SHIFT - 1:], 'head', to_upper)]
  transfers between devices with their start and end apart: 3 -> 1, of which waited for: 0 -> 0; matrix products, arithmetic and copies ran while one was open for 4% -> 2% of each run, Pallas kernels for 63% -> 32%
where the time goes in v4:
time: 200 us; the launch traced here: 197 us
  Pallas kernels  176 us (88%)
  local copies, waits for them, and re-layouts  7.58 us (4%)
  starting transfers between devices  5.1 us (3%)
  between operations  4.12 us (2%)
  matrix products  2.55 us (1%)
  other arithmetic  2.15 us (1%)
    pallas_call x1, Pallas kernels, on_device(): pl.pallas_call(functools.partial(inner_kernel, image_side, own_rows), gri...  64 us
    pallas_call x1, Pallas kernels, exchange(): pl.pallas_call(functools.partial(exchange_kernel, first, orders, sizes[1]...  61.2 us
    pallas_call x1, Pallas kernels, on_device(): pl.pallas_call(functools.partial(last_kernel, image_side, own_rows), grid...  35.8 us
    pallas_call x1, Pallas kernels, on_device(): pl.pallas_call(adam_kernel, in_specs=[smem] + [vmem] * 22, out_specs=[vme...  10.8 us
    ppermute x1, starting transfers between devices, on_device(): lax.ppermute(jnp.concatenate([images[:, :, :SHIFT], cotangent[:, :, :SHIF...  5.1 us
    pallas_call x1, Pallas kernels, on_device(): pl.pallas_call(halo_kernel, grid=(count,), in_specs=[pl.BlockSpec((1, SHI...  4.19 us
  transfers between devices with their start and end apart: 1, of which 0 were waited for; matrix products, arithmetic and copies ran while one was open for 2% of the time, Pallas kernels for 32%

profile of v4, /device:TPU:0, one launch (start us, length us, event | category | flops | bytes accessed | tf_op | source)
XLA Modules:
  0.0 197.4 jit_solution(3624685372743135958)
XLA Ops:
  0.7 1.4 slice.8
  2.1 1.3 slice.9
  3.4 1.0 pad_maximum_fusion
  4.4 0.0 copy-start.1
  4.4 0.0 copy-start.3
  4.4 0.0 copy-start.2
  4.4 0.3 copy.57
  4.7 5.1 %collective-permute-start = (bf16[3,180,9,96]{3,1,2,0:T(8,128)(2,1)S(1)}, bf16[3,180,9,96]{3,1,2,0:T(8,128)(2,1)S(1)}, u32[]{:S(2)}, u32[]{:S(2)}) collective-permute-start(bf16[3,180,9,96]{3,1,2,0:T(8,128)(2,1)S(1)} %copy.57), channel_id=1, source_target_pairs={{1,0},{2,1},{3,2},{0,3},{5,4},{6,5},{7,6},{4,7},{9,8},{10,9},{11,1... | collective-permute-start | bytes 2799368 | tf_op jit(solution)/shard_map/ppermute | solution.py:988
  9.8 0.0 copy-done.1
  9.8 2.6 %fusion = f32[4096,6]{0,1:T(8,128)S(1)} fusion(f32[225,6]{0,1:T(8,128)S(1)} %copy-done.1, s32[4096]{0:T(1024)S(1)} %copy-done.3), kind=kOutput, calls=%fused_computation.1 | convolution fusion | flops 67276800 | bytes 120088 | tf_op jit(solution)/shard_map/dot_general | solution.py:994
  12.4 0.1 reshape.74
  12.5 0.2 copy.61
  12.7 0.8 reshape.75.refs_6_
  14.9 0.0 copy-done.2
  14.9 0.6 pad_add_fusion.info
  15.5 64.0 %inner_windows.1 = (bf16[3,16,96,180]{3,2,1,0:T(8,128)(2,1)}, f32[3,180,24,96]{3,2,1,0:T(8,128)}, f32[192,1728]{1,0:T(8,128)}, f32[3,192,192]{2,1,0:T(8,128)}, f...) custom-call(s32[6]{0:T(128)} %pad_add_fusion.info, ...), custom_call_target="tpu_custom_call" | custom-call | tf_op jit(solution)/shard_map/inner_windows/pallas_call | solution.py:1008
  79.4 0.6 pad_maximum_fusion.1.scal
  80.0 0.0 collective-permute-done
  80.0 1.7 copy.59.halo_ref
  81.7 35.8 %last_windows.1 = (bf16[3,8,96,180]{3,2,1,0:T(8,128)(2,1)}, f32[3,180,24,96]{3,2,1,0:T(8,128)}, bf16[3,4,180,96]{3,2,1,0:T(8,128)(2,1)}, f32[5120,128]{1,0:T(8,128)}) custom-call(s32[6]{0:T(128)} %pad_add_fusion.info, bf16[3,180,24,96]{3,2,1,0:T(8,128)(2,1)} %bitcast.29, bf16[3,180,24,96]{3,2,1,0:T(8,128)(2,1)} %bitcast.34, ...), custom_call_target="tpu_custom_call", output_to_operand_aliasing={{1}: (4, {})} | custom-call | tf_op jit(solution)/shard_map/last_windows/pallas_call | solution.py:1029
  117.6 61.2 %sum_gradients.1 = (bf16[5120,128]{1,0:T(8,128)(2,1)}, bf16[3,180,24,96]{3,2,1,0:T(8,128)(2,1)}, bf16[3,4,180,96]{3,2,1,0:T(8,128)(2,1)}) custom-call(f32[5120,128]{1,0:T(8,128)} %get-tuple-element.72.g_in, bf16[3,16,96,180]{3,2,1,0:T(8,128)(2,1)} %get-tuple-element.73.c1_in, bf16[3,8,96,180]{3,2,1,0:T(8,128)(2,1)} %get-tuple-element.74.c2_in, ...), custom_call_target="tpu_custom_call" | custom-call | tf_op jit(solution)/shard_map/sum_gradients/pallas_call | solution.py:838
  178.8 4.2 %halo_rows.1 = f32[3,180,24,96]{3,2,1,0:T(8,128)} custom-call(bf16[3,4,180,96]{3,2,1,0:T(8,128)(2,1)} %get-tuple-element.77.halo_ref, f32[3,180,24,96]{3,2,1,0:T(8,128)} %get-tuple-element.78.ig_ref), custom_call_target="tpu_custom_call", output_to_operand_aliasing={{}: (1, {})} | custom-call | tf_op jit(solution)/shard_map/halo_rows/pallas_call | solution.py:1066
  183.0 10.8 %adam.1 = (f32[1,1]{1,0:T(1,128)}, f32[1,1]{1,0:T(1,128)}, f32[11,180]{1,0:T(8,128)}, f32[11,180]{1,0:T(8,128)}, f32[11,180]{1,0:T(8,128)}, /*index=5*/f32[180,5...) custom-call(f32[2]{0:T(128)} %pad_maximum_fusion.1.scal, ...), custom_call_target="tpu_custom_call" | custom-call | tf_op jit(solution)/shard_map/adam/pallas_call | solution.py:1083
  194.4 1.7 copy.67
  (3 shorter events, 0.0 us)
Async XLA Ops:
  4.4 5.5 %copy-start.1 = (f32[225,6]{0,1:T(8,128)S(1)}, f32[225,6]{0,1:T(8,128)}, u32[]{:S(2)}) copy-start(f32[225,6]{0,1:T(8,128)} %param.41) | copy-start | bytes 16204
  4.4 5.5 %copy-start.3 = (s32[4096]{0:T(1024)S(1)}, s32[4096]{0:T(1024)}, u32[]{:S(2)}) copy-start(s32[4096]{0:T(1024)} %constant.38.clone) | copy-start | bytes 49156
  4.4 10.5 %copy-start.2 = (s32[3]{0:T(128)S(1)}, s32[3]{0:T(128)}, u32[]{:S(2)}) copy-start(s32[3]{0:T(128)} %param.31) | copy-start | bytes 40
  4.7 75.3 %collective-permute-start = (bf16[3,180,9,96]{3,1,2,0:T(8,128)(2,1)S(1)}, bf16[3,180,9,96]{3,1,2,0:T(8,128)(2,1)S(1)}, u32[]{:S(2)}, u32[]{:S(2)}) collective-permute-start(bf16[3,180,9,96]{3,1,2,0:T(8,128)(2,1)S(1)} %copy.57), channel_id=1, source_target_pairs={{1,0},{2,1},{3,2},{0,3},{5,4},{6,5},{7,6},{4,7},{9,8},{10,9},{11,1... | collective-permute-start | bytes 2799368 | tf_op jit(solution)/shard_map/ppermute | solution.py:988
  183.0 11.4 %copy-start = (bf16[3,180,24,96]{3,2,1,0:T(8,128)(2,1)S(1)}, bf16[3,180,24,96]{3,2,1,0:T(8,128)(2,1)}, u32[]{:S(2)}) copy-start(bf16[3,180,24,96]{3,2,1,0:T(8,128)(2,1)} %get-tuple-element.76) | copy-start | bytes 7464964
